TPU v7x, 512 devices: a whole 4x4x16 slice. The times are simulated.
512 devices in a mesh: tm: 16 (over z), query: 8 (over y, core), rec: 4 (over x).
Axes of the slice: x: 4, y: 4, z: 16, core: 2. Of those that a mesh axis runs over, the one named last changes fastest.
Arguments:
- frames: bfloat16 [4, 8192, 1024], P('rec', 'tm'), may hold values from -100 to 100
- queries: bfloat16 [4096, 1024], P('query'), may hold values from -10 to 10
- kernel: float32 [33, 4096], P(None, 'query'), may hold values from 0.01 to 0.12
- labels: int32 [4, 8192], P('rec', 'tm'), may hold values from 0 to 4095
- lengths: int32 [4], P('rec'), may hold values from 2048 to 8192, as said below
Outputs:
- grad_frames: bfloat16 [4, 8192, 1024], P('rec', 'tm', 'query')
- grad_queries: bfloat16 [4096, 1024], P('query', 'rec')
- grad_kernel: float32 [33, 4096], P(None, 'query')
Inputs may be any that keep to these rules, and one draw needn't show every extreme that they name: `lengths`: each entry counts the valid frames at the start of its recording; at least one recording has all 8192 frames valid.
All inputs are finite; a program needn't handle non-finite values.
Results may differ from a plain program's by a relative error of at most 0.0049.
Values sent between devices are 32-bit elements; how exact they have to be, the bound alone decides.
No kernel may reach another device: no remote copies, remote signals or barrier semaphores. Data moves between devices by JAX's collectives and lax.ppermute only.
A program may use at most 64 MiB of HBM per device.

v0:
```python
import math

import jax
import jax.numpy as jnp
from jax import lax
from jax.sharding import PartitionSpec as P


def merged(x, axis, combine):
    everything = jax.tree.map(lambda part: lax.all_gather(part, axis), x)
    first = jax.tree.map(lambda part: part[0], everything)

    def step(k, so_far):
        return combine(so_far, jax.tree.map(lambda part: part[k], everything))

    return lax.fori_loop(1, lax.axis_size(axis), step, first)


def with_halo(x, sides, width):
    for axis, dim in sides:
        peers, length = (lax.axis_size(axis), x.shape[dim])
        up = [(i, (i + 1) % peers) for i in range(peers - 1)]
        down = [(j, i) for i, j in up]
        last = lax.slice_in_dim(x, length - width, length, axis=dim)
        first = lax.slice_in_dim(x, 0, width, axis=dim)
        before = lax.ppermute(last, axis, up)
        after = lax.ppermute(first, axis, down)
        x = jnp.concatenate([before, x, after], axis=dim)
    return x


def tap_sum(kernel, padded, row_count, flipped):
    tap_count = kernel.shape[0]
    running = jnp.zeros((row_count, padded.shape[1]), jnp.float32)
    for offset in range(tap_count):
        begin_row = tap_count - 1 - offset if flipped else offset
        running = running + kernel[offset][None, :] * padded[begin_row : begin_row + row_count]
    return running


def combine_stats(first_pair, second_pair):
    top_value = jnp.maximum(first_pair[0], second_pair[0])
    total_value = first_pair[1] * jnp.exp(first_pair[0] - top_value) + second_pair[1] * jnp.exp(
        second_pair[0] - top_value
    )
    return (top_value, total_value)


def row_softmax(smooth):
    local_top = jnp.max(smooth, axis=1)
    local_total = jnp.sum(jnp.exp(smooth - local_top[:, None]), axis=1)
    top_value, total_value = merged((local_top, local_total), "query", combine_stats)
    return jnp.exp(smooth - top_value[:, None]) / total_value[:, None]


def per_device(frames, queries, kernel, labels, lengths):
    frame_rows = frames[0]
    label_ids = labels[0]
    length_now = lengths[0]
    row_count = frame_rows.shape[0]
    query_count = queries.shape[0]
    width = frame_rows.shape[1]
    tap_count = kernel.shape[0]
    rim_width = tap_count // 2
    logit_scale = 10.0 / math.sqrt(width)
    frame_start = lax.axis_index("tm") * row_count
    is_valid = frame_start + jnp.arange(row_count, dtype=jnp.int32) < length_now
    query_start = lax.axis_index("query") * query_count
    query_ids = query_start + jnp.arange(query_count, dtype=jnp.int32)
    scores = (
        lax.dot_general(
            frame_rows, queries, (((1,), (1,)), ((), ())), preferred_element_type=jnp.float32
        )
        * logit_scale
    )
    scores = jnp.where(is_valid[:, None], scores, 0.0)
    padded = with_halo(scores, (("tm", 0),), rim_width)
    smooth = tap_sum(kernel, padded, row_count, False)
    softmax_out = row_softmax(smooth)
    positive = (label_ids[:, None] == query_ids[None, :]).astype(jnp.float32)
    map_grad = jnp.where(is_valid[:, None], softmax_out - positive, 0.0)
    grad_pad = with_halo(map_grad, (("tm", 0),), rim_width)
    score_grad = tap_sum(kernel, grad_pad, row_count, True)
    score_grad = jnp.where(is_valid[:, None], score_grad, 0.0).astype(jnp.bfloat16)
    frame_part = jnp.dot(score_grad, queries, preferred_element_type=jnp.float32)
    frame_sum = lax.psum_scatter(frame_part, "query", scatter_dimension=1, tiled=True)
    grad_frames = (frame_sum * logit_scale).astype(jnp.bfloat16)[None]
    query_part = lax.dot_general(
        score_grad, frame_rows, (((0,), (0,)), ((), ())), preferred_element_type=jnp.float32
    )
    kernel_part = jnp.stack(
        [
            jnp.sum(map_grad * padded[offset : offset + row_count], axis=0)
            for offset in range(tap_count)
        ]
    )
    query_whole, grad_kernel = lax.psum((query_part, kernel_part), ("tm", "rec"))
    col_count = width // lax.axis_size("rec")
    query_cols = lax.dynamic_slice_in_dim(
        query_whole, lax.axis_index("rec") * col_count, col_count, 1
    )
    grad_queries = (query_cols * logit_scale).astype(jnp.bfloat16)
    return (grad_frames, grad_queries, grad_kernel)


def solution(mesh):
    in_specs = (P("rec", "tm", None), P("query", None), P(None, "query"), P("rec", "tm"), P("rec"))
    out_specs = (P("rec", "tm", "query"), P("query", "rec"), P(None, "query"))
    return jax.shard_map(
        per_device, mesh=mesh, in_specs=in_specs, out_specs=out_specs, check_vma=False
    )
```

profile of v0, /device:TPU:6, one launch (start us, length us, event | category | flops | bytes accessed | tf_op | source)
XLA Modules:
  0.0 374.9 jit_solution(3690222084819182365)
XLA Ops:
  8.0 0.0 copy-start
  8.0 0.0 all-reduce.3.cloned.1.call-start
  8.8 0.4 copy-done
  9.2 0.0 copy-start.5
  9.2 0.0 copy-start.4
  9.2 2.0 fusion
  11.3 3.8 %collective-permute-start = (f32[16,512]{1,0:T(8,128)S(1)}, f32[16,512]{1,0:T(8,128)S(1)}, u32[]{:S(2)}, u32[]{:S(2)}) collective-permute-start(f32[16,512]{1,0:T(8,128)S(1)} %get-tuple-element.192), channel_id=1, source_target_pairs={{0,32},{32,64},{64,96},{96,128},{128,160},{160,192},{192,224},{224... | collective-permute-start | bytes 98312 | tf_op jit(solution)/shard_map/ppermute | solution.py:26
  15.1 1.3 collective-permute-start.1
  16.4 0.0 copy-done.4
  16.5 0.2 collective-permute-done
  16.7 4.2 %collective-permute-done.1 = f32[16,512]{1,0:T(8,128)S(1)} collective-permute-done((f32[16,512]{1,0:T(8,128)S(1)}, f32[16,512]{1,0:T(8,128)S(1)}, u32[]{:S(2)}, u32[]{:S(2)}) %collective-permute-start.1) | collective-permute-done | bytes 32800 | tf_op jit(solution)/shard_map/ppermute | solution.py:27
  20.9 5.1 %fusion.131 = (f32[512]{0:T(512)S(1)}, f32[512,512]{1,0:T(8,128)S(1)}) fusion(f32[16,512]{1,0:T(8,128)S(1)} %collective-permute-done.1, f32[512,512]{1,0:T(8,128)S(1)} %fusion, f32[512]{0:T(512)S(1)} %bitcast.126, f32[512]{0:T(512)S(1)} %bitcast.128, f32[512]{0:T(512)S(1)} %bitcast.132, f32[512]{0:T(512)S(1)} %bitcast.134, f32[512]{0:T(512)S(1)} %bitcast.136, ...), kind=kLoop, calls=%fused_computation.265 | loop fusion | flops 25689600 | bytes 2232320 | tf_op jit(solution)/shard_map/reduce_max | solution.py:50
  26.0 0.0 copy-start.1
  26.0 0.0 copy-start.6
  26.1 1.0 copy-done.1
  27.0 0.3 exponential_reduce_fusion
  27.3 12.1 %all-gather.3 = f32[8,1,512]{2,1,0:T(1,128)S(1)} all-gather(f32[1,1,512]{2,1,0:T(1,128)S(1)} %bitcast.194), channel_id=3, replica_groups=mesh['tm'=16,'query'=8,'rec'=4] {'query'}, dimensions={0}, use_global_device_ids=true | all-gather | bytes 18432 | tf_op jit(solution)/shard_map/all_gather | solution.py:10
  39.4 11.2 %all-gather.2 = f32[8,1,512]{2,1,0:T(1,128)S(1)} all-gather(f32[1,1,512]{2,1,0:T(1,128)S(1)} %bitcast.168), channel_id=2, replica_groups=mesh['tm'=16,'query'=8,'rec'=4] {'query'}, dimensions={0}, use_global_device_ids=true | all-gather | bytes 18432 | tf_op jit(solution)/shard_map/all_gather | solution.py:10
  50.6 0.4 while.17
  51.0 0.0 copy-done.5
  51.0 0.0 copy-done.6
  51.0 4.3 %multiply_reduce_fusion = (f32[512]{0:T(512)S(1)}, f32[512]{0:T(512)S(1)}, f32[512]{0:T(512)S(1)}, f32[512]{0:T(512)S(1)}, f32[512]{0:T(512)S(1)}, /*index=5*/f3...) fusion(f32[16,512]{1,0:T(8,128)S(1)} %collective-permute-done.1, ...), kind=kLoop, calls=%fused_computation.222 | loop fusion | flops 8646144 | bytes 3205632 | tf_op jit(solution)/shard_map/reduce_sum | solution.py:93
  55.3 1.3 collective-permute-start.2
  56.6 4.5 %collective-permute-start.3 = (f32[16,512]{1,0:T(8,128)S(1)}, f32[16,512]{1,0:T(8,128)S(1)}, u32[]{:S(2)}, u32[]{:S(2)}) collective-permute-start(f32[16,512]{1,0:T(8,128)S(1)} %get-tuple-element.191), channel_id=1, source_target_pairs={{0,32},{32,64},{64,96},{96,128},{128,160},{160,192},{192,224},{224... | collective-permute-start | bytes 98312 | tf_op jit(solution)/shard_map/ppermute | solution.py:26
  61.2 1.9 multiply_reduce_fusion.1
  63.1 1.2 multiply_reduce_fusion.17
  64.3 1.0 multiply_reduce_fusion.26
  65.3 3.9 %stack.135 = f32[33,512]{1,0:T(8,128)} concatenate(f32[1,512]{1,0:T(1,128)S(1)} %bitcast.193, f32[1,512]{1,0:T(1,128)S(1)} %bitcast.192, f32[1,512]{1,0:T(1,128)S(1)} %bitcast.191, f32[1,512]{1,0:T(1,128)S(1)} %bitcast.190, f32[1,512]{1,0:T(1,128)S(1)} %bitcast.189, f32[1,512]{1,0:T(1,128)S(1)} %bitcast.188, f32[1,512]{1,0:T(1,128)S(1)} %bitcast.187, f32[1,512]{1,0:T(1,128)S(1)} %bitcast.186, ...), dimensions={0} | concatenate | bytes 135168 | tf_op jit(solution)/shard_map/stack | solution.py:91
  69.2 0.0 collective-permute-done.2
  69.2 0.0 collective-permute-done.3
  69.2 8.6 %fusion.6 = bf16[512,512]{1,0:T(8,128)(2,1)S(1)} fusion(f32[16,512]{1,0:T(8,128)S(1)} %collective-permute-done.3, f32[16,512]{1,0:T(8,128)S(1)} %collective-permute-done.2, f32[512,512]{1,0:T(8,128)S(1)} %get-tuple-element.185, f32[512]{0:T(512)S(1)} %bitcast.127, f32[512]{0:T(512)S(1)} %bitcast.129, f32[512]{0:T(512)S(1)} %bitcast.133, ...), kind=kLoop, calls=%fused_computation.70 | loop fusion | flops 25952256 | bytes 1706496 | tf_op jit(solution)/shard_map/convert_element_type | solution.py:84
  77.7 2.0 fusion.127
  79.8 0.0 copy-start.2
  79.8 0.0 all-reduce.3.cloned.1.call-update
  79.8 0.0 reduce-scatter.2.cloned.1.call-start
  79.9 1.1 copy-done.2
  81.0 2.0 fusion.136
  83.1 0.0 reduce-scatter.2.cloned.1.call-update
  83.1 280.3 %all-reduce.3.cloned.1.call-done = (f32[512,1024]{1,0:T(8,128)}, f32[33,512]{1,0:T(8,128)}) async-done(((f32[512,1024]{1,0:T(8,128)}, f32[33,512]{1,0:T(8,128)}), (f32[512,1024]{1,0:T(8,128)}, f32[33,512]{1,0:T(8,128)})) %all-reduce.3.cloned.1.call-update) | async-done | bytes 2164752 | tf_op jit(solution)/shard_map/psum | solution.py:97
  363.4 0.0 copy-start.3
  363.4 1.8 multiply_convert_fusion
  365.2 0.0 reduce-scatter.2.cloned.1.call-done
  365.2 1.6 fusion.130
  366.8 0.0 copy-done.3
  366.8 0.6 copy.26
  (24 shorter events, 0.3 us)
Async XLA Ops:
  8.0 1.2 copy-start
  8.0 355.3 %all-reduce.3.cloned.1.call-start = ((), (), s32[]{:S(2)}) async-start(), calls=%async_computation.2 | async-start | bytes 4358144 | tf_op jit(solution)/shard_map/psum | solution.py:97
  9.2 41.8 %copy-start.5 = (pred[512]{0:T(512)(128)(4,1)}, pred[512]{0:T(512)(128)(4,1)S(1)}, u32[]{:S(2)}) copy-start(pred[512]{0:T(512)(128)(4,1)S(1)} %add_compare_fusion) | copy-start | bytes 1540
  9.2 7.2 %copy-start.4 = (f32[33,512]{1,0:T(8,128)S(1)}, f32[33,512]{1,0:T(8,128)}, u32[]{:S(2)}) copy-start(f32[33,512]{1,0:T(8,128)} %param.9) | copy-start | bytes 202756
  11.3 5.4 %collective-permute-start = (f32[16,512]{1,0:T(8,128)S(1)}, f32[16,512]{1,0:T(8,128)S(1)}, u32[]{:S(2)}, u32[]{:S(2)}) collective-permute-start(f32[16,512]{1,0:T(8,128)S(1)} %get-tuple-element.192), channel_id=1, source_target_pairs={{0,32},{32,64},{64,96},{96,128},{128,160},{160,192},{192,224},{224... | collective-permute-start | bytes 98312 | tf_op jit(solution)/shard_map/ppermute | solution.py:26
  15.1 5.8 %collective-permute-start.1 = (f32[16,512]{1,0:T(8,128)S(1)}, f32[16,512]{1,0:T(8,128)S(1)}, u32[]{:S(2)}, u32[]{:S(2)}) collective-permute-start(f32[16,512]{1,0:T(8,128)S(1)} %get-tuple-element.193), channel_id=1, source_target_pairs={{32,0},{64,32},{96,64},{128,96},{160,128},{192,160},{224,192},{256... | collective-permute-start | bytes 98312 | tf_op jit(solution)/shard_map/ppermute | solution.py:27
  26.0 1.0 copy-start.1
  26.0 25.0 %copy-start.6 = (s32[1,512]{1,0:T(1,128)S(1)}, s32[1,512]{1,0:T(1,128)}, u32[]{:S(2)}) copy-start(s32[1,512]{1,0:T(1,128)} %param.10) | copy-start | bytes 6148
  55.3 13.9 %collective-permute-start.2 = (f32[16,512]{1,0:T(8,128)S(1)}, f32[16,512]{1,0:T(8,128)S(1)}, u32[]{:S(2)}, u32[]{:S(2)}) collective-permute-start(f32[16,512]{1,0:T(8,128)S(1)} %get-tuple-element.190), channel_id=1, source_target_pairs={{32,0},{64,32},{96,64},{128,96},{160,128},{192,160},{224,192},{256... | collective-permute-start | bytes 98312 | tf_op jit(solution)/shard_map/ppermute | solution.py:27
  56.6 12.6 %collective-permute-start.3 = (f32[16,512]{1,0:T(8,128)S(1)}, f32[16,512]{1,0:T(8,128)S(1)}, u32[]{:S(2)}, u32[]{:S(2)}) collective-permute-start(f32[16,512]{1,0:T(8,128)S(1)} %get-tuple-element.191), channel_id=1, source_target_pairs={{0,32},{32,64},{64,96},{96,128},{128,160},{160,192},{192,224},{224... | collective-permute-start | bytes 98312 | tf_op jit(solution)/shard_map/ppermute | solution.py:26
  79.8 1.2 copy-start.2
  79.8 285.4 %reduce-scatter.2.cloned.1.call-start = ((), (), s32[]{:S(2)}) async-start(), calls=%async_computation.1 | async-start | bytes 2359296 | tf_op jit(solution)/shard_map/reduce_scatter | solution.py:86
  363.4 3.4 copy-start.3
Sparse Core Ops, SparseCore 0:
  79.9 283.3 all-reduce.2
Sparse Core Ops, SparseCore 1:
  83.2 46.6 reduce-scatter.1
where the time goes:
time: 377 us; the launch traced here: 375 us
  waiting for transfers between devices  285 us (76%)
  other arithmetic  25.9 us (7%)
  blocking collectives  23.3 us (6%)
  between operations  16.4 us (4%)
  starting transfers between devices  11 us (3%)
  local copies, waits for them, and re-layouts  7.24 us (2%)
  matrix products  6.08 us (2%)
    psum x1, waiting for transfers between devices, per_device(): lax.psum((query_part, kernel_part), ('tm', 'rec'))  280 us
    all_gather x2, blocking collectives, merged(): everything = jax.tree.map(lambda part: lax.all_gather(part, axis), x)  23.3 us
    convert_element_type x1, other arithmetic, per_device(): jnp.where(is_valid[:, None], score_grad, 0.0).astype(jnp.bfloat16)  8.56 us
    ppermute x2, starting transfers between devices, with_halo(): before = lax.ppermute(last, axis, up)  8.38 us
    reduce_sum x4, other arithmetic, per_device(): jnp.sum(map_grad * padded[offset:offset + row_count], axis=0)  8.36 us
  transfers between devices with their start and end apart: 6, of which 3 were waited for; matrix products, arithmetic and copies ran while one was open for 3% of the time, Pallas kernels for 0%

commit v1 on v0

v1 whole, which is shorter than its diff:
```python
import math

import jax
import jax.numpy as jnp
from jax import lax
from jax.sharding import PartitionSpec as P


def with_halo(x, axis, width):
    peers, length = lax.axis_size(axis), x.shape[0]
    up = [(i, i + 1) for i in range(peers - 1)]
    down = [(j, i) for i, j in up]
    before = lax.ppermute(x[length - width :], axis, up)
    after = lax.ppermute(x[:width], axis, down)
    return jnp.concatenate([before, x, after], axis=0)


def tap_sum(kernel, padded, row_count, flipped):
    tap_count = kernel.shape[0]
    running = jnp.zeros((row_count, padded.shape[1]), jnp.float32)
    for offset in range(tap_count):
        begin_row = tap_count - 1 - offset if flipped else offset
        running = running + kernel[offset][None, :] * padded[begin_row : begin_row + row_count]
    return running


def row_softmax(smooth):
    local_top = jnp.max(smooth, axis=1)
    local_total = jnp.sum(jnp.exp(smooth - local_top[:, None]), axis=1)
    pairs = lax.all_gather(jnp.stack([local_top, local_total]), "query")
    tops, totals = pairs[:, 0], pairs[:, 1]
    top = jnp.max(tops, axis=0)
    total = jnp.sum(totals * jnp.exp(tops - top[None, :]), axis=0)
    return jnp.exp(smooth - top[:, None]) / total[:, None]


LANES = 128
TAP_ROWS = 16


def reduce_query_side(query_part, kernel_part):
    recs, tms = lax.axis_size("rec"), lax.axis_size("tm")
    queries, width = query_part.shape
    taps = kernel_part.shape[0]
    groups = queries // LANES
    halves = width // recs // LANES
    rows = queries // tms
    q = query_part.reshape(tms, rows, recs, halves, LANES)
    q = q.transpose(2, 0, 3, 1, 4).reshape(recs, tms, halves * rows, LANES)
    k = jnp.pad(kernel_part, ((0, tms * TAP_ROWS // groups - taps), (0, 0)))
    k = k.reshape(-1, groups, LANES).transpose(1, 0, 2).reshape(1, tms, TAP_ROWS, LANES)
    k = jnp.broadcast_to(k, (recs, tms, TAP_ROWS, LANES))
    chunks = jnp.concatenate([q, k], axis=2)
    chunks = jnp.sum(lax.all_to_all(chunks, "rec", 0, 0), axis=0)
    chunk = jnp.sum(lax.all_to_all(chunks, "tm", 0, 0), axis=0)
    whole = lax.all_gather(chunk, "tm")
    q = whole[:, : halves * rows].reshape(tms, halves, rows, LANES)
    q = q.transpose(0, 2, 1, 3).reshape(queries, width // recs)
    k = whole[:, halves * rows :].reshape(groups, tms * TAP_ROWS // groups, LANES)
    k = k.transpose(1, 0, 2).reshape(-1, queries)[:taps]
    return q, k


def per_device(frames, queries, kernel, labels, lengths):
    frame_rows = frames[0]
    label_ids = labels[0]
    length_now = lengths[0]
    row_count = frame_rows.shape[0]
    query_count = queries.shape[0]
    width = frame_rows.shape[1]
    tap_count = kernel.shape[0]
    rim_width = tap_count // 2
    logit_scale = 10.0 / math.sqrt(width)
    frame_start = lax.axis_index("tm") * row_count
    is_valid = frame_start + jnp.arange(row_count, dtype=jnp.int32) < length_now
    query_start = lax.axis_index("query") * query_count
    query_ids = query_start + jnp.arange(query_count, dtype=jnp.int32)
    scores = (
        lax.dot_general(
            frame_rows, queries, (((1,), (1,)), ((), ())), preferred_element_type=jnp.float32
        )
        * logit_scale
    )
    scores = jnp.where(is_valid[:, None], scores, 0.0)
    padded = with_halo(scores, "tm", rim_width)
    smooth = tap_sum(kernel, padded, row_count, False)
    softmax_out = row_softmax(smooth)
    positive = (label_ids[:, None] == query_ids[None, :]).astype(jnp.float32)
    map_grad = jnp.where(is_valid[:, None], softmax_out - positive, 0.0)
    grad_pad = with_halo(map_grad, "tm", rim_width)
    score_grad = tap_sum(kernel, grad_pad, row_count, True)
    score_grad = jnp.where(is_valid[:, None], score_grad, 0.0).astype(jnp.bfloat16)
    frame_part = jnp.dot(score_grad, queries, preferred_element_type=jnp.float32)
    query_part = lax.dot_general(
        score_grad, frame_rows, (((0,), (0,)), ((), ())), preferred_element_type=jnp.float32
    )
    kernel_part = jnp.stack(
        [
            jnp.sum(map_grad * padded[offset : offset + row_count], axis=0)
            for offset in range(tap_count)
        ]
    )
    frame_part, query_part, kernel_part = lax.optimization_barrier((frame_part, query_part, kernel_part))
    frame_sum = lax.psum_scatter(frame_part, "query", scatter_dimension=1, tiled=True)
    query_cols, grad_kernel = reduce_query_side(query_part, kernel_part)
    grad_frames = (frame_sum * logit_scale).astype(jnp.bfloat16)[None]
    grad_queries = (query_cols * logit_scale).astype(jnp.bfloat16)
    return (grad_frames, grad_queries, grad_kernel)


def solution(mesh):
    in_specs = (P("rec", "tm", None), P("query", None), P(None, "query"), P("rec", "tm"), P("rec"))
    out_specs = (P("rec", "tm", "query"), P("query", "rec"), P(None, "query"))
    return jax.shard_map(
        per_device, mesh=mesh, in_specs=in_specs, out_specs=out_specs, check_vma=False
    )
```

time: 377 us -> 206 us (0.55)
  waiting for transfers between devices: 285 us -> 34.8 us
  blocking collectives: 23.3 us -> 85.2 us
  starting transfers between devices: 11 us -> 25.6 us
    psum x1 -> x0, waiting for transfers between devices: 280 us -> none  [per_device(): lax.psum((query_part, kernel_part), ('tm', 'rec'))]
    all_to_all x0 -> x1, blocking collectives: none -> 36.1 us  [reduce_query_side(): chunks = jnp.sum(lax.all_to_all(chunks, 'rec', 0, 0), axis=0)]
    all_to_all x0 -> x1, waiting for transfers between devices: none -> 30.3 us  [reduce_query_side(): chunk = jnp.sum(lax.all_to_all(chunks, 'tm', 0, 0), axis=0)]
    all_gather x2, blocking collectives: 23.3 us -> 49 us  [the longest x1 35.7 us: reduce_query_side(): whole = lax.all_gather(chunk, 'tm')]
    all_to_all x0 -> x1, starting transfers between devices: none -> 14.6 us  [reduce_query_side(): chunk = jnp.sum(lax.all_to_all(chunks, 'tm', 0, 0), axis=0)]
    reshape x0 -> x3, local copies, waits for them, and re-layouts: none -> 4.89 us  [the longest x2 4.84 us: reduce_query_side(): q = query_part.reshape(tms, rows, recs, halves, LANES)]
  transfers between devices with their start and end apart: 6 -> 6, of which waited for: 3 -> 3; matrix products, arithmetic and copies ran while one was open for 3% -> 9% of each run, Pallas kernels for 0% -> 0%
where the time goes in v1:
time: 206 us; the launch traced here: 204 us
  blocking collectives  85.2 us (41%)
  waiting for transfers between devices  34.8 us (17%)
  other arithmetic  27.9 us (14%)
  starting transfers between devices  25.6 us (12%)
  between operations  15.1 us (7%)
  local copies, waits for them, and re-layouts  10.6 us (5%)
  matrix products  4.79 us (2%)
    all_to_all x1, blocking collectives, reduce_query_side(): chunks = jnp.sum(lax.all_to_all(chunks, 'rec', 0, 0), axis=0)  36.1 us
    all_gather x1, blocking collectives, reduce_query_side(): whole = lax.all_gather(chunk, 'tm')  35.7 us
    all_to_all x1, waiting for transfers between devices, reduce_query_side(): chunk = jnp.sum(lax.all_to_all(chunks, 'tm', 0, 0), axis=0)  30.3 us
    all_to_all x1, starting transfers between devices, reduce_query_side(): chunk = jnp.sum(lax.all_to_all(chunks, 'tm', 0, 0), axis=0)  14.6 us
    all_gather x1, blocking collectives, row_softmax(): pairs = lax.all_gather(jnp.stack([local_top, local_total]), 'query')  13.3 us
    reduce_sum x4, other arithmetic, per_device(): jnp.sum(map_grad * padded[offset:offset + row_count], axis=0)  9.08 us
    convert_element_type x1, other arithmetic, per_device(): jnp.where(is_valid[:, None], score_grad, 0.0).astype(jnp.bfloat16)  8.52 us
    ppermute x2, starting transfers between devices, with_halo(): before = lax.ppermute(x[length - width:], axis, up)  8.37 us
  transfers between devices with their start and end apart: 6, of which 3 were waited for; matrix products, arithmetic and copies ran while one was open for 9% of the time, Pallas kernels for 0%

profile of v1, /device:TPU:6, one launch (start us, length us, event | category | flops | bytes accessed | tf_op | source)
XLA Modules:
  0.0 203.9 jit_solution(653930509716895148)
XLA Ops:
  7.2 0.0 copy-start
  7.2 0.0 reduce-scatter.2.cloned.1.call-start
  8.0 0.4 copy-done
  8.4 2.0 fusion
  10.4 3.8 %collective-permute-start = (f32[16,512]{1,0:T(8,128)S(1)}, f32[16,512]{1,0:T(8,128)S(1)}, u32[]{:S(2)}, u32[]{:S(2)}) collective-permute-start(f32[16,512]{1,0:T(8,128)S(1)} %get-tuple-element.47), channel_id=1, source_target_pairs={{0,32},{32,64},{64,96},{96,128},{128,160},{160,192},{192,224},{224... | collective-permute-start | bytes 98312 | tf_op jit(solution)/shard_map/ppermute | solution.py:13
  14.3 1.3 collective-permute-start.1
  15.6 0.0 copy-done.2
  15.7 0.2 collective-permute-done
  15.8 4.2 %collective-permute-done.1 = f32[16,512]{1,0:T(8,128)S(1)} collective-permute-done((f32[16,512]{1,0:T(8,128)S(1)}, f32[16,512]{1,0:T(8,128)S(1)}, u32[]{:S(2)}, u32[]{:S(2)}) %collective-permute-start.1) | collective-permute-done | bytes 32800 | tf_op jit(solution)/shard_map/ppermute | solution.py:14
  20.1 5.1 %fusion.135 = (f32[512]{0:T(512)S(1)}, f32[512,512]{1,0:T(8,128)S(1)}) fusion(f32[16,512]{1,0:T(8,128)S(1)} %collective-permute-done.1, f32[512,512]{1,0:T(8,128)S(1)} %fusion, f32[512]{0:T(512)S(1)} %bitcast.151, f32[512]{0:T(512)S(1)} %bitcast.153, f32[512]{0:T(512)S(1)} %bitcast.157, f32[512]{0:T(512)S(1)} %bitcast.159, f32[512]{0:T(512)S(1)} %bitcast.161, ...), kind=kLoop, calls=%fused_computation.270 | loop fusion | flops 25689600 | bytes 2232320 | tf_op jit(solution)/shard_map/reduce_max | solution.py:28
  25.2 0.0 copy-start.13
  25.2 0.3 exponential_reduce_fusion
  25.5 13.3 %all-gather.2 = f32[8,2,512]{2,1,0:T(2,128)S(1)} all-gather(f32[1,2,512]{2,1,0:T(2,128)S(1)} %maximum_bitcast_fusion), channel_id=2, replica_groups=mesh['tm'=16,'query'=8,'rec'=4] {'query'}, dimensions={0}, use_global_device_ids=true | all-gather | bytes 36864 | tf_op jit(solution)/shard_map/all_gather | solution.py:30
  39.0 0.0 copy-done.12
  39.0 0.0 copy-done.13
  39.0 3.7 %multiply_reduce_fusion = (f32[512]{0:T(512)}, f32[512]{0:T(512)}, f32[512]{0:T(512)}, f32[512]{0:T(512)}, f32[512]{0:T(512)}, /*index=5*/f32[512]{0:T(512)}, f3...) fusion(f32[16,512]{1,0:T(8,128)S(1)} %collective-permute-done.1, f32[512,512]{1,0:T(8,128)S(1)} %fusion, ...), kind=kLoop, calls=%fused_computation.220 | loop fusion | flops 8646144 | bytes 3205632 | tf_op jit(solution)/shard_map/reduce_sum | solution.py:99
  42.7 1.3 collective-permute-start.2
  44.0 4.5 %collective-permute-start.3 = (f32[16,512]{1,0:T(8,128)S(1)}, f32[16,512]{1,0:T(8,128)S(1)}, u32[]{:S(2)}, u32[]{:S(2)}) collective-permute-start(f32[16,512]{1,0:T(8,128)S(1)} %get-tuple-element.46), channel_id=1, source_target_pairs={{0,32},{32,64},{64,96},{96,128},{128,160},{160,192},{192,224},{224... | collective-permute-start | bytes 98312 | tf_op jit(solution)/shard_map/ppermute | solution.py:13
  48.6 1.9 multiply_reduce_fusion.1
  50.5 1.8 multiply_reduce_fusion.17
  52.4 1.6 multiply_reduce_fusion.26
  54.0 0.0 copy-done.8
  54.0 0.0 copy-done.9
  54.0 0.0 copy-done.10
  54.0 0.0 copy-done.11
  54.0 2.9 %stack.147 = f32[33,512]{1,0:T(8,128)S(1)} concatenate(f32[1,512]{1,0:T(1,128)} %bitcast.218, f32[1,512]{1,0:T(1,128)} %bitcast.217, f32[1,512]{1,0:T(1,128)} %bitcast.216, f32[1,512]{1,0:T(1,128)} %bitcast.215, f32[1,512]{1,0:T(1,128)} %bitcast.214, f32[1,512]{1,0:T(1,128)} %bitcast.213, f32[1,512]{1,0:T(1,128)} %bitcast.212, f32[1,512]{1,0:T(1,128)} %bitcast.211, ...), dimensions={0} | concatenate | bytes 135168 | tf_op jit(solution)/shard_map/stack | solution.py:97
  56.9 0.0 collective-permute-done.2
  56.9 0.0 collective-permute-done.3
  57.0 8.5 %fusion.6 = bf16[512,512]{1,0:T(8,128)(2,1)S(1)} fusion(f32[16,512]{1,0:T(8,128)S(1)} %collective-permute-done.3, f32[16,512]{1,0:T(8,128)S(1)} %collective-permute-done.2, f32[512,512]{1,0:T(8,128)S(1)} %get-tuple-element.42, f32[512]{0:T(512)S(1)} %bitcast.152, f32[512]{0:T(512)S(1)} %bitcast.154, f32[512]{0:T(512)S(1)} %bitcast.158, f32[512]{0:T(512)S(1)} %bitcast.160, ...), kind=kLoop, calls=%fused_computation.68 | loop fusion | flops 25952256 | bytes 1706496 | tf_op jit(solution)/shard_map/convert_element_type | solution.py:92
  65.5 0.0 copy-start.1
  65.5 0.7 fusion.127
  66.3 0.5 copy-done.1
  66.7 2.0 %fusion.140 = f32[512,1024]{1,0:T(8,128)} fusion(bf16[512,512]{1,0:T(8,128)(2,1)S(1)} %fusion.6, bf16[512,1024]{1,0:T(8,128)(2,1)S(1)} %copy-done.1), kind=kOutput, calls=%fused_computation.275 | convolution fusion | flops 536870912 | bytes 3670016 | tf_op jit(solution)/shard_map/dot_general | solution.py:93
  68.8 0.0 reduce-scatter.2.cloned.1.call-update
  68.9 2.8 %reshape.44 = f32[16,32,4,2,128]{4,3,2,1,0:T(2,128)} reshape(f32[512,1024]{1,0:T(8,128)S(1)} %fusion.127) | data formatting | bytes 4194304 | tf_op jit(solution)/shard_map/reshape | solution.py:48
  71.7 2.0 copy.22
  73.8 0.2 pad_maximum_fusion
  74.0 36.1 %all_to_all.10 = f32[4,16,80,128]{3,2,1,0:T(8,128)} all-to-all(f32[4,16,80,128]{3,2,1,0:T(8,128)S(1)} %pad_maximum_fusion), channel_id=1, replica_groups=mesh['tm'=16,'query'=8,'rec'=4] {'rec'}, dimensions={0} | all-to-all | bytes 5242880 | tf_op jit(solution)/shard_map/all_to_all | solution.py:54
  110.1 2.8 %reduce_sum.368 = f32[16,80,128]{2,1,0:T(8,128)} reduce(f32[4,16,80,128]{3,2,1,0:T(8,128)} %all_to_all.10, f32[]{:T(128)} %constant.6.clone.1), dimensions={0}, to_apply=%region_38.39 | reduce | flops 491520 | bytes 3276804 | tf_op jit(solution)/shard_map/reduce_sum | solution.py:54
  113.0 14.6 %all-to-all-start.1 = ((f32[16,80,128]{2,1,0:T(8,128)}), f32[16,80,128]{2,1,0:T(8,128)S(1)}, u32[]{:S(2)}, u32[]{:S(2)}) async-start(f32[16,80,128]{2,1,0:T(8,128)} %reduce_sum.368), calls=%async_computation.2 | async-start | bytes 1310720 | tf_op jit(solution)/shard_map/all_to_all | solution.py:55
  127.6 0.0 reduce-scatter.2.cloned.1.call-done
  127.6 1.6 fusion.131
  129.2 30.3 %all-to-all-done.1 = f32[16,80,128]{2,1,0:T(8,128)S(1)} async-done(((f32[16,80,128]{2,1,0:T(8,128)}), f32[16,80,128]{2,1,0:T(8,128)S(1)}, u32[]{:S(2)}, u32[]{:S(2)}) %all-to-all-start.1) | async-done | bytes 655392 | tf_op jit(solution)/shard_map/all_to_all | solution.py:55
  159.6 35.7 %all-gather.1 = f32[1280,128]{1,0:T(8,128)S(1)} all-gather(f32[80,128]{1,0:T(8,128)S(1)} %reduce_sum.369), channel_id=3, replica_groups=mesh['tm'=16,'query'=8,'rec'=4] {'tm'}, dimensions={0}, use_global_device_ids=true | all-gather | bytes 696320 | tf_op jit(solution)/shard_map/all_gather | solution.py:56
  195.3 0.1 fusion.130
  195.3 0.2 copy.24
  195.6 0.7 copy.37
  196.4 0.6 copy.29
  (34 shorter events, 0.4 us)
Async XLA Ops:
  7.2 1.2 copy-start
  7.2 120.4 %reduce-scatter.2.cloned.1.call-start = ((), (), s32[]{:S(2)}) async-start(), calls=%async_computation.3 | async-start | bytes 2359296 | tf_op jit(solution)/shard_map/reduce_scatter | solution.py:104
  8.4 30.5 %copy-start.12 = (pred[512]{0:T(512)(128)(4,1)}, pred[512]{0:T(512)(128)(4,1)S(1)}, u32[]{:S(2)}) copy-start(pred[512]{0:T(512)(128)(4,1)S(1)} %add_compare_fusion) | copy-start | bytes 1540
  8.4 7.2 %copy-start.2 = (f32[33,512]{1,0:T(8,128)S(1)}, f32[33,512]{1,0:T(8,128)}, u32[]{:S(2)}) copy-start(f32[33,512]{1,0:T(8,128)} %param.7) | copy-start | bytes 202756
  10.4 5.4 %collective-permute-start = (f32[16,512]{1,0:T(8,128)S(1)}, f32[16,512]{1,0:T(8,128)S(1)}, u32[]{:S(2)}, u32[]{:S(2)}) collective-permute-start(f32[16,512]{1,0:T(8,128)S(1)} %get-tuple-element.47), channel_id=1, source_target_pairs={{0,32},{32,64},{64,96},{96,128},{128,160},{160,192},{192,224},{224... | collective-permute-start | bytes 98312 | tf_op jit(solution)/shard_map/ppermute | solution.py:13
  14.3 5.8 %collective-permute-start.1 = (f32[16,512]{1,0:T(8,128)S(1)}, f32[16,512]{1,0:T(8,128)S(1)}, u32[]{:S(2)}, u32[]{:S(2)}) collective-permute-start(f32[16,512]{1,0:T(8,128)S(1)} %get-tuple-element.48), channel_id=1, source_target_pairs={{32,0},{64,32},{96,64},{128,96},{160,128},{192,160},{224,192},{256... | collective-permute-start | bytes 98312 | tf_op jit(solution)/shard_map/ppermute | solution.py:14
  15.6 9.5 %copy-start.3 = (f32[1,512]{1,0:T(1,128)}, f32[1,512]{1,0:T(1,128)S(1)}, u32[]{:S(2)}) copy-start(f32[1,512]{1,0:T(1,128)S(1)} %get-tuple-element.67) | copy-start | bytes 6148
  25.2 13.8 %copy-start.13 = (s32[1,512]{1,0:T(1,128)S(1)}, s32[1,512]{1,0:T(1,128)}, u32[]{:S(2)}) copy-start(s32[1,512]{1,0:T(1,128)} %param.8) | copy-start | bytes 6148
  42.7 14.2 %collective-permute-start.2 = (f32[16,512]{1,0:T(8,128)S(1)}, f32[16,512]{1,0:T(8,128)S(1)}, u32[]{:S(2)}, u32[]{:S(2)}) collective-permute-start(f32[16,512]{1,0:T(8,128)S(1)} %get-tuple-element.45), channel_id=1, source_target_pairs={{32,0},{64,32},{96,64},{128,96},{160,128},{192,160},{224,192},{256... | collective-permute-start | bytes 98312 | tf_op jit(solution)/shard_map/ppermute | solution.py:14
  44.0 12.9 %collective-permute-start.3 = (f32[16,512]{1,0:T(8,128)S(1)}, f32[16,512]{1,0:T(8,128)S(1)}, u32[]{:S(2)}, u32[]{:S(2)}) collective-permute-start(f32[16,512]{1,0:T(8,128)S(1)} %get-tuple-element.46), channel_id=1, source_target_pairs={{0,32},{32,64},{64,96},{96,128},{128,160},{160,192},{192,224},{224... | collective-permute-start | bytes 98312 | tf_op jit(solution)/shard_map/ppermute | solution.py:13
  52.3 1.6 copy-start.5
  52.3 1.6 copy-start.6
  52.3 1.6 copy-start.7
  52.4 1.6 copy-start.8
  52.4 1.6 copy-start.9
  52.4 1.6 copy-start.10
  52.4 1.6 copy-start.11
  52.4 4.6 %copy-start.4 = (f32[1,512]{1,0:T(1,128)S(1)}, f32[1,512]{1,0:T(1,128)}, u32[]{:S(2)}) copy-start(f32[1,512]{1,0:T(1,128)} %copy-done.3) | copy-start | bytes 6148
  65.5 1.2 copy-start.1
  113.0 46.6 %all-to-all-start.1 = ((f32[16,80,128]{2,1,0:T(8,128)}), f32[16,80,128]{2,1,0:T(8,128)S(1)}, u32[]{:S(2)}, u32[]{:S(2)}) async-start(f32[16,80,128]{2,1,0:T(8,128)} %reduce_sum.368), calls=%async_computation.2 | async-start | bytes 1310720 | tf_op jit(solution)/shard_map/all_to_all | solution.py:55
Sparse Core Ops, SparseCore 0:
  68.9 46.5 reduce-scatter.1

commit v2 on v0

v2 whole, which is shorter than its diff:
```python
import math

import jax
import jax.numpy as jnp
from jax import lax
from jax.experimental import pallas as pl
from jax.experimental.pallas import tpu as pltpu
from jax.sharding import PartitionSpec as P

SUB = 8
LANES = 128
VMEM = pltpu.VMEM
F32 = jnp.float32
UNIT = 8


def whole_spec(count):
    return [pl.BlockSpec(memory_space=VMEM)] * count


def params():
    return pltpu.CompilerParams(vmem_limit_bytes=48 * 1024 * 1024)


def cost(flops, bytes_accessed):
    return pl.CostEstimate(flops=flops, bytes_accessed=bytes_accessed, transcendentals=0)


def placement(rows, blk, flipped=False):
    m = lax.broadcasted_iota(jnp.int32, (rows, rows), 1 if flipped else 0)
    f = lax.broadcasted_iota(jnp.int32, (rows, rows), 0 if flipped else 1)
    return jnp.where(f == (m & (SUB - 1)) * blk + m // SUB, 1.0, 0.0).astype(jnp.bfloat16)


def dot_t(a, b):
    return lax.dot_general(a, b, (((1,), (1,)), ((), ())), preferred_element_type=F32)


def score_kernel(scale, scalars, frames, queries, out):
    rows = frames.shape[0]
    blk = rows // SUB
    placed = jnp.dot(placement(rows, blk), frames[...], preferred_element_type=F32).astype(jnp.bfloat16)
    m = lax.broadcasted_iota(jnp.int32, (rows, 1), 0)
    frame = scalars[0] + (m & (SUB - 1)) * blk + m // SUB
    out[...] = jnp.where(frame < scalars[1], dot_t(placed, queries[...]) * scale, 0.0)


def broadcast_taps(taps, wide, count):
    for j in range(count):
        wide[j] = jnp.broadcast_to(taps[j : j + 1, :], wide.shape[1:])


def tap_block(load, wide, g, count, flipped):
    sums = [None] * UNIT
    rows = [load(t) for t in range(UNIT + count - 1)]
    for j in range(count):
        tap = wide[count - 1 - j if flipped else j, :, g * LANES : (g + 1) * LANES]
        for u in range(UNIT):
            term = tap * rows[u + j]
            sums[u] = term if sums[u] is None else sums[u] + term
    return sums


def smooth_kernel(scale, half, scalars, main, before, after, queries, taps, scores, powers, stats, wide):
    blk = main.shape[0]
    count = 2 * half + 1
    groups = queries.shape[0] // LANES
    rim = 2 * half
    broadcast_taps(taps, wide, count)
    rim_frames = jnp.concatenate([before[:rim, :], after[:rim, :]], axis=0).astype(jnp.bfloat16)
    k = lax.broadcasted_iota(jnp.int32, (2 * rim, 1), 0)
    frame = scalars[0] + jnp.where(k < rim, k - rim, blk * SUB + k - rim)
    rim_scores = jnp.where(
        (frame >= 0) & (frame < scalars[1]), dot_t(rim_frames, queries[...]) * scale, 0.0
    )
    sub = lax.broadcasted_iota(jnp.int32, main.shape[1:], 0)
    scores[rim : rim + blk] = main[...]
    for t in range(rim):
        low = pltpu.roll(main[blk - rim + t], 1, 0)
        scores[t] = jnp.where(sub == 0, rim_scores[t : t + 1, :], low)
        high = pltpu.roll(main[t], SUB - 1, 0)
        scores[rim + blk + t] = jnp.where(sub == SUB - 1, rim_scores[rim + t : rim + t + 1, :], high)
    lane = lax.broadcasted_iota(jnp.int32, (SUB, LANES), 1)

    def step(b, carry):
        tops, totals = carry
        first = b * UNIT
        tiles = []
        for g in range(groups):
            cols = slice(g * LANES, (g + 1) * LANES)
            tiles.append(tap_block(lambda t: scores[first + t, :, cols], wide, g, count, False))
        for u in range(UNIT):
            mine = [tiles[g][u] for g in range(groups)]
            peak = mine[0]
            for tile in mine[1:]:
                peak = jnp.maximum(peak, tile)
            top = jnp.max(peak, axis=1, keepdims=True)
            total = None
            for g in range(groups):
                e = jnp.exp(mine[g] - top)
                powers[first + u, :, g * LANES : (g + 1) * LANES] = e
                total = e if total is None else total + e
            total = jnp.sum(total, axis=1, keepdims=True)
            here = lane == first + u
            tops = jnp.where(here, top, tops)
            totals = jnp.where(here, total, totals)
        return tops, totals

    zero = jnp.zeros((SUB, LANES), F32)
    tops, totals = lax.fori_loop(0, (blk + rim) // UNIT, step, (zero, zero))
    stats[0] = tops
    stats[1] = totals


def grad_kernel(
    half, chunk_rows, scalars, powers, scores, mine, others, labels, frames, queries, taps,
    chunks, frame_part, wide, grads, tap_grads, placed,
):
    blk = powers.shape[0] - 2 * half
    rows = blk * SUB
    count = 2 * half + 1
    width = queries.shape[1]
    query_count = queries.shape[0]
    groups = query_count // LANES
    broadcast_taps(taps, wide, count)
    tops = others[:, 0]
    top = jnp.max(tops, axis=0)
    total = jnp.sum(others[:, 1] * jnp.exp(tops - top[None]), axis=0)
    lane = lax.broadcasted_iota(jnp.int32, (SUB, LANES), 1)
    frame = scalars[0] + lax.broadcasted_iota(jnp.int32, (SUB, LANES), 0) * blk + lane - half
    valid = (frame >= 0) & (frame < scalars[1]) & (lane < blk + 2 * half)
    weight = jnp.where(valid, jnp.exp(mine[0] - top) / total, 0.0)
    label = jnp.where(valid, labels[...] - scalars[2].astype(F32), -1.0)
    keep = jnp.where(valid, 1.0, 0.0)
    ids = lax.broadcasted_iota(jnp.int32, (SUB, query_count), 1).astype(F32)

    def place(b, _):
        first = b * UNIT
        turn = lax.rem(LANES - first, LANES)
        w = pltpu.roll(weight, turn, 1)
        l = pltpu.roll(label, turn, 1)
        for u in range(UNIT):
            positive = jnp.where(ids == l[:, u : u + 1], 1.0, 0.0)
            grads[first + u] = powers[first + u] * w[:, u : u + 1] - positive * 1.0
        return 0

    lax.fori_loop(0, (blk + 2 * half) // UNIT, place, 0)
    tap_grads[...] = jnp.zeros_like(tap_grads)

    def correlate(b, _):
        first = half + b * UNIT
        for g in range(groups):
            cols = slice(g * LANES, (g + 1) * LANES)
            left = [grads[first + u, :, cols] for u in range(UNIT)]
            right = [scores[first + t, :, cols] for t in range(UNIT + count - 1)]
            for j in range(count):
                terms = [left[u] * right[u + j] for u in range(UNIT)]
                while len(terms) > 1:
                    terms = [terms[n] + terms[n + 1] for n in range(0, len(terms), 2)]
                tap_grads[j, :, cols] += terms[0]
        return 0

    lax.fori_loop(0, blk // UNIT, correlate, 0)

    def spread(b, _):
        first = b * UNIT
        turn = lax.rem(2 * LANES - half - first, LANES)
        kept = pltpu.roll(keep, turn, 1)
        for g in range(groups):
            cols = slice(g * LANES, (g + 1) * LANES)
            sums = tap_block(lambda t: grads[first + t, :, cols], wide, g, count, True)
            sums = [sums[u] * kept[:, u : u + 1] for u in range(UNIT)]
            block = jnp.concatenate(sums, axis=0).astype(jnp.bfloat16)
            placed[pl.ds(pl.multiple_of(first * SUB, UNIT * SUB), UNIT * SUB), cols] = block
        return 0

    lax.fori_loop(0, blk // UNIT, spread, 0)
    score_grad = jnp.dot(placement(rows, blk, True), placed[...], preferred_element_type=F32)
    frame_part[...] = jnp.dot(score_grad.astype(jnp.bfloat16), queries[...], preferred_element_type=F32)
    turned = score_grad.T.astype(jnp.bfloat16)
    recs, tms, padded_rows, part_width = chunks.shape
    parts = jnp.sum(tap_grads[...], axis=1)
    parts = jnp.concatenate([parts, jnp.zeros((padded_rows_of(count) - count, query_count), F32)], axis=0)
    tap_rows = padded_rows - chunk_rows
    halves = query_count // part_width
    per_half = tms // halves
    for r in range(recs):
        part = jnp.dot(turned, frames[:, r * part_width : (r + 1) * part_width], preferred_element_type=F32)
        for z in range(tms):
            chunks[r, z, :chunk_rows, :] = part[z * chunk_rows : (z + 1) * chunk_rows, :]
            start = (z % per_half) * tap_rows
            h = z // per_half
            if start < count:
                chunks[r, z, chunk_rows:, :] = parts[
                    start : start + tap_rows, h * part_width : (h + 1) * part_width
                ]
            else:
                chunks[r, z, chunk_rows:, :] = jnp.zeros((tap_rows, part_width), F32)


def padded_rows_of(count):
    return (count + UNIT - 1) // UNIT * UNIT


def per_device(frames, queries, kernel, labels, lengths):
    frame_rows = frames[0]
    label_ids = labels[0].astype(F32)
    rows, width = frame_rows.shape
    query_count = queries.shape[0]
    count = kernel.shape[0]
    half = count // 2
    rim = 2 * half
    blk = rows // SUB
    scale = 10.0 / math.sqrt(width)
    recs, tms, blocks = lax.axis_size("rec"), lax.axis_size("tm"), lax.axis_size("query")
    scalars = jnp.stack(
        [lax.axis_index("tm") * rows, lengths[0], lax.axis_index("query") * query_count]
    ).astype(jnp.int32)
    smem = pl.BlockSpec(memory_space=pltpu.SMEM)

    def edge(part, ids):
        extra = jnp.pad(ids[None, :], ((0, UNIT - 1), (0, width - rim)))
        return jnp.concatenate([part.astype(F32), extra], axis=0)

    up = [(i, i + 1) for i in range(tms - 1)]
    down = [(j, i) for i, j in up]
    before = lax.ppermute(edge(frame_rows[rows - rim :], label_ids[rows - rim :]), "tm", up)
    after = lax.ppermute(edge(frame_rows[:rim], label_ids[:rim]), "tm", down)
    main = pl.pallas_call(
        lambda *refs: score_kernel(scale, *refs),
        out_shape=jax.ShapeDtypeStruct((rows, query_count), F32),
        in_specs=[smem] + whole_spec(2),
        out_specs=pl.BlockSpec(memory_space=VMEM),
        compiler_params=params(),
        cost_estimate=cost(2 * rows * width * (rows + query_count), 3 << 20),
    )(scalars, frame_rows, queries)
    main = main.reshape(blk, SUB, query_count)
    scores, powers, stats = pl.pallas_call(
        lambda *refs: smooth_kernel(scale, half, *refs),
        out_shape=[
            jax.ShapeDtypeStruct((blk + 2 * rim, SUB, query_count), F32),
            jax.ShapeDtypeStruct((blk + rim, SUB, query_count), F32),
            jax.ShapeDtypeStruct((2, SUB, LANES), F32),
        ],
        in_specs=[smem] + whole_spec(5),
        out_specs=whole_spec(3),
        scratch_shapes=[VMEM((count, SUB, query_count), F32)],
        compiler_params=params(),
        cost_estimate=cost(4 * rows * query_count * count, 6 << 20),
    )(scalars, main, before, after, queries, kernel)
    others = lax.all_to_all(jnp.broadcast_to(stats[None], (blocks,) + stats.shape), "query", 0, 0)
    ext = jnp.concatenate([before[rim, half:rim], label_ids, after[rim, :half], jnp.zeros((blk - rim,), F32)])
    ext = ext.reshape(SUB + 1, blk)
    tile = jnp.concatenate([ext[:SUB], ext[1:, :rim], jnp.zeros((SUB, LANES - blk - rim), F32)], axis=1)
    chunk_rows = query_count // tms
    part_width = width // recs
    chunks, frame_part = pl.pallas_call(
        lambda *refs: grad_kernel(half, chunk_rows, *refs),
        out_shape=[
            jax.ShapeDtypeStruct((recs, tms, chunk_rows + UNIT, part_width), F32),
            jax.ShapeDtypeStruct((rows, width), F32),
        ],
        in_specs=[smem] + whole_spec(8),
        out_specs=whole_spec(2),
        scratch_shapes=[
            VMEM((count, SUB, query_count), F32),
            VMEM((blk + rim, SUB, query_count), F32),
            VMEM((count, SUB, query_count), F32),
            VMEM((rows, query_count), jnp.bfloat16),
        ],
        compiler_params=params(),
        cost_estimate=cost(4 * rows * query_count * (width + 2 * count), 12 << 20),
    )(scalars, powers, scores, stats, others, tile, frame_rows, queries, kernel)
    frame_sum = lax.psum_scatter(frame_part, "query", scatter_dimension=1, tiled=True)
    chunks = jnp.sum(lax.all_to_all(chunks, "rec", 0, 0), axis=0)
    chunk = jnp.sum(lax.all_to_all(chunks, "tm", 0, 0), axis=0)
    whole = lax.all_gather(chunk, "tm")
    query_sum = whole[:, :chunk_rows].reshape(query_count, part_width)
    halves = query_count // part_width
    tap_sum = whole[:, chunk_rows:].reshape(halves, tms // halves * UNIT, part_width)
    tap_sum = jnp.concatenate([tap_sum[h, :count] for h in range(halves)], axis=1)
    grad_frames = (frame_sum * scale).astype(jnp.bfloat16)[None]
    grad_queries = (query_sum * scale).astype(jnp.bfloat16)
    return (grad_frames, grad_queries, tap_sum)


def solution(mesh):
    in_specs = (P("rec", "tm", None), P("query", None), P(None, "query"), P("rec", "tm"), P("rec"))
    out_specs = (P("rec", "tm", "query"), P("query", "rec"), P(None, "query"))
    return jax.shard_map(
        per_device, mesh=mesh, in_specs=in_specs, out_specs=out_specs, check_vma=False
    )
```

time: 377 us -> 186 us (0.49)
  waiting for transfers between devices: 285 us -> 36 us
  blocking collectives: 23.3 us -> 71.3 us
  Pallas kernels: 0 us -> 22.3 us
  other arithmetic: 25.9 us -> 6.03 us
  starting transfers between devices: 11 us -> 25.5 us
  matrix products: 6.08 us -> 0 us
    psum x1 -> x0, waiting for transfers between devices: 280 us -> none  [per_device(): lax.psum((query_part, kernel_part), ('tm', 'rec'))]
    all_to_all x0 -> x2, waiting for transfers between devices: none -> 35.9 us  [the longest x1 30.4 us: per_device(): chunk = jnp.sum(lax.all_to_all(chunks, 'tm', 0, 0), axis=0)]
    all_to_all x0 -> x1, blocking collectives: none -> 35.7 us  [per_device(): chunks = jnp.sum(lax.all_to_all(chunks, 'rec', 0, 0), axis=0)]
    pallas_call x0 -> x3, Pallas kernels: none -> 22.3 us  [the longest x1 11.9 us: per_device(): pl.pallas_call(lambda *refs: grad_kernel(half, chunk_rows, *refs), out_sh...]
    all_to_all x0 -> x2, starting transfers between devices: none -> 20.3 us  [the longest x1 15.9 us: per_device(): chunk = jnp.sum(lax.all_to_all(chunks, 'tm', 0, 0), axis=0)]
    all_gather x2 -> x1, blocking collectives: 23.3 us -> 35.6 us  [per_device(): whole = lax.all_gather(chunk, 'tm')]
    convert_element_type x2 -> x3, other arithmetic: 10.4 us -> 2.33 us  [the longest x1 0.89 us: edge(): return jnp.concatenate([part.astype(F32), extra], axis=0)]
    reduce_sum x5 -> x2, other arithmetic: 8.67 us -> 1.11 us  [the longest x1 1.06 us: per_device(): chunks = jnp.sum(lax.all_to_all(chunks, 'rec', 0, 0), axis=0)]
  transfers between devices with their start and end apart: 6 -> 5, of which waited for: 3 -> 3; matrix products, arithmetic and copies ran while one was open for 3% -> 2% of each run, Pallas kernels for 0% -> 1%
where the time goes in v2:
time: 186 us; the launch traced here: 184 us
  blocking collectives  71.3 us (38%)
  waiting for transfers between devices  36 us (19%)
  starting transfers between devices  25.5 us (14%)
  Pallas kernels  22.3 us (12%)
  between operations  14.8 us (8%)
  local copies, waits for them, and re-layouts  8.32 us (4%)
  other arithmetic  6.03 us (3%)
    all_to_all x1, blocking collectives, per_device(): chunks = jnp.sum(lax.all_to_all(chunks, 'rec', 0, 0), axis=0)  35.7 us
    all_gather x1, blocking collectives, per_device(): whole = lax.all_gather(chunk, 'tm')  35.6 us
    all_to_all x1, waiting for transfers between devices, per_device(): chunk = jnp.sum(lax.all_to_all(chunks, 'tm', 0, 0), axis=0)  30.4 us
    all_to_all x1, starting transfers between devices, per_device(): chunk = jnp.sum(lax.all_to_all(chunks, 'tm', 0, 0), axis=0)  15.9 us
    pallas_call x1, Pallas kernels, per_device(): pl.pallas_call(lambda *refs: grad_kernel(half, chunk_rows, *refs), out_sh...  11.9 us
    pallas_call x1, Pallas kernels, per_device(): pl.pallas_call(lambda *refs: smooth_kernel(scale, half, *refs), out_shape...  8.64 us
    unnamed x16, local copies, waits for them, and re-layouts  7.28 us
    all_to_all x1, waiting for transfers between devices, per_device(): lax.all_to_all(jnp.broadcast_to(stats[None], (blocks,) + stats.shape), 'q...  5.5 us
  transfers between devices with their start and end apart: 5, of which 3 were waited for; matrix products, arithmetic and copies ran while one was open for 2% of the time, Pallas kernels for 1%

profile of v2, /device:TPU:6, one launch (start us, length us, event | category | flops | bytes accessed | tf_op | source)
XLA Modules:
  0.0 184.4 jit_solution(8627198059963676952)
XLA Ops:
  7.2 0.7 convert_element_type.32
  7.8 0.1 fusion.2
  7.9 0.9 bitcast_convert_fusion
  8.8 3.8 %collective-permute-start = (f32[40,1024]{1,0:T(8,128)S(1)}, f32[40,1024]{1,0:T(8,128)S(1)}, u32[]{:S(2)}, u32[]{:S(2)}) collective-permute-start(f32[40,1024]{1,0:T(8,128)S(1)} %select_maximum_fusion.1), channel_id=1, source_target_pairs={{0,32},{32,64},{64,96},{96,128},{128,160},{160,192},{192,224},{224... | collective-permute-start | bytes 491528 | tf_op jit(solution)/shard_map/ppermute | solution.py:227
  12.7 0.0 copy-start.7
  12.7 1.3 collective-permute-start.1
  14.7 0.1 pad.13.clone
  14.7 0.1 pad_add_fusion.refs_0_
  14.8 0.0 copy-start
  14.8 1.2 copy-done
  16.1 0.0 copy-start.3
  16.1 1.2 copy-done.3
  17.3 0.0 copy-start.1
  17.3 1.8 shard_map.76
  19.1 0.0 copy-start.5
  19.1 1.0 copy-done.5
  20.1 0.0 collective-permute-done.refs_2_
  20.1 0.1 slice_bitcast_fusion.3
  20.2 0.1 pad_maximum_fusion.1
  20.2 0.1 slice.52
  20.3 0.1 collective-permute-done.1.refs_3_
  20.4 0.1 pad_maximum_fusion.2
  20.5 0.1 reshape.35
  20.6 0.0 copy-done.7
  20.6 0.0 copy-done.1
  20.6 0.0 copy-start.6
  20.6 1.2 copy-done.6
  21.8 8.6 %shard_map.77 = (f32[128,8,512]{2,1,0:T(8,128)S(1)}, f32[96,8,512]{2,1,0:T(8,128)S(1)}, f32[2,8,128]{2,1,0:T(8,128)S(1)}) custom-call(s32[3]{0:T(128)S(1)} %pad_add_fusion.refs_0_, f32[64,8,512]{2,1,0:T(8,128)S(1)} %bitcast.26, f32[40,1024]{1,0:T(8,128)S(1)} %collective-permute-done.refs_2_, f32[40,1024]{1,0:T(8,128)S(1)} %collective-permute-done.1.refs_3_, ...), custom_call_target="tpu_custom_call" | custom-call | flops 34603008 | bytes 6291456 | tf_op jit(solution)/shard_map/pallas_call | solution.py:238
  30.5 0.0 copy-start.2
  30.5 1.4 copy-done.2
  31.9 0.6 broadcast_in_dim.8
  32.5 4.5 %all-to-all-start = ((f32[8,2,8,128]{3,2,1,0:T(8,128)}), f32[8,2,8,128]{3,2,1,0:T(8,128)S(1)}, u32[]{:S(2)}, u32[]{:S(2)}) async-start(f32[8,2,8,128]{3,2,1,0:T(8,128)} %broadcast_in_dim.8), calls=%async_computation | async-start | bytes 131072 | tf_op jit(solution)/shard_map/all_to_all | solution.py:251
  37.0 0.0 reduce-scatter.2.cloned.1.call-start
  37.0 0.1 maximum_maximum_fusion.refs_5_
  37.1 5.5 %all-to-all-done.refs_4_ = f32[8,2,8,128]{3,2,1,0:T(8,128)S(1)} async-done(((f32[8,2,8,128]{3,2,1,0:T(8,128)}), f32[8,2,8,128]{3,2,1,0:T(8,128)S(1)}, u32[]{:S(2)}, u32[]{:S(2)}) %all-to-all-start) | async-done | bytes 65568 | tf_op jit(solution)/shard_map/all_to_all | solution.py:251
  42.6 0.0 copy-start.4
  42.6 1.2 copy-done.4
  43.9 11.9 %shard_map.78 = (f32[4,16,40,256]{3,2,1,0:T(8,128)}, f32[512,1024]{1,0:T(8,128)}) custom-call(s32[3]{0:T(128)S(1)} %pad_add_fusion.refs_0_, f32[96,8,512]{2,1,0:T(8,128)S(1)} %get-tuple-element.8.refs_1_, f32[128,8,512]{2,1,0:T(8,128)} %copy-done.2, f32[2,8,128]{2,1,0:T(8,128)S(1)} %get-tuple-element.10.refs_3_, f32[8,2,8,128]{3,2,1,0:T(8,128)S(1)} %all-to-all-done.refs_4_, ...), custom_call_target="tpu_custom_call" | custom-call | flops 1142947840 | bytes 12582912 | tf_op jit(solution)/shard_map/pallas_call | solution.py:257
  55.7 0.0 reduce-scatter.2.cloned.1.call-update
  55.8 35.7 %all_to_all.15 = f32[4,16,40,256]{3,2,1,0:T(8,128)S(1)} all-to-all(f32[4,16,40,256]{3,2,1,0:T(8,128)} %get-tuple-element.12), channel_id=1, replica_groups=mesh['tm'=16,'query'=8,'rec'=4] {'rec'}, dimensions={0} | all-to-all | bytes 5242880 | tf_op jit(solution)/shard_map/all_to_all | solution.py:275
  91.5 1.1 reduce_sum.18
  92.5 15.9 %all-to-all-start.2 = ((f32[16,40,256]{2,1,0:T(8,128)}), f32[16,40,256]{2,1,0:T(8,128)S(1)}, u32[]{:S(2)}, u32[]{:S(2)}) async-start(f32[16,40,256]{2,1,0:T(8,128)} %reduce_sum.18), calls=%async_computation.3 | async-start | bytes 1310720 | tf_op jit(solution)/shard_map/all_to_all | solution.py:276
  108.4 0.0 reduce-scatter.2.cloned.1.call-done
  108.4 1.6 fusion.1
  110.0 30.4 %all-to-all-done.2 = f32[16,40,256]{2,1,0:T(8,128)S(1)} async-done(((f32[16,40,256]{2,1,0:T(8,128)}), f32[16,40,256]{2,1,0:T(8,128)S(1)}, u32[]{:S(2)}, u32[]{:S(2)}) %all-to-all-start.2) | async-done | bytes 655392 | tf_op jit(solution)/shard_map/all_to_all | solution.py:276
  140.5 35.6 %all-gather = f32[640,256]{1,0:T(8,128)S(1)} all-gather(f32[40,256]{1,0:T(8,128)S(1)} %reduce_sum.19), channel_id=2, replica_groups=mesh['tm'=16,'query'=8,'rec'=4] {'tm'}, dimensions={0}, use_global_device_ids=true | all-gather | bytes 696320 | tf_op jit(solution)/shard_map/all_gather | solution.py:277
  176.1 0.8 fusion
  176.9 0.6 pad_maximum_fusion
  (9 shorter events, 0.1 us)
Async XLA Ops:
  8.8 11.2 %collective-permute-start = (f32[40,1024]{1,0:T(8,128)S(1)}, f32[40,1024]{1,0:T(8,128)S(1)}, u32[]{:S(2)}, u32[]{:S(2)}) collective-permute-start(f32[40,1024]{1,0:T(8,128)S(1)} %select_maximum_fusion.1), channel_id=1, source_target_pairs={{0,32},{32,64},{64,96},{96,128},{128,160},{160,192},{192,224},{224... | collective-permute-start | bytes 491528 | tf_op jit(solution)/shard_map/ppermute | solution.py:227
  12.7 7.9 %copy-start.7 = (f32[33,512]{1,0:T(8,128)S(1)}, f32[33,512]{1,0:T(8,128)}, u32[]{:S(2)}) copy-start(f32[33,512]{1,0:T(8,128)} %refs_8_.1) | copy-start | bytes 202756
  12.7 7.7 %collective-permute-start.1 = (f32[40,1024]{1,0:T(8,128)S(1)}, f32[40,1024]{1,0:T(8,128)S(1)}, u32[]{:S(2)}, u32[]{:S(2)}) collective-permute-start(f32[40,1024]{1,0:T(8,128)S(1)} %select_maximum_fusion), channel_id=1, source_target_pairs={{32,0},{64,32},{96,64},{128,96},{160,128},{192,160},{224,192},{256... | collective-permute-start | bytes 491528 | tf_op jit(solution)/shard_map/ppermute | solution.py:228
  14.8 1.2 copy-start
  16.1 1.2 copy-start.3
  17.3 3.3 %copy-start.1 = (bf16[512,1024]{1,0:T(8,128)(2,1)S(1)}, bf16[512,1024]{1,0:T(8,128)(2,1)}, u32[]{:S(2)}) copy-start(bf16[512,1024]{1,0:T(8,128)(2,1)} %refs_7_.1) | copy-start | bytes 3145732
  19.1 1.0 copy-start.5
  20.6 1.2 copy-start.6
  30.5 1.4 copy-start.2
  32.5 10.1 %all-to-all-start = ((f32[8,2,8,128]{3,2,1,0:T(8,128)}), f32[8,2,8,128]{3,2,1,0:T(8,128)S(1)}, u32[]{:S(2)}, u32[]{:S(2)}) async-start(f32[8,2,8,128]{3,2,1,0:T(8,128)} %broadcast_in_dim.8), calls=%async_computation | async-start | bytes 131072 | tf_op jit(solution)/shard_map/all_to_all | solution.py:251
  37.0 71.4 %reduce-scatter.2.cloned.1.call-start = ((), (), s32[]{:S(2)}) async-start(), calls=%async_computation.4 | async-start | bytes 2359296 | tf_op jit(solution)/shard_map/reduce_scatter | solution.py:274
  42.6 1.2 copy-start.4
  92.5 47.9 %all-to-all-start.2 = ((f32[16,40,256]{2,1,0:T(8,128)}), f32[16,40,256]{2,1,0:T(8,128)S(1)}, u32[]{:S(2)}, u32[]{:S(2)}) async-start(f32[16,40,256]{2,1,0:T(8,128)} %reduce_sum.18), calls=%async_computation.3 | async-start | bytes 1310720 | tf_op jit(solution)/shard_map/all_to_all | solution.py:276
Sparse Core Ops, SparseCore 0:
  55.9 45.8 reduce-scatter.1

commit v3 on v2

--- a/solution.py
+++ b/solution.py
@@ -18,8 +18,8 @@
     return [pl.BlockSpec(memory_space=VMEM)] * count
 
 
-def params():
-    return pltpu.CompilerParams(vmem_limit_bytes=48 * 1024 * 1024)
+def params(mib):
+    return pltpu.CompilerParams(vmem_limit_bytes=mib << 20)
 
 
 def cost(flops, bytes_accessed):
@@ -113,14 +113,12 @@
 
 
 def grad_kernel(
-    half, chunk_rows, scalars, powers, scores, mine, others, labels, frames, queries, taps,
-    chunks, frame_part, wide, grads, tap_grads, placed,
+    half, scalars, powers, mine, others, labels, frames, taps, grads, score_grad, ahead, behind, wide, placed,
 ):
     blk = powers.shape[0] - 2 * half
     rows = blk * SUB
     count = 2 * half + 1
-    width = queries.shape[1]
-    query_count = queries.shape[0]
+    query_count = taps.shape[1]
     groups = query_count // LANES
     broadcast_taps(taps, wide, count)
     tops = others[:, 0]
@@ -141,10 +139,46 @@
         l = pltpu.roll(label, turn, 1)
         for u in range(UNIT):
             positive = jnp.where(ids == l[:, u : u + 1], 1.0, 0.0)
-            grads[first + u] = powers[first + u] * w[:, u : u + 1] - positive * 1.0
+            grads[first + u] = powers[first + u] * w[:, u : u + 1] - positive
         return 0
 
     lax.fori_loop(0, (blk + 2 * half) // UNIT, place, 0)
+
+    def spread(b, _):
+        first = b * UNIT
+        turn = lax.rem(2 * LANES - half - first, LANES)
+        kept = pltpu.roll(keep, turn, 1)
+        for g in range(groups):
+            cols = slice(g * LANES, (g + 1) * LANES)
+            sums = tap_block(lambda t: grads[first + t, :, cols], wide, g, count, True)
+            sums = [sums[u] * kept[:, u : u + 1] for u in range(UNIT)]
+            block = jnp.concatenate(sums, axis=0).astype(jnp.bfloat16)
+            placed[pl.ds(pl.multiple_of(first * SUB, UNIT * SUB), UNIT * SUB), cols] = block
+        return 0
+
+    lax.fori_loop(0, blk // UNIT, spread, 0)
+    natural = jnp.dot(placement(rows, blk, True), placed[...], preferred_element_type=F32)
+    natural = natural.astype(jnp.bfloat16)
+    score_grad[...] = natural
+    far = column_block(frames, scalars[5], ahead.shape[1])
+    part = jnp.dot(turn_over(natural), far, preferred_element_type=F32)
+    ahead[...] = part[: query_count // 2]
+    behind[...] = part[query_count // 2 :]
+
+
+def column_block(frames, index, width):
+    return frames[:, pl.ds(pl.multiple_of(index * width, LANES), width)]
+
+
+def turn_over(score_grad):
+    return score_grad.astype(F32).T.astype(jnp.bfloat16)
+
+
+def own_kernel(half, scalars, grads, scores, score_grad, frames, own, taps_out, tap_grads):
+    blk = grads.shape[0] - 2 * half
+    count = 2 * half + 1
+    query_count = score_grad.shape[1]
+    groups = query_count // LANES
     tap_grads[...] = jnp.zeros_like(tap_grads)
 
     def correlate(b, _):
@@ -161,41 +195,48 @@
         return 0
 
     lax.fori_loop(0, blk // UNIT, correlate, 0)
-
-    def spread(b, _):
-        first = b * UNIT
-        turn = lax.rem(2 * LANES - half - first, LANES)
-        kept = pltpu.roll(keep, turn, 1)
-        for g in range(groups):
-            cols = slice(g * LANES, (g + 1) * LANES)
-            sums = tap_block(lambda t: grads[first + t, :, cols], wide, g, count, True)
-            sums = [sums[u] * kept[:, u : u + 1] for u in range(UNIT)]
-            block = jnp.concatenate(sums, axis=0).astype(jnp.bfloat16)
-            placed[pl.ds(pl.multiple_of(first * SUB, UNIT * SUB), UNIT * SUB), cols] = block
-        return 0
-
-    lax.fori_loop(0, blk // UNIT, spread, 0)
-    score_grad = jnp.dot(placement(rows, blk, True), placed[...], preferred_element_type=F32)
-    frame_part[...] = jnp.dot(score_grad.astype(jnp.bfloat16), queries[...], preferred_element_type=F32)
-    turned = score_grad.T.astype(jnp.bfloat16)
-    recs, tms, padded_rows, part_width = chunks.shape
     parts = jnp.sum(tap_grads[...], axis=1)
-    parts = jnp.concatenate([parts, jnp.zeros((padded_rows_of(count) - count, query_count), F32)], axis=0)
+    tall = padded_rows_of(count)
+    parts = jnp.concatenate([parts, jnp.zeros((tall - count, query_count), F32)], axis=0)
+    part_width = own.shape[1]
+    for h in range(query_count // part_width):
+        taps_out[h * tall : (h + 1) * tall, :] = parts[:, h * part_width : (h + 1) * part_width]
+    mine = column_block(frames, scalars[3], part_width)
+    own[...] = jnp.dot(turn_over(score_grad[...]), mine, preferred_element_type=F32)
+
+
+def near_kernel(scalars, score_grad, frames, queries, taps_in, from_behind, from_ahead, ahead, behind, frame_part):
+    query_count = score_grad.shape[1]
+    part_width = ahead.shape[1]
+    middle = query_count // 2
+    turned = turn_over(score_grad[...])
+    part = jnp.dot(turned, column_block(frames, scalars[4], part_width), preferred_element_type=F32)
+    ahead[:middle, :] = part[:middle] + from_behind[...]
+    ahead[middle:query_count, :] = part[middle:]
+    ahead[query_count:, :] = taps_in[...]
+    part = jnp.dot(turned, column_block(frames, scalars[6], part_width), preferred_element_type=F32)
+    behind[:middle, :] = part[:middle]
+    behind[middle:query_count, :] = part[middle:] + from_ahead[...]
+    behind[query_count:, :] = taps_in[...]
+    frame_part[...] = jnp.dot(score_grad[...], queries[...], preferred_element_type=F32)
+
+
+def sum_kernel(own, taps_own, from_behind, from_ahead, taps_far, chunks):
+    tms, padded_rows, _ = chunks.shape
+    query_count = own.shape[0]
+    chunk_rows = query_count // tms
     tap_rows = padded_rows - chunk_rows
-    halves = query_count // part_width
-    per_half = tms // halves
-    for r in range(recs):
-        part = jnp.dot(turned, frames[:, r * part_width : (r + 1) * part_width], preferred_element_type=F32)
-        for z in range(tms):
-            chunks[r, z, :chunk_rows, :] = part[z * chunk_rows : (z + 1) * chunk_rows, :]
-            start = (z % per_half) * tap_rows
-            h = z // per_half
-            if start < count:
-                chunks[r, z, chunk_rows:, :] = parts[
-                    start : start + tap_rows, h * part_width : (h + 1) * part_width
-                ]
-            else:
-                chunks[r, z, chunk_rows:, :] = jnp.zeros((tap_rows, part_width), F32)
+    for z in range(tms):
+        rows = slice(z * chunk_rows, (z + 1) * chunk_rows)
+        chunks[z, :chunk_rows, :] = own[rows, :] + from_behind[rows, :] + from_ahead[rows, :]
+        if z * tap_rows < taps_own.shape[0]:
+            rows = slice(z * tap_rows, (z + 1) * tap_rows)
+            late = slice(query_count + z * tap_rows, query_count + (z + 1) * tap_rows)
+            chunks[z, chunk_rows:, :] = (
+                taps_own[rows, :] + taps_far[rows, :] + from_behind[late, :] + from_ahead[late, :]
+            )
+        else:
+            chunks[z, chunk_rows:, :] = jnp.zeros((tap_rows, own.shape[1]), F32)
 
 
 def padded_rows_of(count):
@@ -213,8 +254,10 @@
     blk = rows // SUB
     scale = 10.0 / math.sqrt(width)
     recs, tms, blocks = lax.axis_size("rec"), lax.axis_size("tm"), lax.axis_size("query")
+    rec = lax.axis_index("rec")
+    ring = [(rec + step) % recs for step in range(4)]
     scalars = jnp.stack(
-        [lax.axis_index("tm") * rows, lengths[0], lax.axis_index("query") * query_count]
+        [lax.axis_index("tm") * rows, lengths[0], lax.axis_index("query") * query_count] + ring
     ).astype(jnp.int32)
     smem = pl.BlockSpec(memory_space=pltpu.SMEM)
 
@@ -231,7 +274,7 @@
         out_shape=jax.ShapeDtypeStruct((rows, query_count), F32),
         in_specs=[smem] + whole_spec(2),
         out_specs=pl.BlockSpec(memory_space=VMEM),
-        compiler_params=params(),
+        compiler_params=params(12),
         cost_estimate=cost(2 * rows * width * (rows + query_count), 3 << 20),
     )(scalars, frame_rows, queries)
     main = main.reshape(blk, SUB, query_count)
@@ -245,39 +288,79 @@
         in_specs=[smem] + whole_spec(5),
         out_specs=whole_spec(3),
         scratch_shapes=[VMEM((count, SUB, query_count), F32)],
-        compiler_params=params(),
+        compiler_params=params(12),
         cost_estimate=cost(4 * rows * query_count * count, 6 << 20),
     )(scalars, main, before, after, queries, kernel)
-    others = lax.all_to_all(jnp.broadcast_to(stats[None], (blocks,) + stats.shape), "query", 0, 0)
     ext = jnp.concatenate([before[rim, half:rim], label_ids, after[rim, :half], jnp.zeros((blk - rim,), F32)])
     ext = ext.reshape(SUB + 1, blk)
     tile = jnp.concatenate([ext[:SUB], ext[1:, :rim], jnp.zeros((SUB, LANES - blk - rim), F32)], axis=1)
+    stats, tile = lax.optimization_barrier((stats, tile))
+    others = lax.all_to_all(jnp.broadcast_to(stats[None], (blocks,) + stats.shape), "query", 0, 0)
     chunk_rows = query_count // tms
     part_width = width // recs
-    chunks, frame_part = pl.pallas_call(
-        lambda *refs: grad_kernel(half, chunk_rows, *refs),
+    middle = query_count // 2
+    grads, score_grad, far_a, far_b = pl.pallas_call(
+        lambda *refs: grad_kernel(half, *refs),
         out_shape=[
-            jax.ShapeDtypeStruct((recs, tms, chunk_rows + UNIT, part_width), F32),
-            jax.ShapeDtypeStruct((rows, width), F32),
+            jax.ShapeDtypeStruct((blk + rim, SUB, query_count), F32),
+            jax.ShapeDtypeStruct((rows, query_count), jnp.bfloat16),
+            jax.ShapeDtypeStruct((middle, part_width), F32),
+            jax.ShapeDtypeStruct((query_count - middle, part_width), F32),
         ],
-        in_specs=[smem] + whole_spec(8),
-        out_specs=whole_spec(2),
+        in_specs=[smem] + whole_spec(6),
+        out_specs=whole_spec(4),
         scratch_shapes=[
-            VMEM((count, SUB, query_count), F32),
-            VMEM((blk + rim, SUB, query_count), F32),
             VMEM((count, SUB, query_count), F32),
             VMEM((rows, query_count), jnp.bfloat16),
         ],
-        compiler_params=params(),
-        cost_estimate=cost(4 * rows * query_count * (width + 2 * count), 12 << 20),
-    )(scalars, powers, scores, stats, others, tile, frame_rows, queries, kernel)
+        compiler_params=params(16),
+        cost_estimate=cost(2 * rows * query_count * (width + 2 * count), 8 << 20),
+    )(scalars, powers, stats, others, tile, frame_rows, kernel)
+    onward = [(i, (i + 1) % recs) for i in range(recs)]
+    back = [(j, i) for i, j in onward]
+    far_a = lax.ppermute(far_a, "rec", onward)
+    far_b = lax.ppermute(far_b, "rec", back)
+    halves = query_count // part_width
+    tap_rows = halves * padded_rows_of(count)
+    own, taps_own = pl.pallas_call(
+        lambda *refs: own_kernel(half, *refs),
+        out_shape=[
+            jax.ShapeDtypeStruct((query_count, part_width), F32),
+            jax.ShapeDtypeStruct((tap_rows, part_width), F32),
+        ],
+        in_specs=[smem] + whole_spec(4),
+        out_specs=whole_spec(2),
+        scratch_shapes=[VMEM((count, SUB, query_count), F32)],
+        compiler_params=params(16),
+        cost_estimate=cost(4 * rows * query_count * (width + 2 * count), 16 << 20),
+    )(scalars, grads, scores, score_grad, frame_rows)
+    across = [(i, (i + 2) % recs) for i in range(recs)]
+    taps_far = lax.ppermute(taps_own, "rec", across)
+    near = jax.ShapeDtypeStruct((query_count + tap_rows, part_width), F32)
+    near_a, near_b, frame_part = pl.pallas_call(
+        near_kernel,
+        out_shape=[near, near, jax.ShapeDtypeStruct((rows, width), F32)],
+        in_specs=[smem] + whole_spec(6),
+        out_specs=whole_spec(3),
+        compiler_params=params(12),
+        cost_estimate=cost(rows * query_count * width, 4 << 20),
+    )(scalars, score_grad, frame_rows, queries, taps_own, far_a, far_b)
     frame_sum = lax.psum_scatter(frame_part, "query", scatter_dimension=1, tiled=True)
-    chunks = jnp.sum(lax.all_to_all(chunks, "rec", 0, 0), axis=0)
+    near_a = lax.ppermute(near_a, "rec", onward)
+    near_b = lax.ppermute(near_b, "rec", back)
+    chunks = pl.pallas_call(
+        sum_kernel,
+        out_shape=jax.ShapeDtypeStruct((tms, chunk_rows + UNIT, part_width), F32),
+        in_specs=whole_spec(5),
+        out_specs=pl.BlockSpec(memory_space=VMEM),
+        compiler_params=params(8),
+        cost_estimate=cost(4 * query_count * part_width, 4 << 20),
+    )(own, taps_own, near_a, near_b, taps_far)
     chunk = jnp.sum(lax.all_to_all(chunks, "tm", 0, 0), axis=0)
+    frame_sum, chunk = lax.optimization_barrier((frame_sum, chunk))
     whole = lax.all_gather(chunk, "tm")
     query_sum = whole[:, :chunk_rows].reshape(query_count, part_width)
-    halves = query_count // part_width
-    tap_sum = whole[:, chunk_rows:].reshape(halves, tms // halves * UNIT, part_width)
+    tap_sum = whole[: tap_rows // UNIT, chunk_rows:].reshape(halves, tap_rows // halves, part_width)
     tap_sum = jnp.concatenate([tap_sum[h, :count] for h in range(halves)], axis=1)
     grad_frames = (frame_sum * scale).astype(jnp.bfloat16)[None]
     grad_queries = (query_sum * scale).astype(jnp.bfloat16)

time: 186 us -> 188 us (1.011)
  blocking collectives: 71.3 us -> 91.7 us
  waiting for transfers between devices: 36 us -> 17.8 us
  starting transfers between devices: 25.5 us -> 19 us
  local copies, waits for them, and re-layouts: 8.32 us -> 12.1 us
  other arithmetic: 6.03 us -> 8.27 us
    all_to_all x2 -> x0, waiting for transfers between devices: 35.9 us -> none  [the longest x1 30.4 us: per_device(): chunk = jnp.sum(lax.all_to_all(chunks, 'tm', 0, 0), axis=0)]
    all_to_all x1 -> x2, blocking collectives: 35.7 us -> 59.6 us  [the longest x1 49.7 us: per_device(): chunk = jnp.sum(lax.all_to_all(chunks, 'tm', 0, 0), axis=0)]
    all_to_all x2 -> x0, starting transfers between devices: 20.3 us -> none  [the longest x1 15.9 us: per_device(): chunk = jnp.sum(lax.all_to_all(chunks, 'tm', 0, 0), axis=0)]
    ppermute x0 -> x5, waiting for transfers between devices: none -> 17.7 us  [the longest x1 11.7 us: per_device(): taps_far = lax.ppermute(taps_own, 'rec', across)]
    ppermute x0 -> x5, starting transfers between devices: none -> 13.8 us  [the longest x1 3.92 us: per_device(): near_b = lax.ppermute(near_b, 'rec', back)]
    all_gather x1, blocking collectives: 35.6 us -> 32 us  [per_device(): whole = lax.all_gather(chunk, 'tm')]
    pallas_call x1 -> x4, Pallas kernels: 11.9 us -> 11.1 us  [the longest x1 6.06 us: per_device(): pl.pallas_call(lambda *refs: grad_kernel(half, *refs), out_shape=[jax.Sha...]
    unnamed x16 -> x30, local copies, waits for them, and re-layouts: 7.28 us -> 7.23 us
  transfers between devices with their start and end apart: 5 -> 8, of which waited for: 3 -> 4; matrix products, arithmetic and copies ran while one was open for 2% -> 2% of each run, Pallas kernels for 1% -> 3%
where the time goes in v3:
time: 188 us; the launch traced here: 186 us
  blocking collectives  91.7 us (49%)
  Pallas kernels  22.6 us (12%)
  starting transfers between devices  19 us (10%)
  waiting for transfers between devices  17.8 us (9%)
  between operations  14.9 us (8%)
  local copies, waits for them, and re-layouts  12.1 us (6%)
  other arithmetic  8.27 us (4%)
    all_to_all x1, blocking collectives, per_device(): chunk = jnp.sum(lax.all_to_all(chunks, 'tm', 0, 0), axis=0)  49.7 us
    all_gather x1, blocking collectives, per_device(): whole = lax.all_gather(chunk, 'tm')  32 us
    ppermute x1, waiting for transfers between devices, per_device(): taps_far = lax.ppermute(taps_own, 'rec', across)  11.7 us
    all_to_all x1, blocking collectives, per_device(): lax.all_to_all(jnp.broadcast_to(stats[None], (blocks,) + stats.shape), 'q...  9.91 us
    pallas_call x1, Pallas kernels, per_device(): pl.pallas_call(lambda *refs: smooth_kernel(scale, half, *refs), out_shape...  9.65 us
    unnamed x30, local copies, waits for them, and re-layouts  7.23 us
    pallas_call x1, Pallas kernels, per_device(): pl.pallas_call(lambda *refs: grad_kernel(half, *refs), out_shape=[jax.Sha...  6.06 us
    ppermute x1, waiting for transfers between devices, per_device(): far_b = lax.ppermute(far_b, 'rec', back)  4.27 us
  transfers between devices with their start and end apart: 8, of which 4 were waited for; matrix products, arithmetic and copies ran while one was open for 2% of the time, Pallas kernels for 3%

profile of v3, /device:TPU:6, one launch (start us, length us, event | category | flops | bytes accessed | tf_op | source)
XLA Modules:
  0.0 186.3 jit_solution(8679401324690340469)
XLA Ops:
  7.2 0.0 reduce-scatter.2.cloned.1.call-start
  7.2 0.7 convert_element_type.32
  7.9 0.1 fusion.2
  8.0 1.0 bitcast_convert_fusion
  9.0 0.7 select_maximum_fusion.1
  9.6 3.8 %collective-permute-start = (f32[40,1024]{1,0:T(8,128)}, f32[40,1024]{1,0:T(8,128)S(1)}, u32[]{:S(2)}, u32[]{:S(2)}) collective-permute-start(f32[40,1024]{1,0:T(8,128)} %select_maximum_fusion.1), channel_id=1, source_target_pairs={{0,32},{32,64},{64,96},{96,128},{128,160},{160,192},{192,224},{224... | collective-permute-start | bytes 491528 | tf_op jit(solution)/shard_map/ppermute | solution.py:270
  13.5 0.7 select_maximum_fusion
  14.1 1.3 collective-permute-start.1
  16.1 0.6 pad.13.clone
  16.8 0.1 stack.27.refs_0_.scalars
  16.9 0.5 copy-done.6
  17.4 1.2 copy-done
  18.6 1.2 copy-done.2
  19.8 1.8 shard_map.76
  21.7 0.1 slice_bitcast_fusion.3
  21.8 0.1 pad_maximum_fusion.1
  21.8 0.4 copy-done.13
  22.3 0.6 slice.51
  22.9 1.3 slice.52
  24.2 1.4 pad_maximum_fusion.2
  25.6 1.4 reshape.35
  26.9 0.7 slice.63
  27.6 0.8 maximum_maximum_fusion.refs_4_
  28.4 0.6 copy-done.7
  29.0 9.6 %shard_map.77 = (f32[128,8,512]{2,1,0:T(8,128)S(1)}, f32[96,8,512]{2,1,0:T(8,128)S(1)}, f32[2,8,128]{2,1,0:T(8,128)S(1)}) custom-call(s32[7]{0:T(128)S(1)} %copy-done.7, f32[64,8,512]{2,1,0:T(8,128)S(1)} %bitcast.32, f32[40,1024]{1,0:T(8,128)S(1)} %collective-permute-done.refs_2_, f32[40,1024]{1,0:T(8,128)S(1)} %collective-permute-done.1.refs_3_, ...), custom_call_target="tpu_custom_call" | custom-call | flops 34603008 | bytes 6291456 | tf_op jit(solution)/shard_map/pallas_call | solution.py:281
  38.6 9.9 %all_to_all.10.refs_3_ = f32[8,2,8,128]{3,2,1,0:T(8,128)S(1)} all-to-all(f32[8,2,8,128]{3,2,1,0:T(8,128)S(1)} %broadcast_in_dim.19), channel_id=1, replica_groups=mesh['tm'=16,'query'=8,'rec'=4] {'query'}, dimensions={0} | all-to-all | bytes 131072 | tf_op jit(solution)/shard_map/all_to_all | solution.py:298
  48.5 6.1 %shard_map.78 = (f32[96,8,512]{2,1,0:T(8,128)S(1)}, bf16[512,512]{1,0:T(8,128)(2,1)S(1)}, f32[256,256]{1,0:T(8,128)S(1)}, f32[256,256]{1,0:T(8,128)S(1)}) custom-call(s32[7]{0:T(128)S(1)} %copy-done.7, f32[96,8,512]{2,1,0:T(8,128)S(1)} %get-tuple-element.19.refs_1_, f32[2,8,128]{2,1,0:T(8,128)S(1)} %get-tuple-element.21.refs_2_, ...), custom_call_target="tpu_custom_call" | custom-call | flops 571473920 | bytes 8388608 | tf_op jit(solution)/shard_map/pallas_call | solution.py:302
  54.6 3.3 %collective-permute-start.2 = (f32[256,256]{1,0:T(8,128)S(1)}, f32[256,256]{1,0:T(8,128)S(1)}, u32[]{:S(2)}, u32[]{:S(2)}) collective-permute-start(f32[256,256]{1,0:T(8,128)S(1)} %get-tuple-element.27), channel_id=1, source_target_pairs={{0,1},{1,2},{2,3},{3,0},{4,5},{5,6},{6,7},{7,4},{8,9},{9,10},{10,1... | collective-permute-start | bytes 786440 | tf_op jit(solution)/shard_map/ppermute | solution.py:321
  58.0 2.5 %collective-permute-start.3 = (f32[256,256]{1,0:T(8,128)S(1)}, f32[256,256]{1,0:T(8,128)S(1)}, u32[]{:S(2)}, u32[]{:S(2)}) collective-permute-start(f32[256,256]{1,0:T(8,128)S(1)} %get-tuple-element.28), channel_id=1, source_target_pairs={{1,0},{2,1},{3,2},{0,3},{5,4},{6,5},{7,6},{4,7},{9,8},{10,9},{11,1... | collective-permute-start | bytes 786440 | tf_op jit(solution)/shard_map/ppermute | solution.py:322
  60.5 3.4 %shard_map.79 = (f32[512,256]{1,0:T(8,128)S(1)}, f32[80,256]{1,0:T(8,128)S(1)}) custom-call(s32[7]{0:T(128)S(1)} %copy-done.7, f32[96,8,512]{2,1,0:T(8,128)S(1)} %get-tuple-element.24.refs_1_, f32[128,8,512]{2,1,0:T(8,128)S(1)} %get-tuple-element.25.refs_2_, bf16[512,512]{1,0:T(8,128)(2,1)S(1)} %get-tuple-element.23.refs_3_.score_grad, ...), custom_call_target="tpu_custom_call" | custom-call | flops 1142947840 | bytes 16777216 | tf_op jit(solution)/shard_map/pallas_call | solution.py:325
  63.9 0.6 collective-permute-done.2.from_behind
  64.4 4.3 %collective-permute-done.3.from_ahead = f32[256,256]{1,0:T(8,128)S(1)} collective-permute-done((f32[256,256]{1,0:T(8,128)S(1)}, f32[256,256]{1,0:T(8,128)S(1)}, u32[]{:S(2)}, u32[]{:S(2)}) %collective-permute-start.3) | collective-permute-done | bytes 262176 | tf_op jit(solution)/shard_map/ppermute | solution.py:322
  68.7 1.6 shard_map.80
  70.3 1.3 copy-done.4
  71.7 0.8 copy-done.9
  72.5 1.0 copy-done.10
  73.6 1.9 %collective-permute-start.4 = (f32[592,256]{1,0:T(8,128)S(1)}, f32[592,256]{1,0:T(8,128)S(1)}, u32[]{:S(2)}, u32[]{:S(2)}) collective-permute-start(f32[592,256]{1,0:T(8,128)S(1)} %copy-done.10), channel_id=1, source_target_pairs={{0,1},{1,2},{2,3},{3,0},{4,5},{5,6},{6,7},{7,4},{8,9},{9,10},{10,1... | collective-permute-start | bytes 1818632 | tf_op jit(solution)/shard_map/ppermute | solution.py:349
  75.5 3.9 %collective-permute-start.5 = (f32[592,256]{1,0:T(8,128)S(1)}, f32[592,256]{1,0:T(8,128)S(1)}, u32[]{:S(2)}, u32[]{:S(2)}) collective-permute-start(f32[592,256]{1,0:T(8,128)S(1)} %get-tuple-element.32), channel_id=1, source_target_pairs={{1,0},{2,1},{3,2},{0,3},{5,4},{6,5},{7,6},{4,7},{9,8},{10,9},{11,1... | collective-permute-start | bytes 1818632 | tf_op jit(solution)/shard_map/ppermute | solution.py:350
  79.4 2.2 %collective-permute-start.6 = (f32[80,256]{1,0:T(8,128)S(1)}, f32[80,256]{1,0:T(8,128)S(1)}, u32[]{:S(2)}, u32[]{:S(2)}) collective-permute-start(f32[80,256]{1,0:T(8,128)S(1)} %get-tuple-element.26.taps_in.taps_own), channel_id=1, source_target_pairs={{0,2},{1,3},{2,0},{3,1},{4,6},{5,7},{6,4},{7,5},{8,10},{9,11},{10,... | collective-permute-start | bytes 245768 | tf_op jit(solution)/shard_map/ppermute | solution.py:338
  81.6 11.7 %collective-permute-done.6.taps_far = f32[80,256]{1,0:T(8,128)S(1)} collective-permute-done((f32[80,256]{1,0:T(8,128)S(1)}, f32[80,256]{1,0:T(8,128)S(1)}, u32[]{:S(2)}, u32[]{:S(2)}) %collective-permute-start.6) | collective-permute-done | bytes 81952 | tf_op jit(solution)/shard_map/ppermute | solution.py:338
  93.3 1.1 collective-permute-done.5.from_ahead
  94.5 0.1 shard_map.81
  94.5 49.7 %all_to_all.11 = f32[16,40,256]{2,1,0:T(8,128)S(1)} all-to-all(f32[16,40,256]{2,1,0:T(8,128)S(1)} %shard_map.81), channel_id=1, replica_groups=mesh['tm'=16,'query'=8,'rec'=4] {'tm'}, dimensions={0} | all-to-all | bytes 1310720 | tf_op jit(solution)/shard_map/all_to_all | solution.py:359
  144.3 0.0 reduce-scatter.2.cloned.1.call-done
  144.4 32.0 %all-gather = f32[640,256]{1,0:T(8,128)S(1)} all-gather(f32[40,256]{1,0:T(8,128)S(1)} %reduce_sum.9), channel_id=2, replica_groups=mesh['tm'=16,'query'=8,'rec'=4] {'tm'}, dimensions={0}, use_global_device_ids=true | all-gather | bytes 696320 | tf_op jit(solution)/shard_map/all_gather | solution.py:361
  176.4 0.8 fusion
  177.2 1.6 fusion.1
  178.8 0.6 pad_maximum_fusion
  (32 shorter events, 0.1 us)
Async XLA Ops:
  7.2 137.2 %reduce-scatter.2.cloned.1.call-start = ((), (), s32[]{:S(2)}) async-start(), calls=%async_computation.3 | async-start | bytes 2359296 | tf_op jit(solution)/shard_map/reduce_scatter | solution.py:348
  7.9 6.3 %copy-start.11 = (f32[1,512]{1,0:T(1,128)}, f32[1,512]{1,0:T(1,128)S(1)}, u32[]{:S(2)}) copy-start(f32[1,512]{1,0:T(1,128)S(1)} %convert_element_type.32) | copy-start | bytes 6148
  7.9 20.5 %copy-start.5 = (f32[33,512]{1,0:T(8,128)S(1)}, f32[33,512]{1,0:T(8,128)}, u32[]{:S(2)}) copy-start(f32[33,512]{1,0:T(8,128)} %refs_6_.1) | copy-start | bytes 202756
  8.0 20.4 %copy-start.3 = (bf16[512,1024]{1,0:T(8,128)(2,1)S(1)}, bf16[512,1024]{1,0:T(8,128)(2,1)}, u32[]{:S(2)}) copy-start(bf16[512,1024]{1,0:T(8,128)(2,1)} %queries.1) | copy-start | bytes 3145732
  9.6 12.0 %collective-permute-start = (f32[40,1024]{1,0:T(8,128)}, f32[40,1024]{1,0:T(8,128)S(1)}, u32[]{:S(2)}, u32[]{:S(2)}) collective-permute-start(f32[40,1024]{1,0:T(8,128)} %select_maximum_fusion.1), channel_id=1, source_target_pairs={{0,32},{32,64},{64,96},{96,128},{128,160},{160,192},{192,224},{224... | collective-permute-start | bytes 491528 | tf_op jit(solution)/shard_map/ppermute | solution.py:270
  14.1 10.1 %collective-permute-start.1 = (f32[40,1024]{1,0:T(8,128)}, f32[40,1024]{1,0:T(8,128)S(1)}, u32[]{:S(2)}, u32[]{:S(2)}) collective-permute-start(f32[40,1024]{1,0:T(8,128)} %select_maximum_fusion), channel_id=1, source_target_pairs={{32,0},{64,32},{96,64},{128,96},{160,128},{192,160},{224,192},{256... | collective-permute-start | bytes 491528 | tf_op jit(solution)/shard_map/ppermute | solution.py:271
  16.1 0.7 copy-start.14
  16.9 0.5 copy-start.6
  17.4 1.2 copy-start
  18.6 1.2 copy-start.2
  19.8 1.9 %copy-start.12 = (f32[1,512]{1,0:T(1,128)S(1)}, f32[1,512]{1,0:T(1,128)}, u32[]{:S(2)}) copy-start(f32[1,512]{1,0:T(1,128)} %copy-done.11) | copy-start | bytes 6148
  21.7 26.9 %copy-start.1 = (bf16[1,512,1024]{2,1,0:T(8,128)(2,1)S(1)}, bf16[1,512,1024]{2,1,0:T(8,128)(2,1)}, u32[]{:S(2)}) copy-start(bf16[1,512,1024]{2,1,0:T(8,128)(2,1)} %param.5) | copy-start | bytes 3145732
  21.8 0.5 copy-start.13
  28.4 0.6 copy-start.7
  54.6 9.8 %collective-permute-start.2 = (f32[256,256]{1,0:T(8,128)S(1)}, f32[256,256]{1,0:T(8,128)S(1)}, u32[]{:S(2)}, u32[]{:S(2)}) collective-permute-start(f32[256,256]{1,0:T(8,128)S(1)} %get-tuple-element.27), channel_id=1, source_target_pairs={{0,1},{1,2},{2,3},{3,0},{4,5},{5,6},{6,7},{7,4},{8,9},{9,10},{10,1... | collective-permute-start | bytes 786440 | tf_op jit(solution)/shard_map/ppermute | solution.py:321
  58.0 10.8 %collective-permute-start.3 = (f32[256,256]{1,0:T(8,128)S(1)}, f32[256,256]{1,0:T(8,128)S(1)}, u32[]{:S(2)}, u32[]{:S(2)}) collective-permute-start(f32[256,256]{1,0:T(8,128)S(1)} %get-tuple-element.28), channel_id=1, source_target_pairs={{1,0},{2,1},{3,2},{0,3},{5,4},{6,5},{7,6},{4,7},{9,8},{10,9},{11,1... | collective-permute-start | bytes 786440 | tf_op jit(solution)/shard_map/ppermute | solution.py:322
  60.5 8.3 %copy-start.8 = (s32[7]{0:T(128)S(1)}, s32[7]{0:T(128)}, u32[]{:S(2)}) copy-start(s32[7]{0:T(128)} %copy-done.6) | copy-start | bytes 88
  70.3 1.3 copy-start.4
  71.6 0.8 copy-start.9
  72.5 1.1 copy-start.10
  73.6 19.8 %collective-permute-start.4 = (f32[592,256]{1,0:T(8,128)S(1)}, f32[592,256]{1,0:T(8,128)S(1)}, u32[]{:S(2)}, u32[]{:S(2)}) collective-permute-start(f32[592,256]{1,0:T(8,128)S(1)} %copy-done.10), channel_id=1, source_target_pairs={{0,1},{1,2},{2,3},{3,0},{4,5},{5,6},{6,7},{7,4},{8,9},{9,10},{10,1... | collective-permute-start | bytes 1818632 | tf_op jit(solution)/shard_map/ppermute | solution.py:349
  75.5 19.0 %collective-permute-start.5 = (f32[592,256]{1,0:T(8,128)S(1)}, f32[592,256]{1,0:T(8,128)S(1)}, u32[]{:S(2)}, u32[]{:S(2)}) collective-permute-start(f32[592,256]{1,0:T(8,128)S(1)} %get-tuple-element.32), channel_id=1, source_target_pairs={{1,0},{2,1},{3,2},{0,3},{5,4},{6,5},{7,6},{4,7},{9,8},{10,9},{11,1... | collective-permute-start | bytes 1818632 | tf_op jit(solution)/shard_map/ppermute | solution.py:350
  79.4 13.9 %collective-permute-start.6 = (f32[80,256]{1,0:T(8,128)S(1)}, f32[80,256]{1,0:T(8,128)S(1)}, u32[]{:S(2)}, u32[]{:S(2)}) collective-permute-start(f32[80,256]{1,0:T(8,128)S(1)} %get-tuple-element.26.taps_in.taps_own), channel_id=1, source_target_pairs={{0,2},{1,3},{2,0},{3,1},{4,6},{5,7},{6,4},{7,5},{8,10},{9,11},{10,... | collective-permute-start | bytes 245768 | tf_op jit(solution)/shard_map/ppermute | solution.py:338
Sparse Core Ops, SparseCore 0:
  72.6 44.3 reduce-scatter.1

commit v4 on v3

--- a/solution.py
+++ b/solution.py
@@ -36,13 +36,61 @@
     return lax.dot_general(a, b, (((1,), (1,)), ((), ())), preferred_element_type=F32)
 
 
-def score_kernel(scale, scalars, frames, queries, out):
+def edge_kernel(half, last, first, labels, up, down):
+    rim = 2 * half
+    up[:rim, :] = last[...].astype(F32)
+    down[:rim, :] = first[...].astype(F32)
+    width = labels.shape[1]
+    tail = labels[:, width - LANES :].astype(F32)
+    up[rim:, :LANES] = jnp.broadcast_to(pltpu.roll(tail, half, 1), (UNIT, LANES))
+    down[rim:, :LANES] = jnp.broadcast_to(labels[:, :LANES].astype(F32), (UNIT, LANES))
+
+
+def score_kernel(scale, steps, scalars, frames, queries, out, place):
     rows = frames.shape[0]
     blk = rows // SUB
-    placed = jnp.dot(placement(rows, blk), frames[...], preferred_element_type=F32).astype(jnp.bfloat16)
-    m = lax.broadcasted_iota(jnp.int32, (rows, 1), 0)
-    frame = scalars[0] + (m & (SUB - 1)) * blk + m // SUB
-    out[...] = jnp.where(frame < scalars[1], dot_t(placed, queries[...]) * scale, 0.0)
+    step = pl.program_id(0)
+
+    @pl.when(step == 0)
+    def _():
+        place[...] = placement(rows, blk)
+
+    placed = jnp.dot(place[...], frames[...], preferred_element_type=F32).astype(jnp.bfloat16)
+    term = dot_t(placed, queries[...])
+
+    @pl.when(step == 0)
+    def _():
+        out[...] = term
+
+    @pl.when(step > 0)
+    def _():
+        out[...] += term
+
+    @pl.when(step == steps - 1)
+    def _():
+        m = lax.broadcasted_iota(jnp.int32, (rows, 1), 0)
+        frame = scalars[0] + (m & (SUB - 1)) * blk + m // SUB
+        out[...] = jnp.where(frame < scalars[1], out[...] * scale, 0.0)
+
+
+def label_tile(half, blk, labels, before, after):
+    rim = 2 * half
+    sub = lax.broadcasted_iota(jnp.int32, (SUB, LANES), 0)
+    lane = lax.broadcasted_iota(jnp.int32, (SUB, LANES), 1)
+    base = jnp.zeros((SUB, LANES), F32)
+    for s in range(SUB):
+        at = s * blk
+        row = labels[:, at // LANES * LANES : at // LANES * LANES + LANES].astype(F32)
+        row = jnp.broadcast_to(row, (SUB, LANES))
+        if at % LANES:
+            row = pltpu.roll(row, LANES - at % LANES, 1)
+        base = jnp.where(sub == s, row, base)
+    low = pltpu.roll(pltpu.roll(base, LANES - blk + half, 1), 1, 0)
+    low = jnp.where(sub == 0, before[rim:, :LANES], low)
+    high = pltpu.roll(pltpu.roll(base, half + blk, 1), SUB - 1, 0)
+    high = jnp.where(sub == SUB - 1, pltpu.roll(after[rim:, :LANES], half + blk, 1), high)
+    tile = jnp.where(lane < half, low, pltpu.roll(base, half, 1))
+    return jnp.where(lane >= half + blk, high, tile)
 
 
 def broadcast_taps(taps, wide, count):
@@ -61,12 +109,15 @@
     return sums
 
 
-def smooth_kernel(scale, half, scalars, main, before, after, queries, taps, scores, powers, stats, wide):
+def smooth_kernel(
+    scale, half, scalars, main, before, after, labels, queries, taps, scores, powers, stats, tile, wide
+):
     blk = main.shape[0]
     count = 2 * half + 1
     groups = queries.shape[0] // LANES
     rim = 2 * half
     broadcast_taps(taps, wide, count)
+    tile[...] = label_tile(half, blk, labels, before, after)
     rim_frames = jnp.concatenate([before[:rim, :], after[:rim, :]], axis=0).astype(jnp.bfloat16)
     k = lax.broadcasted_iota(jnp.int32, (2 * rim, 1), 0)
     frame = scalars[0] + jnp.where(k < rim, k - rim, blk * SUB + k - rim)
@@ -205,7 +256,9 @@
     own[...] = jnp.dot(turn_over(score_grad[...]), mine, preferred_element_type=F32)
 
 
-def near_kernel(scalars, score_grad, frames, queries, taps_in, from_behind, from_ahead, ahead, behind, frame_part):
+def near_kernel(
+    scalars, score_grad, frames, queries, taps_own, taps_far, from_behind, from_ahead, ahead, behind, frame_part
+):
     query_count = score_grad.shape[1]
     part_width = ahead.shape[1]
     middle = query_count // 2
@@ -213,11 +266,10 @@
     part = jnp.dot(turned, column_block(frames, scalars[4], part_width), preferred_element_type=F32)
     ahead[:middle, :] = part[:middle] + from_behind[...]
     ahead[middle:query_count, :] = part[middle:]
-    ahead[query_count:, :] = taps_in[...]
+    ahead[query_count:, :] = taps_own[...] + taps_far[...]
     part = jnp.dot(turned, column_block(frames, scalars[6], part_width), preferred_element_type=F32)
     behind[:middle, :] = part[:middle]
     behind[middle:query_count, :] = part[middle:] + from_ahead[...]
-    behind[query_count:, :] = taps_in[...]
     frame_part[...] = jnp.dot(score_grad[...], queries[...], preferred_element_type=F32)
 
 
@@ -232,9 +284,7 @@
         if z * tap_rows < taps_own.shape[0]:
             rows = slice(z * tap_rows, (z + 1) * tap_rows)
             late = slice(query_count + z * tap_rows, query_count + (z + 1) * tap_rows)
-            chunks[z, chunk_rows:, :] = (
-                taps_own[rows, :] + taps_far[rows, :] + from_behind[late, :] + from_ahead[late, :]
-            )
+            chunks[z, chunk_rows:, :] = taps_own[rows, :] + taps_far[rows, :] + from_behind[late, :]
         else:
             chunks[z, chunk_rows:, :] = jnp.zeros((tap_rows, own.shape[1]), F32)
 
@@ -245,7 +295,6 @@
 
 def per_device(frames, queries, kernel, labels, lengths):
     frame_rows = frames[0]
-    label_ids = labels[0].astype(F32)
     rows, width = frame_rows.shape
     query_count = queries.shape[0]
     count = kernel.shape[0]
@@ -261,40 +310,54 @@
     ).astype(jnp.int32)
     smem = pl.BlockSpec(memory_space=pltpu.SMEM)
 
-    def edge(part, ids):
-        extra = jnp.pad(ids[None, :], ((0, UNIT - 1), (0, width - rim)))
-        return jnp.concatenate([part.astype(F32), extra], axis=0)
-
+    edge = jax.ShapeDtypeStruct((rim + UNIT, width), F32)
+    last, first = pl.pallas_call(
+        lambda *refs: edge_kernel(half, *refs),
+        out_shape=[edge, edge],
+        grid=(1,),
+        in_specs=[
+            pl.BlockSpec((rim, width), lambda i: (rows // rim - 1, 0)),
+            pl.BlockSpec((rim, width), lambda i: (0, 0)),
+            pl.BlockSpec(labels.shape, lambda i: (0, 0)),
+        ],
+        out_specs=[pl.BlockSpec(edge.shape, lambda i: (0, 0))] * 2,
+        compiler_params=params(8),
+        cost_estimate=cost(rim * width, 1 << 19),
+    )(frame_rows, frame_rows, labels)
     up = [(i, i + 1) for i in range(tms - 1)]
     down = [(j, i) for i, j in up]
-    before = lax.ppermute(edge(frame_rows[rows - rim :], label_ids[rows - rim :]), "tm", up)
-    after = lax.ppermute(edge(frame_rows[:rim], label_ids[:rim]), "tm", down)
+    before = lax.ppermute(last, "tm", up)
+    after = lax.ppermute(first, "tm", down)
+    steps = 4
     main = pl.pallas_call(
-        lambda *refs: score_kernel(scale, *refs),
+        lambda *refs: score_kernel(scale, steps, *refs),
         out_shape=jax.ShapeDtypeStruct((rows, query_count), F32),
-        in_specs=[smem] + whole_spec(2),
-        out_specs=pl.BlockSpec(memory_space=VMEM),
-        compiler_params=params(12),
+        grid=(steps,),
+        in_specs=[
+            smem,
+            pl.BlockSpec((rows, width // steps), lambda k: (0, k)),
+            pl.BlockSpec((query_count, width // steps), lambda k: (0, k)),
+        ],
+        out_specs=pl.BlockSpec((rows, query_count), lambda k: (0, 0)),
+        scratch_shapes=[VMEM((rows, rows), jnp.bfloat16)],
+        compiler_params=params(16),
         cost_estimate=cost(2 * rows * width * (rows + query_count), 3 << 20),
     )(scalars, frame_rows, queries)
     main = main.reshape(blk, SUB, query_count)
-    scores, powers, stats = pl.pallas_call(
+    scores, powers, stats, tile = pl.pallas_call(
         lambda *refs: smooth_kernel(scale, half, *refs),
         out_shape=[
             jax.ShapeDtypeStruct((blk + 2 * rim, SUB, query_count), F32),
             jax.ShapeDtypeStruct((blk + rim, SUB, query_count), F32),
             jax.ShapeDtypeStruct((2, SUB, LANES), F32),
-        ],
-        in_specs=[smem] + whole_spec(5),
-        out_specs=whole_spec(3),
+            jax.ShapeDtypeStruct((SUB, LANES), F32),
+        ],
+        in_specs=[smem] + whole_spec(6),
+        out_specs=whole_spec(4),
         scratch_shapes=[VMEM((count, SUB, query_count), F32)],
         compiler_params=params(12),
         cost_estimate=cost(4 * rows * query_count * count, 6 << 20),
-    )(scalars, main, before, after, queries, kernel)
-    ext = jnp.concatenate([before[rim, half:rim], label_ids, after[rim, :half], jnp.zeros((blk - rim,), F32)])
-    ext = ext.reshape(SUB + 1, blk)
-    tile = jnp.concatenate([ext[:SUB], ext[1:, :rim], jnp.zeros((SUB, LANES - blk - rim), F32)], axis=1)
-    stats, tile = lax.optimization_barrier((stats, tile))
+    )(scalars, main, before, after, labels, queries, kernel)
     others = lax.all_to_all(jnp.broadcast_to(stats[None], (blocks,) + stats.shape), "query", 0, 0)
     chunk_rows = query_count // tms
     part_width = width // recs
@@ -336,18 +399,22 @@
     )(scalars, grads, scores, score_grad, frame_rows)
     across = [(i, (i + 2) % recs) for i in range(recs)]
     taps_far = lax.ppermute(taps_own, "rec", across)
-    near = jax.ShapeDtypeStruct((query_count + tap_rows, part_width), F32)
     near_a, near_b, frame_part = pl.pallas_call(
         near_kernel,
-        out_shape=[near, near, jax.ShapeDtypeStruct((rows, width), F32)],
-        in_specs=[smem] + whole_spec(6),
+        out_shape=[
+            jax.ShapeDtypeStruct((query_count + tap_rows, part_width), F32),
+            jax.ShapeDtypeStruct((query_count, part_width), F32),
+            jax.ShapeDtypeStruct((rows, width), F32),
+        ],
+        in_specs=[smem] + whole_spec(7),
         out_specs=whole_spec(3),
         compiler_params=params(12),
         cost_estimate=cost(rows * query_count * width, 4 << 20),
-    )(scalars, score_grad, frame_rows, queries, taps_own, far_a, far_b)
-    frame_sum = lax.psum_scatter(frame_part, "query", scatter_dimension=1, tiled=True)
+    )(scalars, score_grad, frame_rows, queries, taps_own, taps_far, far_a, far_b)
     near_a = lax.ppermute(near_a, "rec", onward)
     near_b = lax.ppermute(near_b, "rec", back)
+    near_a, near_b, frame_part = lax.optimization_barrier((near_a, near_b, frame_part))
+    frame_sum = lax.psum_scatter(frame_part, "query", scatter_dimension=1, tiled=True)
     chunks = pl.pallas_call(
         sum_kernel,
         out_shape=jax.ShapeDtypeStruct((tms, chunk_rows + UNIT, part_width), F32),

time: 188 us -> 177 us (0.941)
  local copies, waits for them, and re-layouts: 12.1 us -> 3.36 us
  other arithmetic: 8.27 us -> 3.06 us
  Pallas kernels: 22.6 us -> 25.2 us
    ppermute x1, waiting for transfers between devices: 1.13 us -> 12.7 us  [per_device(): near_b = lax.ppermute(near_b, 'rec', back)]
    ppermute x1, waiting for transfers between devices: 11.7 us -> 4.52 us  [per_device(): taps_far = lax.ppermute(taps_own, 'rec', across)]
    ppermute x1, waiting for transfers between devices: 4.27 us -> 0.01 us  [per_device(): far_b = lax.ppermute(far_b, 'rec', back)]
    unnamed x30 -> x14, local copies, waits for them, and re-layouts: 7.23 us -> 3.25 us
    concatenate x5 -> x0, other arithmetic: 3.55 us -> none  [the longest x2 1.43 us: per_device(): jnp.concatenate([before[rim, half:rim], label_ids, after[rim, :half], jnp...]
    slice x4 -> x0, local copies, waits for them, and re-layouts: 2.7 us -> none  [the longest x2 1.93 us: per_device(): ext[:SUB]]
    pallas_call x2 -> x3, Pallas kernels: 3.4 us -> 5.99 us  [the longest x1 4.31 us: per_device(): pl.pallas_call(lambda *refs: score_kernel(scale, steps, *refs), out_shape...]
    ppermute x1, starting transfers between devices: 1.91 us -> 4.01 us  [per_device(): near_a = lax.ppermute(near_a, 'rec', onward)]
  transfers between devices with their start and end apart: 8 -> 8, of which waited for: 4 -> 3; matrix products, arithmetic and copies ran while one was open for 2% -> 0% of each run, Pallas kernels for 3% -> 4%
where the time goes in v4:
time: 177 us; the launch traced here: 176 us
  blocking collectives  91 us (51%)
  Pallas kernels  25.2 us (14%)
  starting transfers between devices  20.4 us (12%)
  waiting for transfers between devices  18.6 us (11%)
  between operations  14.8 us (8%)
  local copies, waits for them, and re-layouts  3.36 us (2%)
  other arithmetic  3.06 us (2%)
    all_to_all x1, blocking collectives, per_device(): chunk = jnp.sum(lax.all_to_all(chunks, 'tm', 0, 0), axis=0)  49.1 us
    all_gather x1, blocking collectives, per_device(): whole = lax.all_gather(chunk, 'tm')  32 us
    ppermute x1, waiting for transfers between devices, per_device(): near_b = lax.ppermute(near_b, 'rec', back)  12.7 us
    all_to_all x1, blocking collectives, per_device(): lax.all_to_all(jnp.broadcast_to(stats[None], (blocks,) + stats.shape), 'q...  9.92 us
    pallas_call x1, Pallas kernels, per_device(): pl.pallas_call(lambda *refs: smooth_kernel(scale, half, *refs), out_shape...  9.65 us
    pallas_call x1, Pallas kernels, per_device(): pl.pallas_call(lambda *refs: grad_kernel(half, *refs), out_shape=[jax.Sha...  6.06 us
    ppermute x1, waiting for transfers between devices, per_device(): taps_far = lax.ppermute(taps_own, 'rec', across)  4.52 us
    pallas_call x1, Pallas kernels, per_device(): pl.pallas_call(lambda *refs: score_kernel(scale, steps, *refs), out_shape...  4.31 us
  transfers between devices with their start and end apart: 8, of which 3 were waited for; matrix products, arithmetic and copies ran while one was open for 0% of the time, Pallas kernels for 4%

profile of v4, /device:TPU:6, one launch (start us, length us, event | category | flops | bytes accessed | tf_op | source)
XLA Modules:
  0.0 176.5 jit_solution(12383405253582628591)
XLA Ops:
  7.2 0.0 reduce-scatter.2.cloned.1.call-start
  7.2 0.0 copy-start
  7.2 1.2 copy-done
  8.4 0.0 copy-start.5
  8.4 0.7 copy-done.5
  9.1 0.0 copy-start.1
  9.1 0.0 copy-start.2
  9.1 0.1 shard_map.77
  9.2 0.0 copy-start.4
  9.2 0.0 copy-start.6
  9.2 4.0 %collective-permute-start = (f32[40,1024]{1,0:T(8,128)S(1)}, f32[40,1024]{1,0:T(8,128)S(1)}, u32[]{:S(2)}, u32[]{:S(2)}) collective-permute-start(f32[40,1024]{1,0:T(8,128)S(1)} %get-tuple-element.23), channel_id=1, source_target_pairs={{0,32},{32,64},{64,96},{96,128},{128,160},{160,192},{192,224},{224... | collective-permute-start | bytes 491528 | tf_op jit(solution)/shard_map/ppermute | solution.py:329
  13.2 1.3 collective-permute-start.1
  15.2 0.1 stack.27.refs_0_.scalars
  15.2 0.0 copy-done.1
  15.2 0.0 copy-done.2
  15.2 4.3 %shard_map.76 = f32[512,512]{1,0:T(8,128)S(1)} custom-call(s32[7]{0:T(128)S(1)} %stack.27.refs_0_.scalars, bf16[512,1024]{1,0:T(8,128)(2,1)S(1)} %bitcast.19, bf16[512,1024]{1,0:T(8,128)(2,1)S(1)} %copy-done.2), custom_call_target="tpu_custom_call" | custom-call | flops 1073741824 | bytes 3145728 | tf_op jit(solution)/shard_map/pallas_call | solution.py:332
  19.6 0.0 collective-permute-done.refs_2_
  19.6 1.3 collective-permute-done.1.refs_3_
  20.9 0.0 copy-done.4
  20.9 0.0 copy-done.6
  20.9 9.7 %shard_map.78 = (f32[128,8,512]{2,1,0:T(8,128)S(1)}, f32[96,8,512]{2,1,0:T(8,128)S(1)}, f32[2,8,128]{2,1,0:T(8,128)S(1)}, f32[8,128]{1,0:T(8,128)S(1)}) custom-call(s32[7]{0:T(128)S(1)} %stack.27.refs_0_.scalars, f32[64,8,512]{2,1,0:T(8,128)S(1)} %bitcast.23, f32[40,1024]{1,0:T(8,128)S(1)} %collective-permute-done.refs_2_, ...), custom_call_target="tpu_custom_call" | custom-call | flops 34603008 | bytes 6291456 | tf_op jit(solution)/shard_map/pallas_call | solution.py:347
  30.6 9.9 %all_to_all.10.refs_3_ = f32[8,2,8,128]{3,2,1,0:T(8,128)S(1)} all-to-all(f32[8,2,8,128]{3,2,1,0:T(8,128)S(1)} %broadcast_in_dim.4), channel_id=1, replica_groups=mesh['tm'=16,'query'=8,'rec'=4] {'query'}, dimensions={0} | all-to-all | bytes 131072 | tf_op jit(solution)/shard_map/all_to_all | solution.py:361
  40.5 6.1 %shard_map.79 = (f32[96,8,512]{2,1,0:T(8,128)S(1)}, bf16[512,512]{1,0:T(8,128)(2,1)S(1)}, f32[256,256]{1,0:T(8,128)S(1)}, f32[256,256]{1,0:T(8,128)S(1)}) custom-call(s32[7]{0:T(128)S(1)} %stack.27.refs_0_.scalars, f32[96,8,512]{2,1,0:T(8,128)S(1)} %get-tuple-element.25.refs_1_, f32[2,8,128]{2,1,0:T(8,128)S(1)} %get-tuple-element.26.refs_2_, ...), custom_call_target="tpu_custom_call" | custom-call | flops 571473920 | bytes 8388608 | tf_op jit(solution)/shard_map/pallas_call | solution.py:365
  46.5 2.8 %collective-permute-start.3 = (f32[256,256]{1,0:T(8,128)S(1)}, f32[256,256]{1,0:T(8,128)S(1)}, u32[]{:S(2)}, u32[]{:S(2)}) collective-permute-start(f32[256,256]{1,0:T(8,128)S(1)} %get-tuple-element.32), channel_id=1, source_target_pairs={{0,1},{1,2},{2,3},{3,0},{4,5},{5,6},{6,7},{7,4},{8,9},{9,10},{10,1... | collective-permute-start | bytes 786440 | tf_op jit(solution)/shard_map/ppermute | solution.py:384
  49.4 3.0 %collective-permute-start.4 = (f32[256,256]{1,0:T(8,128)S(1)}, f32[256,256]{1,0:T(8,128)S(1)}, u32[]{:S(2)}, u32[]{:S(2)}) collective-permute-start(f32[256,256]{1,0:T(8,128)S(1)} %get-tuple-element.33), channel_id=1, source_target_pairs={{1,0},{2,1},{3,2},{0,3},{5,4},{6,5},{7,6},{4,7},{9,8},{10,9},{11,1... | collective-permute-start | bytes 786440 | tf_op jit(solution)/shard_map/ppermute | solution.py:385
  52.4 3.4 %shard_map.80 = (f32[512,256]{1,0:T(8,128)S(1)}, f32[80,256]{1,0:T(8,128)S(1)}) custom-call(s32[7]{0:T(128)S(1)} %stack.27.refs_0_.scalars, f32[96,8,512]{2,1,0:T(8,128)S(1)} %get-tuple-element.29.refs_1_, f32[128,8,512]{2,1,0:T(8,128)S(1)} %get-tuple-element.30.refs_2_, bf16[512,512]{1,0:T(8,128)(2,1)S(1)} %get-tuple-element.28.refs_3_.score_grad, ...), custom_call_target="tpu_custom_call" | custom-call | flops 1142947840 | bytes 16777216 | tf_op jit(solution)/shard_map/pallas_call | solution.py:388
  55.8 3.3 %collective-permute-start.2 = (f32[80,256]{1,0:T(8,128)S(1)}, f32[80,256]{1,0:T(8,128)S(1)}, u32[]{:S(2)}, u32[]{:S(2)}) collective-permute-start(f32[80,256]{1,0:T(8,128)S(1)} %get-tuple-element.31.taps_own), channel_id=1, source_target_pairs={{0,2},{1,3},{2,0},{3,1},{4,6},{5,7},{6,4},{7,5},{8,10},{9,11},{10,... | collective-permute-start | bytes 245768 | tf_op jit(solution)/shard_map/ppermute | solution.py:401
  59.1 4.5 %collective-permute-done.2.taps_far = f32[80,256]{1,0:T(8,128)S(1)} collective-permute-done((f32[80,256]{1,0:T(8,128)S(1)}, f32[80,256]{1,0:T(8,128)S(1)}, u32[]{:S(2)}, u32[]{:S(2)}) %collective-permute-start.2) | collective-permute-done | bytes 81952 | tf_op jit(solution)/shard_map/ppermute | solution.py:401
  63.6 0.0 collective-permute-done.3.from_behind
  63.6 0.0 collective-permute-done.4.from_ahead
  63.6 1.6 shard_map.81
  65.2 0.0 copy-start.3
  65.3 1.3 copy-done.3
  66.6 4.0 %collective-permute-start.5 = (f32[592,256]{1,0:T(8,128)S(1)}, f32[592,256]{1,0:T(8,128)S(1)}, u32[]{:S(2)}, u32[]{:S(2)}) collective-permute-start(f32[592,256]{1,0:T(8,128)S(1)} %get-tuple-element.34), channel_id=1, source_target_pairs={{0,1},{1,2},{2,3},{3,0},{4,5},{5,6},{6,7},{7,4},{8,9},{9,10},{10,1... | collective-permute-start | bytes 1818632 | tf_op jit(solution)/shard_map/ppermute | solution.py:414
  70.6 1.9 %collective-permute-start.6 = (f32[512,256]{1,0:T(8,128)S(1)}, f32[512,256]{1,0:T(8,128)S(1)}, u32[]{:S(2)}, u32[]{:S(2)}) collective-permute-start(f32[512,256]{1,0:T(8,128)S(1)} %get-tuple-element.35), channel_id=1, source_target_pairs={{1,0},{2,1},{3,2},{0,3},{5,4},{6,5},{7,6},{4,7},{9,8},{10,9},{11,1... | collective-permute-start | bytes 1572872 | tf_op jit(solution)/shard_map/ppermute | solution.py:415
  72.5 12.7 %collective-permute-done.6.from_ahead = f32[512,256]{1,0:T(8,128)S(1)} collective-permute-done((f32[512,256]{1,0:T(8,128)S(1)}, f32[512,256]{1,0:T(8,128)S(1)}, u32[]{:S(2)}, u32[]{:S(2)}) %collective-permute-start.6) | collective-permute-done | bytes 524320 | tf_op jit(solution)/shard_map/ppermute | solution.py:415
  85.3 0.0 collective-permute-done.5.from_behind
  85.3 0.0 reduce-scatter.2.cloned.1.call-update
  85.3 0.1 shard_map.82
  85.4 49.1 %all_to_all.11 = f32[16,40,256]{2,1,0:T(8,128)S(1)} all-to-all(f32[16,40,256]{2,1,0:T(8,128)S(1)} %shard_map.82), channel_id=1, replica_groups=mesh['tm'=16,'query'=8,'rec'=4] {'tm'}, dimensions={0} | all-to-all | bytes 1310720 | tf_op jit(solution)/shard_map/all_to_all | solution.py:426
  134.5 0.0 reduce-scatter.2.cloned.1.call-done
  134.5 32.0 %all-gather = f32[640,256]{1,0:T(8,128)S(1)} all-gather(f32[40,256]{1,0:T(8,128)S(1)} %reduce_sum.9), channel_id=2, replica_groups=mesh['tm'=16,'query'=8,'rec'=4] {'tm'}, dimensions={0}, use_global_device_ids=true | all-gather | bytes 696320 | tf_op jit(solution)/shard_map/all_gather | solution.py:428
  166.6 0.8 fusion
  167.3 1.6 fusion.1
  169.0 0.6 pad_maximum_fusion
  (4 shorter events, 0.1 us)
Async XLA Ops:
  7.2 127.4 %reduce-scatter.2.cloned.1.call-start = ((), (), s32[]{:S(2)}) async-start(), calls=%async_computation.3 | async-start | bytes 2359296 | tf_op jit(solution)/shard_map/reduce_scatter | solution.py:417
  7.2 1.2 copy-start
  8.4 0.7 copy-start.5
  9.1 6.1 %copy-start.1 = (bf16[1,512,1024]{2,1,0:T(8,128)(2,1)S(1)}, bf16[1,512,1024]{2,1,0:T(8,128)(2,1)}, u32[]{:S(2)}) copy-start(bf16[1,512,1024]{2,1,0:T(8,128)(2,1)} %param.5) | copy-start | bytes 3145732
  9.1 6.1 %copy-start.2 = (bf16[512,1024]{1,0:T(8,128)(2,1)S(1)}, bf16[512,1024]{1,0:T(8,128)(2,1)}, u32[]{:S(2)}) copy-start(bf16[512,1024]{1,0:T(8,128)(2,1)} %queries.1) | copy-start | bytes 3145732
  9.2 11.7 %copy-start.4 = (f32[33,512]{1,0:T(8,128)S(1)}, f32[33,512]{1,0:T(8,128)}, u32[]{:S(2)}) copy-start(f32[33,512]{1,0:T(8,128)} %refs_6_.3) | copy-start | bytes 202756
  9.2 11.7 %copy-start.6 = (s32[1,512]{1,0:T(1,128)S(1)}, s32[1,512]{1,0:T(1,128)}, u32[]{:S(2)}) copy-start(s32[1,512]{1,0:T(1,128)} %refs_4_.1) | copy-start | bytes 6148
  9.2 10.4 %collective-permute-start = (f32[40,1024]{1,0:T(8,128)S(1)}, f32[40,1024]{1,0:T(8,128)S(1)}, u32[]{:S(2)}, u32[]{:S(2)}) collective-permute-start(f32[40,1024]{1,0:T(8,128)S(1)} %get-tuple-element.23), channel_id=1, source_target_pairs={{0,32},{32,64},{64,96},{96,128},{128,160},{160,192},{192,224},{224... | collective-permute-start | bytes 491528 | tf_op jit(solution)/shard_map/ppermute | solution.py:329
  13.2 7.7 %collective-permute-start.1 = (f32[40,1024]{1,0:T(8,128)S(1)}, f32[40,1024]{1,0:T(8,128)S(1)}, u32[]{:S(2)}, u32[]{:S(2)}) collective-permute-start(f32[40,1024]{1,0:T(8,128)S(1)} %get-tuple-element.24), channel_id=1, source_target_pairs={{32,0},{64,32},{96,64},{128,96},{160,128},{192,160},{224,192},{256... | collective-permute-start | bytes 491528 | tf_op jit(solution)/shard_map/ppermute | solution.py:330
  46.5 17.1 %collective-permute-start.3 = (f32[256,256]{1,0:T(8,128)S(1)}, f32[256,256]{1,0:T(8,128)S(1)}, u32[]{:S(2)}, u32[]{:S(2)}) collective-permute-start(f32[256,256]{1,0:T(8,128)S(1)} %get-tuple-element.32), channel_id=1, source_target_pairs={{0,1},{1,2},{2,3},{3,0},{4,5},{5,6},{6,7},{7,4},{8,9},{9,10},{10,1... | collective-permute-start | bytes 786440 | tf_op jit(solution)/shard_map/ppermute | solution.py:384
  49.4 14.3 %collective-permute-start.4 = (f32[256,256]{1,0:T(8,128)S(1)}, f32[256,256]{1,0:T(8,128)S(1)}, u32[]{:S(2)}, u32[]{:S(2)}) collective-permute-start(f32[256,256]{1,0:T(8,128)S(1)} %get-tuple-element.33), channel_id=1, source_target_pairs={{1,0},{2,1},{3,2},{0,3},{5,4},{6,5},{7,6},{4,7},{9,8},{10,9},{11,1... | collective-permute-start | bytes 786440 | tf_op jit(solution)/shard_map/ppermute | solution.py:385
  55.8 7.8 %collective-permute-start.2 = (f32[80,256]{1,0:T(8,128)S(1)}, f32[80,256]{1,0:T(8,128)S(1)}, u32[]{:S(2)}, u32[]{:S(2)}) collective-permute-start(f32[80,256]{1,0:T(8,128)S(1)} %get-tuple-element.31.taps_own), channel_id=1, source_target_pairs={{0,2},{1,3},{2,0},{3,1},{4,6},{5,7},{6,4},{7,5},{8,10},{9,11},{10,... | collective-permute-start | bytes 245768 | tf_op jit(solution)/shard_map/ppermute | solution.py:401
  65.2 1.3 copy-start.3
  66.6 18.7 %collective-permute-start.5 = (f32[592,256]{1,0:T(8,128)S(1)}, f32[592,256]{1,0:T(8,128)S(1)}, u32[]{:S(2)}, u32[]{:S(2)}) collective-permute-start(f32[592,256]{1,0:T(8,128)S(1)} %get-tuple-element.34), channel_id=1, source_target_pairs={{0,1},{1,2},{2,3},{3,0},{4,5},{5,6},{6,7},{7,4},{8,9},{9,10},{10,1... | collective-permute-start | bytes 1818632 | tf_op jit(solution)/shard_map/ppermute | solution.py:414
  70.6 14.7 %collective-permute-start.6 = (f32[512,256]{1,0:T(8,128)S(1)}, f32[512,256]{1,0:T(8,128)S(1)}, u32[]{:S(2)}, u32[]{:S(2)}) collective-permute-start(f32[512,256]{1,0:T(8,128)S(1)} %get-tuple-element.35), channel_id=1, source_target_pairs={{1,0},{2,1},{3,2},{0,3},{5,4},{6,5},{7,6},{4,7},{9,8},{10,9},{11,1... | collective-permute-start | bytes 1572872 | tf_op jit(solution)/shard_map/ppermute | solution.py:415
Sparse Core Ops, SparseCore 0:
  85.4 44.1 reduce-scatter.1

commit v5 on v4

--- a/solution.py
+++ b/solution.py
@@ -164,7 +164,8 @@
 
 
 def grad_kernel(
-    half, scalars, powers, mine, others, labels, frames, taps, grads, score_grad, ahead, behind, wide, placed,
+    half, scalars, powers, scores, mine, others, labels, frames, queries, taps,
+    score_grad, ahead, behind, keep_frames, cross_frames, wide, grads, tap_grads, placed, frame_part,
 ):
     blk = powers.shape[0] - 2 * half
     rows = blk * SUB
@@ -208,28 +209,6 @@
         return 0
 
     lax.fori_loop(0, blk // UNIT, spread, 0)
-    natural = jnp.dot(placement(rows, blk, True), placed[...], preferred_element_type=F32)
-    natural = natural.astype(jnp.bfloat16)
-    score_grad[...] = natural
-    far = column_block(frames, scalars[5], ahead.shape[1])
-    part = jnp.dot(turn_over(natural), far, preferred_element_type=F32)
-    ahead[...] = part[: query_count // 2]
-    behind[...] = part[query_count // 2 :]
-
-
-def column_block(frames, index, width):
-    return frames[:, pl.ds(pl.multiple_of(index * width, LANES), width)]
-
-
-def turn_over(score_grad):
-    return score_grad.astype(F32).T.astype(jnp.bfloat16)
-
-
-def own_kernel(half, scalars, grads, scores, score_grad, frames, own, taps_out, tap_grads):
-    blk = grads.shape[0] - 2 * half
-    count = 2 * half + 1
-    query_count = score_grad.shape[1]
-    groups = query_count // LANES
     tap_grads[...] = jnp.zeros_like(tap_grads)
 
     def correlate(b, _):
@@ -249,42 +228,68 @@
     parts = jnp.sum(tap_grads[...], axis=1)
     tall = padded_rows_of(count)
     parts = jnp.concatenate([parts, jnp.zeros((tall - count, query_count), F32)], axis=0)
-    part_width = own.shape[1]
-    for h in range(query_count // part_width):
-        taps_out[h * tall : (h + 1) * tall, :] = parts[:, h * part_width : (h + 1) * part_width]
-    mine = column_block(frames, scalars[3], part_width)
-    own[...] = jnp.dot(turn_over(score_grad[...]), mine, preferred_element_type=F32)
-
-
-def near_kernel(
-    scalars, score_grad, frames, queries, taps_own, taps_far, from_behind, from_ahead, ahead, behind, frame_part
-):
-    query_count = score_grad.shape[1]
+    natural = jnp.dot(placement(rows, blk, True), placed[...], preferred_element_type=F32)
+    natural = natural.astype(jnp.bfloat16)
+    score_grad[...] = natural
     part_width = ahead.shape[1]
     middle = query_count // 2
+    far = column_block(frames, scalars[5], part_width)
+    part = jnp.dot(turn_over(natural), far, preferred_element_type=F32)
+    ahead[:middle, :] = part[:middle]
+    behind[:middle, :] = part[middle:]
+    for h in range(query_count // part_width):
+        block = parts[:, h * part_width : (h + 1) * part_width]
+        ahead[middle + h * tall : middle + (h + 1) * tall, :] = block
+        behind[middle + h * tall : middle + (h + 1) * tall, :] = block
+    frame_part[...] = jnp.dot(natural, queries[...], preferred_element_type=F32)
+    chips, _, out_width = keep_frames.shape
+    for k in range(chips):
+        keep_frames[k] = column_block(frame_part, scalars[7 + k], out_width)
+        cross_frames[k] = column_block(frame_part, scalars[7 + chips + k], out_width)
+
+
+def column_block(frames, index, width):
+    return frames[:, pl.ds(pl.multiple_of(index * width, LANES), width)]
+
+
+def turn_over(score_grad):
+    return score_grad.astype(F32).T.astype(jnp.bfloat16)
+
+
+def near_kernel(scalars, score_grad, frames, own, ahead, behind):
     turned = turn_over(score_grad[...])
-    part = jnp.dot(turned, column_block(frames, scalars[4], part_width), preferred_element_type=F32)
-    ahead[:middle, :] = part[:middle] + from_behind[...]
-    ahead[middle:query_count, :] = part[middle:]
-    ahead[query_count:, :] = taps_own[...] + taps_far[...]
-    part = jnp.dot(turned, column_block(frames, scalars[6], part_width), preferred_element_type=F32)
-    behind[:middle, :] = part[:middle]
-    behind[middle:query_count, :] = part[middle:] + from_ahead[...]
-    frame_part[...] = jnp.dot(score_grad[...], queries[...], preferred_element_type=F32)
-
-
-def sum_kernel(own, taps_own, from_behind, from_ahead, taps_far, chunks):
+    for index, out in ((3, own), (4, ahead), (6, behind)):
+        block = column_block(frames, scalars[index], out.shape[1])
+        out[...] = jnp.dot(turned, block, preferred_element_type=F32)
+
+
+def join_kernel(ahead_in, behind_in, from_behind, from_ahead, keep, crossed, ahead, behind, *frame_out):
+    query_count = ahead_in.shape[0]
+    middle = query_count // 2
+    ahead[:middle, :] = ahead_in[:middle, :] + from_behind[:middle, :]
+    ahead[middle:query_count, :] = ahead_in[middle:, :]
+    ahead[query_count:, :] = from_behind[middle:, :]
+    behind[:middle, :] = behind_in[:middle, :]
+    behind[middle:, :] = behind_in[middle:, :] + from_ahead[:middle, :]
+    for k, out in enumerate(frame_out):
+        out[...] = keep[k] + crossed[k]
+
+
+def sum_kernel(own, taps, taps_behind, taps_ahead, from_behind, from_ahead, chunks):
     tms, padded_rows, _ = chunks.shape
     query_count = own.shape[0]
+    middle = query_count // 2
     chunk_rows = query_count // tms
     tap_rows = padded_rows - chunk_rows
     for z in range(tms):
         rows = slice(z * chunk_rows, (z + 1) * chunk_rows)
         chunks[z, :chunk_rows, :] = own[rows, :] + from_behind[rows, :] + from_ahead[rows, :]
-        if z * tap_rows < taps_own.shape[0]:
-            rows = slice(z * tap_rows, (z + 1) * tap_rows)
+        if z * tap_rows < from_behind.shape[0] - query_count:
+            rows = slice(middle + z * tap_rows, middle + (z + 1) * tap_rows)
             late = slice(query_count + z * tap_rows, query_count + (z + 1) * tap_rows)
-            chunks[z, chunk_rows:, :] = taps_own[rows, :] + taps_far[rows, :] + from_behind[late, :]
+            chunks[z, chunk_rows:, :] = (
+                taps[rows, :] + taps_behind[rows, :] + taps_ahead[rows, :] + from_behind[late, :]
+            )
         else:
             chunks[z, chunk_rows:, :] = jnp.zeros((tap_rows, own.shape[1]), F32)
 
@@ -305,8 +310,13 @@
     recs, tms, blocks = lax.axis_size("rec"), lax.axis_size("tm"), lax.axis_size("query")
     rec = lax.axis_index("rec")
     ring = [(rec + step) % recs for step in range(4)]
+    query_index = lax.axis_index("query")
+    chips = blocks // 2
+    chip, core = query_index // 2, query_index % 2
+    keep_ids = [(chip + k) % chips * 2 + core for k in range(chips)]
+    cross_ids = [(chip + k) % chips * 2 + 1 - core for k in range(chips)]
     scalars = jnp.stack(
-        [lax.axis_index("tm") * rows, lengths[0], lax.axis_index("query") * query_count] + ring
+        [lax.axis_index("tm") * rows, lengths[0], query_index * query_count] + ring + keep_ids + cross_ids
     ).astype(jnp.int32)
     smem = pl.BlockSpec(memory_space=pltpu.SMEM)
 
@@ -362,70 +372,69 @@
     chunk_rows = query_count // tms
     part_width = width // recs
     middle = query_count // 2
-    grads, score_grad, far_a, far_b = pl.pallas_call(
+    halves = query_count // part_width
+    tap_rows = halves * padded_rows_of(count)
+    out_width = width // blocks
+    step = jax.ShapeDtypeStruct((middle + tap_rows, part_width), F32)
+    terms = jax.ShapeDtypeStruct((chips, rows, out_width), F32)
+    score_grad, far_a, far_b, keep, cross = pl.pallas_call(
         lambda *refs: grad_kernel(half, *refs),
-        out_shape=[
-            jax.ShapeDtypeStruct((blk + rim, SUB, query_count), F32),
-            jax.ShapeDtypeStruct((rows, query_count), jnp.bfloat16),
-            jax.ShapeDtypeStruct((middle, part_width), F32),
-            jax.ShapeDtypeStruct((query_count - middle, part_width), F32),
-        ],
-        in_specs=[smem] + whole_spec(6),
-        out_specs=whole_spec(4),
+        out_shape=[jax.ShapeDtypeStruct((rows, query_count), jnp.bfloat16), step, step, terms, terms],
+        in_specs=[smem] + whole_spec(8),
+        out_specs=whole_spec(5),
         scratch_shapes=[
             VMEM((count, SUB, query_count), F32),
+            VMEM((blk + rim, SUB, query_count), F32),
+            VMEM((count, SUB, query_count), F32),
             VMEM((rows, query_count), jnp.bfloat16),
+            VMEM((rows, width), F32),
         ],
-        compiler_params=params(16),
+        compiler_params=params(20),
         cost_estimate=cost(2 * rows * query_count * (width + 2 * count), 8 << 20),
-    )(scalars, powers, stats, others, tile, frame_rows, kernel)
+    )(scalars, powers, scores, stats, others, tile, frame_rows, queries, kernel)
     onward = [(i, (i + 1) % recs) for i in range(recs)]
     back = [(j, i) for i, j in onward]
-    far_a = lax.ppermute(far_a, "rec", onward)
-    far_b = lax.ppermute(far_b, "rec", back)
-    halves = query_count // part_width
-    tap_rows = halves * padded_rows_of(count)
-    own, taps_own = pl.pallas_call(
-        lambda *refs: own_kernel(half, *refs),
-        out_shape=[
-            jax.ShapeDtypeStruct((query_count, part_width), F32),
-            jax.ShapeDtypeStruct((tap_rows, part_width), F32),
-        ],
-        in_specs=[smem] + whole_spec(4),
-        out_specs=whole_spec(2),
-        scratch_shapes=[VMEM((count, SUB, query_count), F32)],
-        compiler_params=params(16),
-        cost_estimate=cost(4 * rows * query_count * (width + 2 * count), 16 << 20),
-    )(scalars, grads, scores, score_grad, frame_rows)
-    across = [(i, (i + 2) % recs) for i in range(recs)]
-    taps_far = lax.ppermute(taps_own, "rec", across)
-    near_a, near_b, frame_part = pl.pallas_call(
+    taps_behind = lax.ppermute(far_a, "rec", onward)
+    taps_ahead = lax.ppermute(far_b, "rec", back)
+    crossed = lax.ppermute(cross, "query", [(i, i ^ 1) for i in range(blocks)])
+    near = jax.ShapeDtypeStruct((query_count, part_width), F32)
+    own, near_a, near_b = pl.pallas_call(
         near_kernel,
-        out_shape=[
-            jax.ShapeDtypeStruct((query_count + tap_rows, part_width), F32),
-            jax.ShapeDtypeStruct((query_count, part_width), F32),
-            jax.ShapeDtypeStruct((rows, width), F32),
-        ],
-        in_specs=[smem] + whole_spec(7),
+        out_shape=[near, near, near],
+        in_specs=[smem] + whole_spec(2),
         out_specs=whole_spec(3),
         compiler_params=params(12),
-        cost_estimate=cost(rows * query_count * width, 4 << 20),
-    )(scalars, score_grad, frame_rows, queries, taps_own, taps_far, far_a, far_b)
+        cost_estimate=cost(2 * rows * query_count * width, 4 << 20),
+    )(scalars, score_grad, frame_rows)
+    near_a, near_b, *sends = pl.pallas_call(
+        join_kernel,
+        out_shape=[jax.ShapeDtypeStruct((query_count + tap_rows, part_width), F32), near]
+        + [jax.ShapeDtypeStruct((rows, out_width), F32)] * chips,
+        in_specs=whole_spec(6),
+        out_specs=whole_spec(2 + chips),
+        compiler_params=params(8),
+        cost_estimate=cost(rows * width, 4 << 20),
+    )(near_a, near_b, taps_behind, taps_ahead, keep, crossed)
     near_a = lax.ppermute(near_a, "rec", onward)
     near_b = lax.ppermute(near_b, "rec", back)
-    near_a, near_b, frame_part = lax.optimization_barrier((near_a, near_b, frame_part))
-    frame_sum = lax.psum_scatter(frame_part, "query", scatter_dimension=1, tiled=True)
+    arrived = [
+        lax.ppermute(sends[k], "query", [(i, (i + 2 * k) % blocks) for i in range(blocks)])
+        for k in range(1, chips)
+    ]
     chunks = pl.pallas_call(
         sum_kernel,
         out_shape=jax.ShapeDtypeStruct((tms, chunk_rows + UNIT, part_width), F32),
-        in_specs=whole_spec(5),
+        in_specs=whole_spec(6),
         out_specs=pl.BlockSpec(memory_space=VMEM),
         compiler_params=params(8),
         cost_estimate=cost(4 * query_count * part_width, 4 << 20),
-    )(own, taps_own, near_a, near_b, taps_far)
+    )(own, far_a, taps_behind, taps_ahead, near_a, near_b)
     chunk = jnp.sum(lax.all_to_all(chunks, "tm", 0, 0), axis=0)
-    frame_sum, chunk = lax.optimization_barrier((frame_sum, chunk))
     whole = lax.all_gather(chunk, "tm")
+    *arrived, whole = lax.optimization_barrier((*arrived, whole))
+    frame_sum = sends[0]
+    for term in arrived:
+        frame_sum = frame_sum + term
     query_sum = whole[:, :chunk_rows].reshape(query_count, part_width)
     tap_sum = whole[: tap_rows // UNIT, chunk_rows:].reshape(halves, tap_rows // halves, part_width)
     tap_sum = jnp.concatenate([tap_sum[h, :count] for h in range(halves)], axis=1)

time: 177 us -> 169 us (0.955)
  blocking collectives: 91 us -> 45.8 us
  starting transfers between devices: 20.4 us -> 47 us
  waiting for transfers between devices: 18.6 us -> 43.8 us
  between operations: 14.8 us -> 1.58 us
    all_to_all x1 -> x0, blocking collectives: 49.1 us -> none  [per_device(): chunk = jnp.sum(lax.all_to_all(chunks, 'tm', 0, 0), axis=0)]
    all_to_all x0 -> x1, waiting for transfers between devices: none -> 21.9 us  [per_device(): chunk = jnp.sum(lax.all_to_all(chunks, 'tm', 0, 0), axis=0)]
    all_to_all x0 -> x1, starting transfers between devices: none -> 16 us  [per_device(): chunk = jnp.sum(lax.all_to_all(chunks, 'tm', 0, 0), axis=0)]
    ppermute x3 -> x6, starting transfers between devices: 9.15 us -> 18.3 us  [the longest x3 9.34 us: per_device(): lax.ppermute(sends[k], 'query', [(i, (i + 2 * k) % blocks) for i in range...]
    all_gather x1, blocking collectives: 32 us -> 35.9 us  [per_device(): whole = lax.all_gather(chunk, 'tm')]
    pallas_call x2, Pallas kernels: 4.99 us -> 1.44 us  [the longest x1 1.17 us: per_device(): pl.pallas_call(near_kernel, out_shape=[near, near, near], in_specs=[smem]...]
    pallas_call x1, Pallas kernels: 6.06 us -> 9.31 us  [per_device(): pl.pallas_call(lambda *refs: grad_kernel(half, *refs), out_shape=[jax.Sha...]
    ppermute x3 -> x6, waiting for transfers between devices: 4.53 us -> 6.57 us  [the longest x1 5.32 us: per_device(): taps_ahead = lax.ppermute(far_b, 'rec', back)]
  transfers between devices with their start and end apart: 8 -> 11, of which waited for: 3 -> 5; matrix products, arithmetic and copies ran while one was open for 0% -> 0% of each run, Pallas kernels for 4% -> 3%
where the time goes in v5:
time: 169 us; the launch traced here: 168 us
  starting transfers between devices  47 us (28%)
  blocking collectives  45.8 us (27%)
  waiting for transfers between devices  43.8 us (26%)
  Pallas kernels  25.8 us (15%)
  other arithmetic  2.15 us (1%)
  local copies, waits for them, and re-layouts  2.03 us (1%)
    all_gather x1, blocking collectives, per_device(): whole = lax.all_gather(chunk, 'tm')  35.9 us
    all_to_all x1, waiting for transfers between devices, per_device(): chunk = jnp.sum(lax.all_to_all(chunks, 'tm', 0, 0), axis=0)  21.9 us
    all_to_all x1, starting transfers between devices, per_device(): chunk = jnp.sum(lax.all_to_all(chunks, 'tm', 0, 0), axis=0)  16 us
    ppermute x1, waiting for transfers between devices, per_device(): near_b = lax.ppermute(near_b, 'rec', back)  14.1 us
    all_to_all x1, blocking collectives, per_device(): lax.all_to_all(jnp.broadcast_to(stats[None], (blocks,) + stats.shape), 'q...  9.92 us
    pallas_call x1, Pallas kernels, per_device(): pl.pallas_call(lambda *refs: smooth_kernel(scale, half, *refs), out_shape...  9.65 us
    ppermute x3, starting transfers between devices, per_device(): lax.ppermute(sends[k], 'query', [(i, (i + 2 * k) % blocks) for i in range...  9.34 us
    pallas_call x1, Pallas kernels, per_device(): pl.pallas_call(lambda *refs: grad_kernel(half, *refs), out_shape=[jax.Sha...  9.31 us
  transfers between devices with their start and end apart: 11, of which 5 were waited for; matrix products, arithmetic and copies ran while one was open for 0% of the time, Pallas kernels for 3%

profile of v5, /device:TPU:6, one launch (start us, length us, event | category | flops | bytes accessed | tf_op | source)
XLA Modules:
  0.0 168.1 jit_solution(4592976863215634328)
XLA Ops:
  0.6 0.0 copy-start
  0.6 1.2 copy-done
  1.9 0.0 copy-start.4
  1.9 0.7 copy-done.4
  2.5 0.0 copy-start.1
  2.5 0.0 copy-start.2
  2.5 0.1 shard_map.77
  2.6 4.0 %collective-permute-start = (f32[40,1024]{1,0:T(8,128)S(1)}, f32[40,1024]{1,0:T(8,128)S(1)}, u32[]{:S(2)}, u32[]{:S(2)}) collective-permute-start(f32[40,1024]{1,0:T(8,128)S(1)} %get-tuple-element.27), channel_id=1, source_target_pairs={{0,32},{32,64},{64,96},{96,128},{128,160},{160,192},{192,224},{224... | collective-permute-start | bytes 491528 | tf_op jit(solution)/shard_map/ppermute | solution.py:339
  6.6 1.3 collective-permute-start.1
  7.9 0.0 copy-start.3
  7.9 0.0 copy-start.5
  8.7 0.1 stack.59.refs_0_.scalars
  8.8 0.0 copy-done.1
  8.8 0.0 copy-done.2
  8.8 4.3 %shard_map.76 = f32[512,512]{1,0:T(8,128)S(1)} custom-call(s32[15]{0:T(128)S(1)} %stack.59.refs_0_.scalars, bf16[512,1024]{1,0:T(8,128)(2,1)S(1)} %bitcast.27, bf16[512,1024]{1,0:T(8,128)(2,1)S(1)} %copy-done.2), custom_call_target="tpu_custom_call" | custom-call | flops 1073741824 | bytes 3145728 | tf_op jit(solution)/shard_map/pallas_call | solution.py:342
  13.1 0.0 collective-permute-done.refs_2_
  13.1 1.2 collective-permute-done.1.refs_3_
  14.3 0.0 copy-done.3
  14.3 0.0 copy-done.5
  14.3 9.7 %shard_map.78 = (f32[128,8,512]{2,1,0:T(8,128)S(1)}, f32[96,8,512]{2,1,0:T(8,128)S(1)}, f32[2,8,128]{2,1,0:T(8,128)S(1)}, f32[8,128]{1,0:T(8,128)S(1)}) custom-call(s32[15]{0:T(128)S(1)} %stack.59.refs_0_.scalars, f32[64,8,512]{2,1,0:T(8,128)S(1)} %bitcast.30, f32[40,1024]{1,0:T(8,128)S(1)} %collective-permute-done.refs_2_, ...), custom_call_target="tpu_custom_call" | custom-call | flops 34603008 | bytes 6291456 | tf_op jit(solution)/shard_map/pallas_call | solution.py:357
  24.0 9.9 %all_to_all.10.refs_4_ = f32[8,2,8,128]{3,2,1,0:T(8,128)S(1)} all-to-all(f32[8,2,8,128]{3,2,1,0:T(8,128)S(1)} %broadcast_in_dim.4), channel_id=1, replica_groups=mesh['tm'=16,'query'=8,'rec'=4] {'query'}, dimensions={0} | all-to-all | bytes 131072 | tf_op jit(solution)/shard_map/all_to_all | solution.py:371
  33.9 9.3 %shard_map.79 = (bf16[512,512]{1,0:T(8,128)(2,1)S(1)}, f32[336,256]{1,0:T(8,128)S(1)}, f32[336,256]{1,0:T(8,128)S(1)}, f32[4,512,128]{2,1,0:T(8,128)S(1)}, f32[4,512,128]{2,1,0:T(8,128)S(1)}) custom-call(s32[15]{0:T(128)S(1)} %stack.59.refs_0_.scalars, f32[96,8,512]{2,1,0:T(8,128)S(1)} %get-tuple-element.29.refs_1_, ...), custom_call_target="tpu_custom_call" | custom-call | flops 571473920 | bytes 8388608 | tf_op jit(solution)/shard_map/pallas_call | solution.py:380
  43.2 1.9 %collective-permute-start.4 = (f32[4,512,128]{2,1,0:T(8,128)S(1)}, f32[4,512,128]{2,1,0:T(8,128)S(1)}, u32[]{:S(2)}, u32[]{:S(2)}) collective-permute-start(f32[4,512,128]{2,1,0:T(8,128)S(1)} %get-tuple-element.39), channel_id=1, source_target_pairs={{0,4},{4,0},{8,12},{12,8},{16,20},{20,16},{24,28},{28,24},{1,5},{5... | collective-permute-start | bytes 3145736 | tf_op jit(solution)/shard_map/ppermute | solution.py:399
  45.1 2.7 %collective-permute-start.3 = (f32[336,256]{1,0:T(8,128)S(1)}, f32[336,256]{1,0:T(8,128)S(1)}, u32[]{:S(2)}, u32[]{:S(2)}) collective-permute-start(f32[336,256]{1,0:T(8,128)S(1)} %get-tuple-element.37), channel_id=1, source_target_pairs={{1,0},{2,1},{3,2},{0,3},{5,4},{6,5},{7,6},{4,7},{9,8},{10,9},{11,1... | collective-permute-start | bytes 1032200 | tf_op jit(solution)/shard_map/ppermute | solution.py:398
  47.9 4.3 %collective-permute-start.2 = (f32[336,256]{1,0:T(8,128)S(1)}, f32[336,256]{1,0:T(8,128)S(1)}, u32[]{:S(2)}, u32[]{:S(2)}) collective-permute-start(f32[336,256]{1,0:T(8,128)S(1)} %get-tuple-element.36.taps), channel_id=1, source_target_pairs={{0,1},{1,2},{2,3},{3,0},{4,5},{5,6},{6,7},{7,4},{8,9},{9,10},{10,1... | collective-permute-start | bytes 1032200 | tf_op jit(solution)/shard_map/ppermute | solution.py:397
  52.2 1.2 shard_map.80
  53.4 5.3 %collective-permute-done.3.from_ahead.taps_ahead = f32[336,256]{1,0:T(8,128)S(1)} collective-permute-done((f32[336,256]{1,0:T(8,128)S(1)}, f32[336,256]{1,0:T(8,128)S(1)}, u32[]{:S(2)}, u32[]{:S(2)}) %collective-permute-start.3) | collective-permute-done | bytes 344096 | tf_op jit(solution)/shard_map/ppermute | solution.py:398
  58.7 1.2 collective-permute-done.2.from_behind.taps_behind
  60.0 0.0 collective-permute-done.4.crossed
  60.0 0.3 shard_map.81
  60.2 5.5 %collective-permute-start.8 = (f32[592,256]{1,0:T(8,128)S(1)}, f32[592,256]{1,0:T(8,128)S(1)}, u32[]{:S(2)}, u32[]{:S(2)}) collective-permute-start(f32[592,256]{1,0:T(8,128)S(1)} %get-tuple-element.45), channel_id=1, source_target_pairs={{0,1},{1,2},{2,3},{3,0},{4,5},{5,6},{6,7},{7,4},{8,9},{9,10},{10,1... | collective-permute-start | bytes 1818632 | tf_op jit(solution)/shard_map/ppermute | solution.py:418
  65.8 1.9 %collective-permute-start.9 = (f32[512,256]{1,0:T(8,128)S(1)}, f32[512,256]{1,0:T(8,128)S(1)}, u32[]{:S(2)}, u32[]{:S(2)}) collective-permute-start(f32[512,256]{1,0:T(8,128)S(1)} %get-tuple-element.46), channel_id=1, source_target_pairs={{1,0},{2,1},{3,2},{0,3},{5,4},{6,5},{7,6},{4,7},{9,8},{10,9},{11,1... | collective-permute-start | bytes 1572872 | tf_op jit(solution)/shard_map/ppermute | solution.py:419
  67.7 14.1 %collective-permute-done.9.from_ahead = f32[512,256]{1,0:T(8,128)S(1)} collective-permute-done((f32[512,256]{1,0:T(8,128)S(1)}, f32[512,256]{1,0:T(8,128)S(1)}, u32[]{:S(2)}, u32[]{:S(2)}) %collective-permute-start.9) | collective-permute-done | bytes 524320 | tf_op jit(solution)/shard_map/ppermute | solution.py:419
  81.8 0.0 collective-permute-done.8.from_behind
  81.8 1.0 shard_map.82
  82.8 16.0 %all-to-all-start.1 = ((f32[16,40,256]{2,1,0:T(8,128)}), f32[16,40,256]{2,1,0:T(8,128)S(1)}, u32[]{:S(2)}, u32[]{:S(2)}) async-start(f32[16,40,256]{2,1,0:T(8,128)} %shard_map.82), calls=%async_computation.1 | async-start | bytes 1310720 | tf_op jit(solution)/shard_map/all_to_all | solution.py:432
  98.8 2.5 %collective-permute-start.5 = (f32[512,128]{1,0:T(8,128)S(1)}, f32[512,128]{1,0:T(8,128)S(1)}, u32[]{:S(2)}, u32[]{:S(2)}) collective-permute-start(f32[512,128]{1,0:T(8,128)S(1)} %get-tuple-element.41), channel_id=1, source_target_pairs={{0,8},{4,12},{8,16},{12,20},{16,24},{20,28},{24,0},{28,4},{1,9},{5... | collective-permute-start | bytes 786440 | tf_op jit(solution)/shard_map/ppermute | solution.py:421
  101.2 4.0 %collective-permute-start.6 = (f32[512,128]{1,0:T(8,128)S(1)}, f32[512,128]{1,0:T(8,128)S(1)}, u32[]{:S(2)}, u32[]{:S(2)}) collective-permute-start(f32[512,128]{1,0:T(8,128)S(1)} %get-tuple-element.42), channel_id=1, source_target_pairs={{0,16},{4,20},{8,24},{12,28},{16,0},{20,4},{24,8},{28,12},{1,17},{... | collective-permute-start | bytes 786440 | tf_op jit(solution)/shard_map/ppermute | solution.py:421
  105.2 2.9 %collective-permute-start.7 = (f32[512,128]{1,0:T(8,128)S(1)}, f32[512,128]{1,0:T(8,128)S(1)}, u32[]{:S(2)}, u32[]{:S(2)}) collective-permute-start(f32[512,128]{1,0:T(8,128)S(1)} %get-tuple-element.43), channel_id=1, source_target_pairs={{0,24},{4,28},{8,0},{12,4},{16,8},{20,12},{24,16},{28,20},{1,25},{... | collective-permute-start | bytes 786440 | tf_op jit(solution)/shard_map/ppermute | solution.py:421
  108.1 21.9 %all-to-all-done.1 = f32[16,40,256]{2,1,0:T(8,128)S(1)} async-done(((f32[16,40,256]{2,1,0:T(8,128)}), f32[16,40,256]{2,1,0:T(8,128)S(1)}, u32[]{:S(2)}, u32[]{:S(2)}) %all-to-all-start.1) | async-done | bytes 655392 | tf_op jit(solution)/shard_map/all_to_all | solution.py:432
  130.1 35.9 %all-gather = f32[640,256]{1,0:T(8,128)S(1)} all-gather(f32[40,256]{1,0:T(8,128)S(1)} %reduce_sum.9), channel_id=2, replica_groups=mesh['tm'=16,'query'=8,'rec'=4] {'tm'}, dimensions={0}, use_global_device_ids=true | all-gather | bytes 696320 | tf_op jit(solution)/shard_map/all_gather | solution.py:433
  166.0 0.0 collective-permute-done.5
  166.0 0.0 collective-permute-done.6
  166.0 0.0 collective-permute-done.7
  166.0 0.8 multiply_convert_fusion
  166.8 0.6 pad_maximum_fusion
  167.4 0.7 fusion
  (4 shorter events, 0.1 us)
Async XLA Ops:
  0.6 1.2 copy-start
  1.9 0.7 copy-start.4
  2.5 6.2 %copy-start.1 = (bf16[1,512,1024]{2,1,0:T(8,128)(2,1)S(1)}, bf16[1,512,1024]{2,1,0:T(8,128)(2,1)}, u32[]{:S(2)}) copy-start(bf16[1,512,1024]{2,1,0:T(8,128)(2,1)} %param.5) | copy-start | bytes 3145732
  2.5 6.2 %copy-start.2 = (bf16[512,1024]{1,0:T(8,128)(2,1)S(1)}, bf16[512,1024]{1,0:T(8,128)(2,1)}, u32[]{:S(2)}) copy-start(bf16[512,1024]{1,0:T(8,128)(2,1)} %refs_7_.1) | copy-start | bytes 3145732
  2.6 10.5 %collective-permute-start = (f32[40,1024]{1,0:T(8,128)S(1)}, f32[40,1024]{1,0:T(8,128)S(1)}, u32[]{:S(2)}, u32[]{:S(2)}) collective-permute-start(f32[40,1024]{1,0:T(8,128)S(1)} %get-tuple-element.27), channel_id=1, source_target_pairs={{0,32},{32,64},{64,96},{96,128},{128,160},{160,192},{192,224},{224... | collective-permute-start | bytes 491528 | tf_op jit(solution)/shard_map/ppermute | solution.py:339
  6.6 7.7 %collective-permute-start.1 = (f32[40,1024]{1,0:T(8,128)S(1)}, f32[40,1024]{1,0:T(8,128)S(1)}, u32[]{:S(2)}, u32[]{:S(2)}) collective-permute-start(f32[40,1024]{1,0:T(8,128)S(1)} %get-tuple-element.28), channel_id=1, source_target_pairs={{32,0},{64,32},{96,64},{128,96},{160,128},{192,160},{224,192},{256... | collective-permute-start | bytes 491528 | tf_op jit(solution)/shard_map/ppermute | solution.py:340
  7.9 6.4 %copy-start.3 = (f32[33,512]{1,0:T(8,128)S(1)}, f32[33,512]{1,0:T(8,128)}, u32[]{:S(2)}) copy-start(f32[33,512]{1,0:T(8,128)} %refs_8_.1) | copy-start | bytes 202756
  7.9 6.4 %copy-start.5 = (s32[1,512]{1,0:T(1,128)S(1)}, s32[1,512]{1,0:T(1,128)}, u32[]{:S(2)}) copy-start(s32[1,512]{1,0:T(1,128)} %refs_4_.1) | copy-start | bytes 6148
  43.2 16.7 %collective-permute-start.4 = (f32[4,512,128]{2,1,0:T(8,128)S(1)}, f32[4,512,128]{2,1,0:T(8,128)S(1)}, u32[]{:S(2)}, u32[]{:S(2)}) collective-permute-start(f32[4,512,128]{2,1,0:T(8,128)S(1)} %get-tuple-element.39), channel_id=1, source_target_pairs={{0,4},{4,0},{8,12},{12,8},{16,20},{20,16},{24,28},{28,24},{1,5},{5... | collective-permute-start | bytes 3145736 | tf_op jit(solution)/shard_map/ppermute | solution.py:399
  45.1 13.6 %collective-permute-start.3 = (f32[336,256]{1,0:T(8,128)S(1)}, f32[336,256]{1,0:T(8,128)S(1)}, u32[]{:S(2)}, u32[]{:S(2)}) collective-permute-start(f32[336,256]{1,0:T(8,128)S(1)} %get-tuple-element.37), channel_id=1, source_target_pairs={{1,0},{2,1},{3,2},{0,3},{5,4},{6,5},{7,6},{4,7},{9,8},{10,9},{11,1... | collective-permute-start | bytes 1032200 | tf_op jit(solution)/shard_map/ppermute | solution.py:398
  47.9 12.1 %collective-permute-start.2 = (f32[336,256]{1,0:T(8,128)S(1)}, f32[336,256]{1,0:T(8,128)S(1)}, u32[]{:S(2)}, u32[]{:S(2)}) collective-permute-start(f32[336,256]{1,0:T(8,128)S(1)} %get-tuple-element.36.taps), channel_id=1, source_target_pairs={{0,1},{1,2},{2,3},{3,0},{4,5},{5,6},{6,7},{7,4},{8,9},{9,10},{10,1... | collective-permute-start | bytes 1032200 | tf_op jit(solution)/shard_map/ppermute | solution.py:397
  60.2 21.6 %collective-permute-start.8 = (f32[592,256]{1,0:T(8,128)S(1)}, f32[592,256]{1,0:T(8,128)S(1)}, u32[]{:S(2)}, u32[]{:S(2)}) collective-permute-start(f32[592,256]{1,0:T(8,128)S(1)} %get-tuple-element.45), channel_id=1, source_target_pairs={{0,1},{1,2},{2,3},{3,0},{4,5},{5,6},{6,7},{7,4},{8,9},{9,10},{10,1... | collective-permute-start | bytes 1818632 | tf_op jit(solution)/shard_map/ppermute | solution.py:418
  65.8 16.0 %collective-permute-start.9 = (f32[512,256]{1,0:T(8,128)S(1)}, f32[512,256]{1,0:T(8,128)S(1)}, u32[]{:S(2)}, u32[]{:S(2)}) collective-permute-start(f32[512,256]{1,0:T(8,128)S(1)} %get-tuple-element.46), channel_id=1, source_target_pairs={{1,0},{2,1},{3,2},{0,3},{5,4},{6,5},{7,6},{4,7},{9,8},{10,9},{11,1... | collective-permute-start | bytes 1572872 | tf_op jit(solution)/shard_map/ppermute | solution.py:419
  82.8 47.3 %all-to-all-start.1 = ((f32[16,40,256]{2,1,0:T(8,128)}), f32[16,40,256]{2,1,0:T(8,128)S(1)}, u32[]{:S(2)}, u32[]{:S(2)}) async-start(f32[16,40,256]{2,1,0:T(8,128)} %shard_map.82), calls=%async_computation.1 | async-start | bytes 1310720 | tf_op jit(solution)/shard_map/all_to_all | solution.py:432
  98.8 67.2 %collective-permute-start.5 = (f32[512,128]{1,0:T(8,128)S(1)}, f32[512,128]{1,0:T(8,128)S(1)}, u32[]{:S(2)}, u32[]{:S(2)}) collective-permute-start(f32[512,128]{1,0:T(8,128)S(1)} %get-tuple-element.41), channel_id=1, source_target_pairs={{0,8},{4,12},{8,16},{12,20},{16,24},{20,28},{24,0},{28,4},{1,9},{5... | collective-permute-start | bytes 786440 | tf_op jit(solution)/shard_map/ppermute | solution.py:421
  101.2 64.7 %collective-permute-start.6 = (f32[512,128]{1,0:T(8,128)S(1)}, f32[512,128]{1,0:T(8,128)S(1)}, u32[]{:S(2)}, u32[]{:S(2)}) collective-permute-start(f32[512,128]{1,0:T(8,128)S(1)} %get-tuple-element.42), channel_id=1, source_target_pairs={{0,16},{4,20},{8,24},{12,28},{16,0},{20,4},{24,8},{28,12},{1,17},{... | collective-permute-start | bytes 786440 | tf_op jit(solution)/shard_map/ppermute | solution.py:421
  105.2 60.8 %collective-permute-start.7 = (f32[512,128]{1,0:T(8,128)S(1)}, f32[512,128]{1,0:T(8,128)S(1)}, u32[]{:S(2)}, u32[]{:S(2)}) collective-permute-start(f32[512,128]{1,0:T(8,128)S(1)} %get-tuple-element.43), channel_id=1, source_target_pairs={{0,24},{4,28},{8,0},{12,4},{16,8},{20,12},{24,16},{28,20},{1,25},{... | collective-permute-start | bytes 786440 | tf_op jit(solution)/shard_map/ppermute | solution.py:421

commit v6 on v5

--- a/solution.py
+++ b/solution.py
@@ -165,7 +165,7 @@
 
 def grad_kernel(
     half, scalars, powers, scores, mine, others, labels, frames, queries, taps,
-    score_grad, ahead, behind, keep_frames, cross_frames, wide, grads, tap_grads, placed, frame_part,
+    chunks, tap_sums, keep_frames, cross_frames, wide, grads, tap_grads, placed, frame_part,
 ):
     blk = powers.shape[0] - 2 * half
     rows = blk * SUB
@@ -225,73 +225,43 @@
         return 0
 
     lax.fori_loop(0, blk // UNIT, correlate, 0)
-    parts = jnp.sum(tap_grads[...], axis=1)
-    tall = padded_rows_of(count)
-    parts = jnp.concatenate([parts, jnp.zeros((tall - count, query_count), F32)], axis=0)
+    tap_sums[:count, :] = jnp.sum(tap_grads[...], axis=1)
+    tap_sums[count:, :] = jnp.zeros((tap_sums.shape[0] - count, query_count), F32)
     natural = jnp.dot(placement(rows, blk, True), placed[...], preferred_element_type=F32)
+    turned = natural.T.astype(jnp.bfloat16)
     natural = natural.astype(jnp.bfloat16)
-    score_grad[...] = natural
-    part_width = ahead.shape[1]
-    middle = query_count // 2
-    far = column_block(frames, scalars[5], part_width)
-    part = jnp.dot(turn_over(natural), far, preferred_element_type=F32)
-    ahead[:middle, :] = part[:middle]
-    behind[:middle, :] = part[middle:]
-    for h in range(query_count // part_width):
-        block = parts[:, h * part_width : (h + 1) * part_width]
-        ahead[middle + h * tall : middle + (h + 1) * tall, :] = block
-        behind[middle + h * tall : middle + (h + 1) * tall, :] = block
+    recs, part_rows, part_width = chunks.shape
+    for r in range(recs):
+        chunks[r] = jnp.dot(turned, frames[:, r * part_width : (r + 1) * part_width], preferred_element_type=F32)
     frame_part[...] = jnp.dot(natural, queries[...], preferred_element_type=F32)
     chips, _, out_width = keep_frames.shape
     for k in range(chips):
-        keep_frames[k] = column_block(frame_part, scalars[7 + k], out_width)
-        cross_frames[k] = column_block(frame_part, scalars[7 + chips + k], out_width)
+        keep_frames[k] = column_block(frame_part, scalars[3 + k], out_width)
+        cross_frames[k] = column_block(frame_part, scalars[3 + chips + k], out_width)
 
 
 def column_block(frames, index, width):
     return frames[:, pl.ds(pl.multiple_of(index * width, LANES), width)]
 
 
-def turn_over(score_grad):
-    return score_grad.astype(F32).T.astype(jnp.bfloat16)
-
-
-def near_kernel(scalars, score_grad, frames, own, ahead, behind):
-    turned = turn_over(score_grad[...])
-    for index, out in ((3, own), (4, ahead), (6, behind)):
-        block = column_block(frames, scalars[index], out.shape[1])
-        out[...] = jnp.dot(turned, block, preferred_element_type=F32)
-
-
-def join_kernel(ahead_in, behind_in, from_behind, from_ahead, keep, crossed, ahead, behind, *frame_out):
-    query_count = ahead_in.shape[0]
-    middle = query_count // 2
-    ahead[:middle, :] = ahead_in[:middle, :] + from_behind[:middle, :]
-    ahead[middle:query_count, :] = ahead_in[middle:, :]
-    ahead[query_count:, :] = from_behind[middle:, :]
-    behind[:middle, :] = behind_in[:middle, :]
-    behind[middle:, :] = behind_in[middle:, :] + from_ahead[:middle, :]
-    for k, out in enumerate(frame_out):
-        out[...] = keep[k] + crossed[k]
-
-
-def sum_kernel(own, taps, taps_behind, taps_ahead, from_behind, from_ahead, chunks):
-    tms, padded_rows, _ = chunks.shape
-    query_count = own.shape[0]
-    middle = query_count // 2
+def sum_kernel(arrived, taps_own, taps_far, taps_behind, taps_ahead, chunks, taps):
+    tms, padded_rows, part_width = chunks.shape
+    tall, query_count = taps.shape
+    taps[...] = (taps_own[...] + taps_far[...]) + (taps_behind[...] + taps_ahead[...])
     chunk_rows = query_count // tms
-    tap_rows = padded_rows - chunk_rows
+    tap_blocks = tall // UNIT
     for z in range(tms):
         rows = slice(z * chunk_rows, (z + 1) * chunk_rows)
-        chunks[z, :chunk_rows, :] = own[rows, :] + from_behind[rows, :] + from_ahead[rows, :]
-        if z * tap_rows < from_behind.shape[0] - query_count:
-            rows = slice(middle + z * tap_rows, middle + (z + 1) * tap_rows)
-            late = slice(query_count + z * tap_rows, query_count + (z + 1) * tap_rows)
-            chunks[z, chunk_rows:, :] = (
-                taps[rows, :] + taps_behind[rows, :] + taps_ahead[rows, :] + from_behind[late, :]
-            )
+        total = arrived[0, rows, :]
+        for r in range(1, arrived.shape[0]):
+            total = total + arrived[r, rows, :]
+        chunks[z, :chunk_rows, :] = total
+        h, t = z // tap_blocks, z % tap_blocks
+        if h * part_width < query_count:
+            block = taps[t * UNIT : (t + 1) * UNIT, h * part_width : (h + 1) * part_width]
+            chunks[z, chunk_rows:, :] = block
         else:
-            chunks[z, chunk_rows:, :] = jnp.zeros((tap_rows, own.shape[1]), F32)
+            chunks[z, chunk_rows:, :] = jnp.zeros((UNIT, part_width), F32)
 
 
 def padded_rows_of(count):
@@ -308,15 +278,13 @@
     blk = rows // SUB
     scale = 10.0 / math.sqrt(width)
     recs, tms, blocks = lax.axis_size("rec"), lax.axis_size("tm"), lax.axis_size("query")
-    rec = lax.axis_index("rec")
-    ring = [(rec + step) % recs for step in range(4)]
     query_index = lax.axis_index("query")
     chips = blocks // 2
     chip, core = query_index // 2, query_index % 2
     keep_ids = [(chip + k) % chips * 2 + core for k in range(chips)]
     cross_ids = [(chip + k) % chips * 2 + 1 - core for k in range(chips)]
     scalars = jnp.stack(
-        [lax.axis_index("tm") * rows, lengths[0], query_index * query_count] + ring + keep_ids + cross_ids
+        [lax.axis_index("tm") * rows, lengths[0], query_index * query_count] + keep_ids + cross_ids
     ).astype(jnp.int32)
     smem = pl.BlockSpec(memory_space=pltpu.SMEM)
 
@@ -371,17 +339,18 @@
     others = lax.all_to_all(jnp.broadcast_to(stats[None], (blocks,) + stats.shape), "query", 0, 0)
     chunk_rows = query_count // tms
     part_width = width // recs
-    middle = query_count // 2
-    halves = query_count // part_width
-    tap_rows = halves * padded_rows_of(count)
     out_width = width // blocks
-    step = jax.ShapeDtypeStruct((middle + tap_rows, part_width), F32)
     terms = jax.ShapeDtypeStruct((chips, rows, out_width), F32)
-    score_grad, far_a, far_b, keep, cross = pl.pallas_call(
+    parts, tap_sum, keep, cross = pl.pallas_call(
         lambda *refs: grad_kernel(half, *refs),
-        out_shape=[jax.ShapeDtypeStruct((rows, query_count), jnp.bfloat16), step, step, terms, terms],
+        out_shape=[
+            jax.ShapeDtypeStruct((recs, query_count, part_width), F32),
+            jax.ShapeDtypeStruct((padded_rows_of(count), query_count), F32),
+            terms,
+            terms,
+        ],
         in_specs=[smem] + whole_spec(8),
-        out_specs=whole_spec(5),
+        out_specs=whole_spec(4),
         scratch_shapes=[
             VMEM((count, SUB, query_count), F32),
             VMEM((blk + rim, SUB, query_count), F32),
@@ -392,51 +361,32 @@
         compiler_params=params(20),
         cost_estimate=cost(2 * rows * query_count * (width + 2 * count), 8 << 20),
     )(scalars, powers, scores, stats, others, tile, frame_rows, queries, kernel)
-    onward = [(i, (i + 1) % recs) for i in range(recs)]
-    back = [(j, i) for i, j in onward]
-    taps_behind = lax.ppermute(far_a, "rec", onward)
-    taps_ahead = lax.ppermute(far_b, "rec", back)
+    parts = lax.all_to_all(parts, "rec", 0, 0)
     crossed = lax.ppermute(cross, "query", [(i, i ^ 1) for i in range(blocks)])
-    near = jax.ShapeDtypeStruct((query_count, part_width), F32)
-    own, near_a, near_b = pl.pallas_call(
-        near_kernel,
-        out_shape=[near, near, near],
-        in_specs=[smem] + whole_spec(2),
-        out_specs=whole_spec(3),
-        compiler_params=params(12),
-        cost_estimate=cost(2 * rows * query_count * width, 4 << 20),
-    )(scalars, score_grad, frame_rows)
-    near_a, near_b, *sends = pl.pallas_call(
-        join_kernel,
-        out_shape=[jax.ShapeDtypeStruct((query_count + tap_rows, part_width), F32), near]
-        + [jax.ShapeDtypeStruct((rows, out_width), F32)] * chips,
-        in_specs=whole_spec(6),
-        out_specs=whole_spec(2 + chips),
-        compiler_params=params(8),
-        cost_estimate=cost(rows * width, 4 << 20),
-    )(near_a, near_b, taps_behind, taps_ahead, keep, crossed)
-    near_a = lax.ppermute(near_a, "rec", onward)
-    near_b = lax.ppermute(near_b, "rec", back)
-    arrived = [
-        lax.ppermute(sends[k], "query", [(i, (i + 2 * k) % blocks) for i in range(blocks)])
-        for k in range(1, chips)
+    far, behind, ahead = [
+        lax.ppermute(tap_sum, "rec", [(i, (i + k) % recs) for i in range(recs)]) for k in (2, 1, 3)
     ]
+    parts, keep, crossed = lax.optimization_barrier((parts, keep, crossed))
     chunks = pl.pallas_call(
         sum_kernel,
         out_shape=jax.ShapeDtypeStruct((tms, chunk_rows + UNIT, part_width), F32),
-        in_specs=whole_spec(6),
+        in_specs=whole_spec(5),
         out_specs=pl.BlockSpec(memory_space=VMEM),
+        scratch_shapes=[VMEM((padded_rows_of(count), query_count), F32)],
         compiler_params=params(8),
         cost_estimate=cost(4 * query_count * part_width, 4 << 20),
-    )(own, far_a, taps_behind, taps_ahead, near_a, near_b)
+    )(parts, tap_sum, far, behind, ahead)
     chunk = jnp.sum(lax.all_to_all(chunks, "tm", 0, 0), axis=0)
+    sends = [keep[k] + crossed[k] for k in range(chips)]
+    frame_sum = sends[0]
+    for k in range(1, chips):
+        frame_sum = frame_sum + lax.ppermute(sends[k], "query", [(i, (i + 2 * k) % blocks) for i in range(blocks)])
+    chunk, frame_sum = lax.optimization_barrier((chunk, frame_sum))
     whole = lax.all_gather(chunk, "tm")
-    *arrived, whole = lax.optimization_barrier((*arrived, whole))
-    frame_sum = sends[0]
-    for term in arrived:
-        frame_sum = frame_sum + term
     query_sum = whole[:, :chunk_rows].reshape(query_count, part_width)
-    tap_sum = whole[: tap_rows // UNIT, chunk_rows:].reshape(halves, tap_rows // halves, part_width)
+    halves = query_count // part_width
+    tall = padded_rows_of(count)
+    tap_sum = whole[: halves * tall // UNIT, chunk_rows:].reshape(halves, tall, part_width)
     tap_sum = jnp.concatenate([tap_sum[h, :count] for h in range(halves)], axis=1)
     grad_frames = (frame_sum * scale).astype(jnp.bfloat16)[None]
     grad_queries = (query_sum * scale).astype(jnp.bfloat16)

time: 169 us -> 165 us (0.976)
  waiting for transfers between devices: 43.8 us -> 38.1 us
  Pallas kernels: 25.8 us -> 23.4 us
  local copies, waits for them, and re-layouts: 2.03 us -> 4.3 us
  other arithmetic: 2.15 us -> 4.34 us
    ppermute x4 -> x3, waiting for transfers between devices: 20.7 us -> 1.93 us  [per_device(): lax.ppermute(tap_sum, 'rec', [(i, (i + k) % recs) for i in range(recs)])]
    all_to_all x0 -> x1, waiting for transfers between devices: none -> 14.6 us  [per_device(): parts = lax.all_to_all(parts, 'rec', 0, 0)]
    all_to_all x1, waiting for transfers between devices: 21.9 us -> 12.3 us  [per_device(): chunk = jnp.sum(lax.all_to_all(chunks, 'tm', 0, 0), axis=0)]
    ppermute x3, waiting for transfers between devices: 0.01 us -> 7.84 us  [per_device(): lax.ppermute(sends[k], 'query', [(i, (i + 2 * k) % blocks) for i in range...]
    ppermute x4 -> x3, starting transfers between devices: 14.5 us -> 9.21 us  [per_device(): lax.ppermute(tap_sum, 'rec', [(i, (i + k) % recs) for i in range(recs)])]
    all_to_all x0 -> x1, starting transfers between devices: none -> 4.77 us  [per_device(): parts = lax.all_to_all(parts, 'rec', 0, 0)]
    unnamed x12 -> x16, local copies, waits for them, and re-layouts: 1.92 us -> 4.19 us
    add x0 -> x2, other arithmetic: none -> 2.23 us  [the longest x1 1.19 us: per_device(): sends = [keep[k] + crossed[k] for k in range(chips)]]
  transfers between devices with their start and end apart: 11 -> 11, of which waited for: 5 -> 8; matrix products, arithmetic and copies ran while one was open for 0% -> 1% of each run, Pallas kernels for 3% -> 3%
where the time goes in v6:
time: 165 us; the launch traced here: 163 us
  starting transfers between devices  45.9 us (28%)
  blocking collectives  45.7 us (28%)
  waiting for transfers between devices  38.1 us (23%)
  Pallas kernels  23.4 us (14%)
  other arithmetic  4.34 us (3%)
  local copies, waits for them, and re-layouts  4.3 us (3%)
    all_gather x1, blocking collectives, per_device(): whole = lax.all_gather(chunk, 'tm')  35.8 us
    all_to_all x1, starting transfers between devices, per_device(): chunk = jnp.sum(lax.all_to_all(chunks, 'tm', 0, 0), axis=0)  15.8 us
    all_to_all x1, waiting for transfers between devices, per_device(): parts = lax.all_to_all(parts, 'rec', 0, 0)  14.6 us
    all_to_all x1, waiting for transfers between devices, per_device(): chunk = jnp.sum(lax.all_to_all(chunks, 'tm', 0, 0), axis=0)  12.3 us
    all_to_all x1, blocking collectives, per_device(): lax.all_to_all(jnp.broadcast_to(stats[None], (blocks,) + stats.shape), 'q...  9.92 us
    pallas_call x1, Pallas kernels, per_device(): pl.pallas_call(lambda *refs: grad_kernel(half, *refs), out_shape=[jax.Sha...  9.5 us
    ppermute x3, starting transfers between devices, per_device(): lax.ppermute(tap_sum, 'rec', [(i, (i + k) % recs) for i in range(recs)])  9.21 us
    ppermute x3, starting transfers between devices, per_device(): lax.ppermute(sends[k], 'query', [(i, (i + 2 * k) % blocks) for i in range...  8.97 us
  transfers between devices with their start and end apart: 11, of which 8 were waited for; matrix products, arithmetic and copies ran while one was open for 1% of the time, Pallas kernels for 3%

profile of v6, /device:TPU:6, one launch (start us, length us, event | category | flops | bytes accessed | tf_op | source)
XLA Modules:
  0.0 163.3 jit_solution(7608421182088240431)
XLA Ops:
  0.6 0.0 copy-start
  0.6 1.2 copy-done
  1.9 0.0 copy-start.5
  1.9 0.7 copy-done.5
  2.5 0.0 copy-start.1
  2.5 0.0 copy-start.2
  2.5 0.1 shard_map.77
  2.6 4.0 %collective-permute-start = (f32[40,1024]{1,0:T(8,128)S(1)}, f32[40,1024]{1,0:T(8,128)S(1)}, u32[]{:S(2)}, u32[]{:S(2)}) collective-permute-start(f32[40,1024]{1,0:T(8,128)S(1)} %get-tuple-element.18), channel_id=1, source_target_pairs={{0,32},{32,64},{64,96},{96,128},{128,160},{160,192},{192,224},{224... | collective-permute-start | bytes 491528 | tf_op jit(solution)/shard_map/ppermute | solution.py:307
  6.6 1.3 collective-permute-start.1
  8.6 0.1 stack.43.refs_0_
  8.7 0.0 copy-done.1
  8.7 0.0 copy-done.2
  8.7 4.2 %shard_map.76 = f32[512,512]{1,0:T(8,128)S(1)} custom-call(s32[11]{0:T(128)S(1)} %stack.43.refs_0_, bf16[512,1024]{1,0:T(8,128)(2,1)S(1)} %bitcast.35, bf16[512,1024]{1,0:T(8,128)(2,1)S(1)} %copy-done.2), custom_call_target="tpu_custom_call" | custom-call | flops 1073741824 | bytes 3145728 | tf_op jit(solution)/shard_map/pallas_call | solution.py:310
  12.9 0.0 collective-permute-done.refs_2_
  13.0 1.4 collective-permute-done.1.refs_3_
  14.3 0.0 copy-done.4
  14.3 0.0 copy-done.6
  14.3 8.7 %shard_map.78 = (f32[128,8,512]{2,1,0:T(8,128)S(1)}, f32[96,8,512]{2,1,0:T(8,128)S(1)}, f32[2,8,128]{2,1,0:T(8,128)S(1)}, f32[8,128]{1,0:T(8,128)S(1)}) custom-call(s32[11]{0:T(128)S(1)} %stack.43.refs_0_, f32[64,8,512]{2,1,0:T(8,128)S(1)} %bitcast.37, f32[40,1024]{1,0:T(8,128)S(1)} %collective-permute-done.refs_2_, ...), custom_call_target="tpu_custom_call" | custom-call | flops 34603008 | bytes 6291456 | tf_op jit(solution)/shard_map/pallas_call | solution.py:325
  23.0 9.9 %all_to_all.15.refs_4_ = f32[8,2,8,128]{3,2,1,0:T(8,128)S(1)} all-to-all(f32[8,2,8,128]{3,2,1,0:T(8,128)S(1)} %broadcast_in_dim.4), channel_id=1, replica_groups=mesh['tm'=16,'query'=8,'rec'=4] {'query'}, dimensions={0} | all-to-all | bytes 131072 | tf_op jit(solution)/shard_map/all_to_all | solution.py:339
  32.9 9.5 %shard_map.79 = (f32[4,512,256]{2,1,0:T(8,128)S(1)}, f32[40,512]{1,0:T(8,128)S(1)}, f32[4,512,128]{2,1,0:T(8,128)S(1)}, f32[4,512,128]{2,1,0:T(8,128)S(1)}) custom-call(s32[11]{0:T(128)S(1)} %stack.43.refs_0_, f32[96,8,512]{2,1,0:T(8,128)S(1)} %get-tuple-element.20.refs_1_, f32[128,8,512]{2,1,0:T(8,128)S(1)} %get-tuple-element.21.refs_2_, ...), custom_call_target="tpu_custom_call" | custom-call | flops 571473920 | bytes 8388608 | tf_op jit(solution)/shard_map/pallas_call | solution.py:344
  42.4 0.0 copy-start.3
  42.4 1.3 copy-done.3
  43.8 1.0 copy-done.7
  44.7 4.8 %all-to-all-start.1 = ((f32[4,512,256]{2,1,0:T(8,128)}), f32[4,512,256]{2,1,0:T(8,128)S(1)}, u32[]{:S(2)}, u32[]{:S(2)}) async-start(f32[4,512,256]{2,1,0:T(8,128)} %copy-done.3), calls=%async_computation.1 | async-start | bytes 4194304 | tf_op jit(solution)/shard_map/all_to_all | solution.py:364
  49.5 1.9 %collective-permute-start.2 = (f32[4,512,128]{2,1,0:T(8,128)}, f32[4,512,128]{2,1,0:T(8,128)}, u32[]{:S(2)}, u32[]{:S(2)}) collective-permute-start(f32[4,512,128]{2,1,0:T(8,128)} %copy-done.7), channel_id=1, source_target_pairs={{0,4},{4,0},{8,12},{12,8},{16,20},{20,16},{24,28},{28,24},{1,5},{5... | collective-permute-start | bytes 3145736 | tf_op jit(solution)/shard_map/ppermute | solution.py:365
  51.4 2.8 %collective-permute-start.5 = (f32[40,512]{1,0:T(8,128)S(1)}, f32[40,512]{1,0:T(8,128)S(1)}, u32[]{:S(2)}, u32[]{:S(2)}) collective-permute-start(f32[40,512]{1,0:T(8,128)S(1)} %get-tuple-element.28.taps_own), channel_id=1, source_target_pairs={{0,3},{1,0},{2,1},{3,2},{4,7},{5,4},{6,5},{7,6},{8,11},{9,8},{10,9... | collective-permute-start | bytes 245768 | tf_op jit(solution)/shard_map/ppermute | solution.py:367
  54.2 4.3 %collective-permute-start.4 = (f32[40,512]{1,0:T(8,128)S(1)}, f32[40,512]{1,0:T(8,128)S(1)}, u32[]{:S(2)}, u32[]{:S(2)}) collective-permute-start(f32[40,512]{1,0:T(8,128)S(1)} %get-tuple-element.28.taps_own), channel_id=1, source_target_pairs={{0,1},{1,2},{2,3},{3,0},{4,5},{5,6},{6,7},{7,4},{8,9},{9,10},{10,1... | collective-permute-start | bytes 245768 | tf_op jit(solution)/shard_map/ppermute | solution.py:367
  58.5 2.2 %collective-permute-start.3 = (f32[40,512]{1,0:T(8,128)S(1)}, f32[40,512]{1,0:T(8,128)S(1)}, u32[]{:S(2)}, u32[]{:S(2)}) collective-permute-start(f32[40,512]{1,0:T(8,128)S(1)} %get-tuple-element.28.taps_own), channel_id=1, source_target_pairs={{0,2},{1,3},{2,0},{3,1},{4,6},{5,7},{6,4},{7,5},{8,10},{9,11},{10,... | collective-permute-start | bytes 245768 | tf_op jit(solution)/shard_map/ppermute | solution.py:367
  60.6 0.0 collective-permute-done.2
  60.6 14.6 %all-to-all-done.1.arrived = f32[4,512,256]{2,1,0:T(8,128)S(1)} async-done(((f32[4,512,256]{2,1,0:T(8,128)}), f32[4,512,256]{2,1,0:T(8,128)S(1)}, u32[]{:S(2)}, u32[]{:S(2)}) %all-to-all-start.1) | async-done | bytes 2097184 | tf_op jit(solution)/shard_map/all_to_all | solution.py:364
  75.3 0.0 collective-permute-done.5.taps_ahead
  75.3 0.4 collective-permute-done.4.taps_behind
  75.7 1.5 collective-permute-done.3.taps_far
  77.2 1.0 shard_map.80
  78.2 15.8 %all-to-all-start.2 = ((f32[16,40,256]{2,1,0:T(8,128)}), f32[16,40,256]{2,1,0:T(8,128)S(1)}, u32[]{:S(2)}, u32[]{:S(2)}) async-start(f32[16,40,256]{2,1,0:T(8,128)} %shard_map.80), calls=%async_computation.2 | async-start | bytes 1310720 | tf_op jit(solution)/shard_map/all_to_all | solution.py:379
  94.0 1.2 add_bitcast_fusion.2
  95.2 2.5 %collective-permute-start.6 = (f32[512,128]{1,0:T(8,128)S(1)}, f32[512,128]{1,0:T(8,128)S(1)}, u32[]{:S(2)}, u32[]{:S(2)}) collective-permute-start(f32[512,128]{1,0:T(8,128)S(1)} %get-tuple-element.33), channel_id=1, source_target_pairs={{0,8},{4,12},{8,16},{12,20},{16,24},{20,28},{24,0},{28,4},{1,9},{5... | collective-permute-start | bytes 786440 | tf_op jit(solution)/shard_map/ppermute | solution.py:383
  97.7 4.6 %collective-permute-start.8 = (f32[512,128]{1,0:T(8,128)S(1)}, f32[512,128]{1,0:T(8,128)S(1)}, u32[]{:S(2)}, u32[]{:S(2)}) collective-permute-start(f32[512,128]{1,0:T(8,128)S(1)} %get-tuple-element.34), channel_id=1, source_target_pairs={{0,24},{4,28},{8,0},{12,4},{16,8},{20,12},{24,16},{28,20},{1,25},{... | collective-permute-start | bytes 786440 | tf_op jit(solution)/shard_map/ppermute | solution.py:383
  102.2 1.9 %collective-permute-start.7 = (f32[512,128]{1,0:T(8,128)S(1)}, f32[512,128]{1,0:T(8,128)S(1)}, u32[]{:S(2)}, u32[]{:S(2)}) collective-permute-start(f32[512,128]{1,0:T(8,128)S(1)} %get-tuple-element.35), channel_id=1, source_target_pairs={{0,16},{4,20},{8,24},{12,28},{16,0},{20,4},{24,8},{28,12},{1,17},{... | collective-permute-start | bytes 786440 | tf_op jit(solution)/shard_map/ppermute | solution.py:383
  104.2 0.5 collective-permute-done.6
  104.6 6.6 %collective-permute-done.8 = f32[512,128]{1,0:T(8,128)S(1)} collective-permute-done((f32[512,128]{1,0:T(8,128)S(1)}, f32[512,128]{1,0:T(8,128)S(1)}, u32[]{:S(2)}, u32[]{:S(2)}) %collective-permute-start.8) | collective-permute-done | bytes 262176 | tf_op jit(solution)/shard_map/ppermute | solution.py:383
  111.3 0.7 collective-permute-done.7
  112.0 1.0 fusion.2
  113.1 12.3 %all-to-all-done.2 = f32[16,40,256]{2,1,0:T(8,128)S(1)} async-done(((f32[16,40,256]{2,1,0:T(8,128)}), f32[16,40,256]{2,1,0:T(8,128)S(1)}, u32[]{:S(2)}, u32[]{:S(2)}) %all-to-all-start.2) | async-done | bytes 655392 | tf_op jit(solution)/shard_map/all_to_all | solution.py:379
  125.4 35.8 %all-gather = f32[640,256]{1,0:T(8,128)S(1)} all-gather(f32[40,256]{1,0:T(8,128)S(1)} %reduce_sum.9), channel_id=2, replica_groups=mesh['tm'=16,'query'=8,'rec'=4] {'tm'}, dimensions={0}, use_global_device_ids=true | all-gather | bytes 696320 | tf_op jit(solution)/shard_map/all_gather | solution.py:385
  161.2 0.8 fusion
  162.0 0.7 fusion.3
  162.7 0.6 pad_maximum_fusion
  (7 shorter events, 0.1 us)
Async XLA Ops:
  0.6 1.2 copy-start
  1.9 0.7 copy-start.5
  2.5 6.2 %copy-start.1 = (bf16[1,512,1024]{2,1,0:T(8,128)(2,1)S(1)}, bf16[1,512,1024]{2,1,0:T(8,128)(2,1)}, u32[]{:S(2)}) copy-start(bf16[1,512,1024]{2,1,0:T(8,128)(2,1)} %param.5) | copy-start | bytes 3145732
  2.5 6.2 %copy-start.2 = (bf16[512,1024]{1,0:T(8,128)(2,1)S(1)}, bf16[512,1024]{1,0:T(8,128)(2,1)}, u32[]{:S(2)}) copy-start(bf16[512,1024]{1,0:T(8,128)(2,1)} %refs_7_.1) | copy-start | bytes 3145732
  2.6 11.7 %copy-start.4 = (f32[33,512]{1,0:T(8,128)S(1)}, f32[33,512]{1,0:T(8,128)}, u32[]{:S(2)}) copy-start(f32[33,512]{1,0:T(8,128)} %refs_8_.1) | copy-start | bytes 202756
  2.6 11.7 %copy-start.6 = (s32[1,512]{1,0:T(1,128)S(1)}, s32[1,512]{1,0:T(1,128)}, u32[]{:S(2)}) copy-start(s32[1,512]{1,0:T(1,128)} %refs_4_.1) | copy-start | bytes 6148
  2.6 10.3 %collective-permute-start = (f32[40,1024]{1,0:T(8,128)S(1)}, f32[40,1024]{1,0:T(8,128)S(1)}, u32[]{:S(2)}, u32[]{:S(2)}) collective-permute-start(f32[40,1024]{1,0:T(8,128)S(1)} %get-tuple-element.18), channel_id=1, source_target_pairs={{0,32},{32,64},{64,96},{96,128},{128,160},{160,192},{192,224},{224... | collective-permute-start | bytes 491528 | tf_op jit(solution)/shard_map/ppermute | solution.py:307
  6.6 7.7 %collective-permute-start.1 = (f32[40,1024]{1,0:T(8,128)S(1)}, f32[40,1024]{1,0:T(8,128)S(1)}, u32[]{:S(2)}, u32[]{:S(2)}) collective-permute-start(f32[40,1024]{1,0:T(8,128)S(1)} %get-tuple-element.19), channel_id=1, source_target_pairs={{32,0},{64,32},{96,64},{128,96},{160,128},{192,160},{224,192},{256... | collective-permute-start | bytes 491528 | tf_op jit(solution)/shard_map/ppermute | solution.py:308
  42.4 1.3 copy-start.3
  43.8 1.0 copy-start.7
  44.7 30.6 %all-to-all-start.1 = ((f32[4,512,256]{2,1,0:T(8,128)}), f32[4,512,256]{2,1,0:T(8,128)S(1)}, u32[]{:S(2)}, u32[]{:S(2)}) async-start(f32[4,512,256]{2,1,0:T(8,128)} %copy-done.3), calls=%async_computation.1 | async-start | bytes 4194304 | tf_op jit(solution)/shard_map/all_to_all | solution.py:364
  49.5 11.2 %collective-permute-start.2 = (f32[4,512,128]{2,1,0:T(8,128)}, f32[4,512,128]{2,1,0:T(8,128)}, u32[]{:S(2)}, u32[]{:S(2)}) collective-permute-start(f32[4,512,128]{2,1,0:T(8,128)} %copy-done.7), channel_id=1, source_target_pairs={{0,4},{4,0},{8,12},{12,8},{16,20},{20,16},{24,28},{28,24},{1,5},{5... | collective-permute-start | bytes 3145736 | tf_op jit(solution)/shard_map/ppermute | solution.py:365
  51.4 23.9 %collective-permute-start.5 = (f32[40,512]{1,0:T(8,128)S(1)}, f32[40,512]{1,0:T(8,128)S(1)}, u32[]{:S(2)}, u32[]{:S(2)}) collective-permute-start(f32[40,512]{1,0:T(8,128)S(1)} %get-tuple-element.28.taps_own), channel_id=1, source_target_pairs={{0,3},{1,0},{2,1},{3,2},{4,7},{5,4},{6,5},{7,6},{8,11},{9,8},{10,9... | collective-permute-start | bytes 245768 | tf_op jit(solution)/shard_map/ppermute | solution.py:367
  54.2 21.5 %collective-permute-start.4 = (f32[40,512]{1,0:T(8,128)S(1)}, f32[40,512]{1,0:T(8,128)S(1)}, u32[]{:S(2)}, u32[]{:S(2)}) collective-permute-start(f32[40,512]{1,0:T(8,128)S(1)} %get-tuple-element.28.taps_own), channel_id=1, source_target_pairs={{0,1},{1,2},{2,3},{3,0},{4,5},{5,6},{6,7},{7,4},{8,9},{9,10},{10,1... | collective-permute-start | bytes 245768 | tf_op jit(solution)/shard_map/ppermute | solution.py:367
  58.5 18.7 %collective-permute-start.3 = (f32[40,512]{1,0:T(8,128)S(1)}, f32[40,512]{1,0:T(8,128)S(1)}, u32[]{:S(2)}, u32[]{:S(2)}) collective-permute-start(f32[40,512]{1,0:T(8,128)S(1)} %get-tuple-element.28.taps_own), channel_id=1, source_target_pairs={{0,2},{1,3},{2,0},{3,1},{4,6},{5,7},{6,4},{7,5},{8,10},{9,11},{10,... | collective-permute-start | bytes 245768 | tf_op jit(solution)/shard_map/ppermute | solution.py:367
  78.2 47.2 %all-to-all-start.2 = ((f32[16,40,256]{2,1,0:T(8,128)}), f32[16,40,256]{2,1,0:T(8,128)S(1)}, u32[]{:S(2)}, u32[]{:S(2)}) async-start(f32[16,40,256]{2,1,0:T(8,128)} %shard_map.80), calls=%async_computation.2 | async-start | bytes 1310720 | tf_op jit(solution)/shard_map/all_to_all | solution.py:379
  95.2 9.5 %collective-permute-start.6 = (f32[512,128]{1,0:T(8,128)S(1)}, f32[512,128]{1,0:T(8,128)S(1)}, u32[]{:S(2)}, u32[]{:S(2)}) collective-permute-start(f32[512,128]{1,0:T(8,128)S(1)} %get-tuple-element.33), channel_id=1, source_target_pairs={{0,8},{4,12},{8,16},{12,20},{16,24},{20,28},{24,0},{28,4},{1,9},{5... | collective-permute-start | bytes 786440 | tf_op jit(solution)/shard_map/ppermute | solution.py:383
  97.7 13.6 %collective-permute-start.8 = (f32[512,128]{1,0:T(8,128)S(1)}, f32[512,128]{1,0:T(8,128)S(1)}, u32[]{:S(2)}, u32[]{:S(2)}) collective-permute-start(f32[512,128]{1,0:T(8,128)S(1)} %get-tuple-element.34), channel_id=1, source_target_pairs={{0,24},{4,28},{8,0},{12,4},{16,8},{20,12},{24,16},{28,20},{1,25},{... | collective-permute-start | bytes 786440 | tf_op jit(solution)/shard_map/ppermute | solution.py:383
  102.2 9.8 %collective-permute-start.7 = (f32[512,128]{1,0:T(8,128)S(1)}, f32[512,128]{1,0:T(8,128)S(1)}, u32[]{:S(2)}, u32[]{:S(2)}) collective-permute-start(f32[512,128]{1,0:T(8,128)S(1)} %get-tuple-element.35), channel_id=1, source_target_pairs={{0,16},{4,20},{8,24},{12,28},{16,0},{20,4},{24,8},{28,12},{1,17},{... | collective-permute-start | bytes 786440 | tf_op jit(solution)/shard_map/ppermute | solution.py:383

commit v7 on v6

--- a/solution.py
+++ b/solution.py
@@ -110,7 +110,7 @@
 
 
 def smooth_kernel(
-    scale, half, scalars, main, before, after, labels, queries, taps, scores, powers, stats, tile, wide
+    scale, half, scalars, main, before, after, labels, queries, taps, scores_out, powers, stats, tile, wide, scores, sem
 ):
     blk = main.shape[0]
     count = 2 * half + 1
@@ -131,6 +131,8 @@
         scores[t] = jnp.where(sub == 0, rim_scores[t : t + 1, :], low)
         high = pltpu.roll(main[t], SUB - 1, 0)
         scores[rim + blk + t] = jnp.where(sub == SUB - 1, rim_scores[rim + t : rim + t + 1, :], high)
+    copy = pltpu.make_async_copy(scores, scores_out, sem)
+    copy.start()
     lane = lax.broadcasted_iota(jnp.int32, (SUB, LANES), 1)
 
     def step(b, carry):
@@ -161,17 +163,20 @@
     tops, totals = lax.fori_loop(0, (blk + rim) // UNIT, step, (zero, zero))
     stats[0] = tops
     stats[1] = totals
+    copy.wait()
 
 
 def grad_kernel(
-    half, scalars, powers, scores, mine, others, labels, frames, queries, taps,
-    chunks, tap_sums, keep_frames, cross_frames, wide, grads, tap_grads, placed, frame_part,
+    half, scalars, powers, scores_in, mine, others, labels, frames, queries, taps,
+    chunks_out, tap_sums, keep_frames, cross_out, wide, grads, tap_grads, placed, frame_part, chunks, cross_frames, scores, sems,
 ):
     blk = powers.shape[0] - 2 * half
     rows = blk * SUB
     count = 2 * half + 1
     query_count = taps.shape[1]
     groups = query_count // LANES
+    fetch = pltpu.make_async_copy(scores_in, scores, sems.at[sems.shape[0] - 1])
+    fetch.start()
     broadcast_taps(taps, wide, count)
     tops = others[:, 0]
     top = jnp.max(tops, axis=0)
@@ -209,7 +214,24 @@
         return 0
 
     lax.fori_loop(0, blk // UNIT, spread, 0)
+    natural = jnp.dot(placement(rows, blk, True), placed[...], preferred_element_type=F32)
+    turned = natural.T.astype(jnp.bfloat16)
+    natural = natural.astype(jnp.bfloat16)
+    recs, part_rows, part_width = chunks.shape
+    copies = []
+    for r in range(recs):
+        chunks[r] = jnp.dot(turned, frames[:, r * part_width : (r + 1) * part_width], preferred_element_type=F32)
+        copies.append(pltpu.make_async_copy(chunks.at[r], chunks_out.at[r], sems.at[r]))
+        copies[r].start()
+    frame_part[...] = jnp.dot(natural, queries[...], preferred_element_type=F32)
+    chips, _, out_width = keep_frames.shape
+    for k in range(chips):
+        keep_frames[k] = column_block(frame_part, scalars[3 + k], out_width)
+        cross_frames[k] = column_block(frame_part, scalars[3 + chips + k], out_width)
+    copies.append(pltpu.make_async_copy(cross_frames, cross_out, sems.at[recs]))
+    copies[recs].start()
     tap_grads[...] = jnp.zeros_like(tap_grads)
+    fetch.wait()
 
     def correlate(b, _):
         first = half + b * UNIT
@@ -227,17 +249,8 @@
     lax.fori_loop(0, blk // UNIT, correlate, 0)
     tap_sums[:count, :] = jnp.sum(tap_grads[...], axis=1)
     tap_sums[count:, :] = jnp.zeros((tap_sums.shape[0] - count, query_count), F32)
-    natural = jnp.dot(placement(rows, blk, True), placed[...], preferred_element_type=F32)
-    turned = natural.T.astype(jnp.bfloat16)
-    natural = natural.astype(jnp.bfloat16)
-    recs, part_rows, part_width = chunks.shape
-    for r in range(recs):
-        chunks[r] = jnp.dot(turned, frames[:, r * part_width : (r + 1) * part_width], preferred_element_type=F32)
-    frame_part[...] = jnp.dot(natural, queries[...], preferred_element_type=F32)
-    chips, _, out_width = keep_frames.shape
-    for k in range(chips):
-        keep_frames[k] = column_block(frame_part, scalars[3 + k], out_width)
-        cross_frames[k] = column_block(frame_part, scalars[3 + chips + k], out_width)
+    for copy in copies:
+        copy.wait()
 
 
 def column_block(frames, index, width):
@@ -262,6 +275,23 @@
             chunks[z, chunk_rows:, :] = block
         else:
             chunks[z, chunk_rows:, :] = jnp.zeros((UNIT, part_width), F32)
+
+
+def last_kernel(scale, whole, grad_queries, tap_sums):
+    tms = whole.shape[0]
+    query_count, part_width = grad_queries.shape
+    count = tap_sums.shape[0]
+    chunk_rows = query_count // tms
+    blocks = padded_rows_of(count) // UNIT
+    for z in range(tms):
+        block = whole[z, :chunk_rows, :] * scale
+        grad_queries[z * chunk_rows : (z + 1) * chunk_rows, :] = block.astype(jnp.bfloat16)
+    for h in range(query_count // part_width):
+        for t in range(blocks):
+            used = min(UNIT, count - t * UNIT)
+            tap_sums[t * UNIT : t * UNIT + used, h * part_width : (h + 1) * part_width] = whole[
+                h * blocks + t, chunk_rows : chunk_rows + used, :
+            ]
 
 
 def padded_rows_of(count):
@@ -287,6 +317,7 @@
         [lax.axis_index("tm") * rows, lengths[0], query_index * query_count] + keep_ids + cross_ids
     ).astype(jnp.int32)
     smem = pl.BlockSpec(memory_space=pltpu.SMEM)
+    hbm = pl.BlockSpec(memory_space=pltpu.HBM)
 
     edge = jax.ShapeDtypeStruct((rim + UNIT, width), F32)
     last, first = pl.pallas_call(
@@ -331,9 +362,13 @@
             jax.ShapeDtypeStruct((SUB, LANES), F32),
         ],
         in_specs=[smem] + whole_spec(6),
-        out_specs=whole_spec(4),
-        scratch_shapes=[VMEM((count, SUB, query_count), F32)],
-        compiler_params=params(12),
+        out_specs=[hbm] + whole_spec(3),
+        scratch_shapes=[
+            VMEM((count, SUB, query_count), F32),
+            VMEM((blk + 2 * rim, SUB, query_count), F32),
+            pltpu.SemaphoreType.DMA(()),
+        ],
+        compiler_params=params(50),
         cost_estimate=cost(4 * rows * query_count * count, 6 << 20),
     )(scalars, main, before, after, labels, queries, kernel)
     others = lax.all_to_all(jnp.broadcast_to(stats[None], (blocks,) + stats.shape), "query", 0, 0)
@@ -349,16 +384,20 @@
             terms,
             terms,
         ],
-        in_specs=[smem] + whole_spec(8),
-        out_specs=whole_spec(4),
+        in_specs=[smem] + whole_spec(1) + [hbm] + whole_spec(6),
+        out_specs=[hbm] + whole_spec(2) + [hbm],
         scratch_shapes=[
             VMEM((count, SUB, query_count), F32),
             VMEM((blk + rim, SUB, query_count), F32),
             VMEM((count, SUB, query_count), F32),
             VMEM((rows, query_count), jnp.bfloat16),
             VMEM((rows, width), F32),
-        ],
-        compiler_params=params(20),
+            VMEM((recs, query_count, part_width), F32),
+            VMEM(terms.shape, F32),
+            VMEM(scores.shape, F32),
+            pltpu.SemaphoreType.DMA((recs + 2,)),
+        ],
+        compiler_params=params(48),
         cost_estimate=cost(2 * rows * query_count * (width + 2 * count), 8 << 20),
     )(scalars, powers, scores, stats, others, tile, frame_rows, queries, kernel)
     parts = lax.all_to_all(parts, "rec", 0, 0)
@@ -381,15 +420,20 @@
     frame_sum = sends[0]
     for k in range(1, chips):
         frame_sum = frame_sum + lax.ppermute(sends[k], "query", [(i, (i + 2 * k) % blocks) for i in range(blocks)])
-    chunk, frame_sum = lax.optimization_barrier((chunk, frame_sum))
+    grad_frames = (frame_sum * scale).astype(jnp.bfloat16)[None]
+    chunk, grad_frames = lax.optimization_barrier((chunk, grad_frames))
     whole = lax.all_gather(chunk, "tm")
-    query_sum = whole[:, :chunk_rows].reshape(query_count, part_width)
-    halves = query_count // part_width
-    tall = padded_rows_of(count)
-    tap_sum = whole[: halves * tall // UNIT, chunk_rows:].reshape(halves, tall, part_width)
-    tap_sum = jnp.concatenate([tap_sum[h, :count] for h in range(halves)], axis=1)
-    grad_frames = (frame_sum * scale).astype(jnp.bfloat16)[None]
-    grad_queries = (query_sum * scale).astype(jnp.bfloat16)
+    grad_queries, tap_sum = pl.pallas_call(
+        lambda *refs: last_kernel(scale, *refs),
+        out_shape=[
+            jax.ShapeDtypeStruct((query_count, part_width), jnp.bfloat16),
+            jax.ShapeDtypeStruct((count, query_count), F32),
+        ],
+        in_specs=whole_spec(1),
+        out_specs=whole_spec(2),
+        compiler_params=params(8),
+        cost_estimate=cost(query_count * part_width, 1 << 20),
+    )(whole)
     return (grad_frames, grad_queries, tap_sum)
 
 

time: 165 us -> 163 us (0.988)
    unnamed x16 -> x14, local copies, waits for them, and re-layouts: 4.19 us -> 2.88 us
  transfers between devices with their start and end apart: 11 -> 11, of which waited for: 8 -> 8; matrix products, arithmetic and copies ran while one was open for 1% -> 2% of each run, Pallas kernels for 3% -> 3%
where the time goes in v7:
time: 163 us; the launch traced here: 161 us
  starting transfers between devices  46 us (28%)
  blocking collectives  45.7 us (28%)
  waiting for transfers between devices  37.3 us (23%)
  Pallas kernels  24.9 us (15%)
  local copies, waits for them, and re-layouts  2.97 us (2%)
  other arithmetic  2.93 us (2%)
    all_gather x1, blocking collectives, per_device(): whole = lax.all_gather(chunk, 'tm')  35.8 us
    all_to_all x1, starting transfers between devices, per_device(): chunk = jnp.sum(lax.all_to_all(chunks, 'tm', 0, 0), axis=0)  15.9 us
    all_to_all x1, waiting for transfers between devices, per_device(): parts = lax.all_to_all(parts, 'rec', 0, 0)  14.6 us
    all_to_all x1, waiting for transfers between devices, per_device(): chunk = jnp.sum(lax.all_to_all(chunks, 'tm', 0, 0), axis=0)  11.7 us
    all_to_all x1, blocking collectives, per_device(): lax.all_to_all(jnp.broadcast_to(stats[None], (blocks,) + stats.shape), 'q...  9.89 us
    pallas_call x1, Pallas kernels, per_device(): pl.pallas_call(lambda *refs: grad_kernel(half, *refs), out_shape=[jax.Sha...  9.81 us
    ppermute x3, starting transfers between devices, per_device(): lax.ppermute(tap_sum, 'rec', [(i, (i + k) % recs) for i in range(recs)])  9.21 us
    pallas_call x1, Pallas kernels, per_device(): pl.pallas_call(lambda *refs: smooth_kernel(scale, half, *refs), out_shape...  8.98 us
  transfers between devices with their start and end apart: 11, of which 8 were waited for; matrix products, arithmetic and copies ran while one was open for 2% of the time, Pallas kernels for 3%

profile of v7, /device:TPU:6, one launch (start us, length us, event | category | flops | bytes accessed | tf_op | source)
XLA Modules:
  0.0 161.4 jit_solution(762039356721479659)
XLA Ops:
  0.6 0.0 copy-start
  0.6 1.2 copy-done
  1.9 0.0 copy-start.4
  1.9 0.7 copy-done.4
  2.5 0.0 copy-start.1
  2.5 0.0 copy-start.2
  2.5 0.1 shard_map.77
  2.6 0.0 copy-start.3
  2.6 0.0 copy-start.5
  2.6 4.0 %collective-permute-start = (f32[40,1024]{1,0:T(8,128)S(1)}, f32[40,1024]{1,0:T(8,128)S(1)}, u32[]{:S(2)}, u32[]{:S(2)}) collective-permute-start(f32[40,1024]{1,0:T(8,128)S(1)} %get-tuple-element.20), channel_id=1, source_target_pairs={{0,32},{32,64},{64,96},{96,128},{128,160},{160,192},{192,224},{224... | collective-permute-start | bytes 491528 | tf_op jit(solution)/shard_map/ppermute | solution.py:338
  6.6 1.3 collective-permute-start.1
  8.6 0.1 stack.43.refs_0_
  8.7 0.0 copy-done.1
  8.7 0.0 copy-done.2
  8.7 4.3 %shard_map.76 = f32[512,512]{1,0:T(8,128)S(1)} custom-call(s32[11]{0:T(128)S(1)} %stack.43.refs_0_, bf16[512,1024]{1,0:T(8,128)(2,1)S(1)} %bitcast.35, bf16[512,1024]{1,0:T(8,128)(2,1)S(1)} %copy-done.2), custom_call_target="tpu_custom_call" | custom-call | flops 1073741824 | bytes 3145728 | tf_op jit(solution)/shard_map/pallas_call | solution.py:341
  13.1 0.0 collective-permute-done.refs_2_
  13.1 1.2 collective-permute-done.1.refs_3_
  14.3 0.0 copy-done.3
  14.3 0.0 copy-done.5
  14.3 9.0 %shard_map.78 = (f32[128,8,512]{2,1,0:T(8,128)}, f32[96,8,512]{2,1,0:T(8,128)S(1)}, f32[2,8,128]{2,1,0:T(8,128)S(1)}, f32[8,128]{1,0:T(8,128)S(1)}) custom-call(s32[11]{0:T(128)S(1)} %stack.43.refs_0_, f32[64,8,512]{2,1,0:T(8,128)S(1)} %bitcast.38, f32[40,1024]{1,0:T(8,128)S(1)} %collective-permute-done.refs_2_, ...), custom_call_target="tpu_custom_call" | custom-call | flops 34603008 | bytes 6291456 | tf_op jit(solution)/shard_map/pallas_call | solution.py:356
  23.3 9.9 %all_to_all.15.refs_4_ = f32[8,2,8,128]{3,2,1,0:T(8,128)S(1)} all-to-all(f32[8,2,8,128]{3,2,1,0:T(8,128)S(1)} %broadcast_in_dim.4), channel_id=1, replica_groups=mesh['tm'=16,'query'=8,'rec'=4] {'query'}, dimensions={0} | all-to-all | bytes 131072 | tf_op jit(solution)/shard_map/all_to_all | solution.py:374
  33.2 9.8 %shard_map.79 = (f32[4,512,256]{2,1,0:T(8,128)}, f32[40,512]{1,0:T(8,128)S(1)}, f32[4,512,128]{2,1,0:T(8,128)S(1)}, f32[4,512,128]{2,1,0:T(8,128)S(1)}) custom-call(s32[11]{0:T(128)S(1)} %stack.43.refs_0_, f32[96,8,512]{2,1,0:T(8,128)S(1)} %get-tuple-element.22.refs_1_, f32[128,8,512]{2,1,0:T(8,128)} %get-tuple-element.23.refs_2_, ...), custom_call_target="tpu_custom_call" | custom-call | flops 571473920 | bytes 8388608 | tf_op jit(solution)/shard_map/pallas_call | solution.py:379
  43.0 0.0 copy-start.6
  43.0 1.0 copy-done.6
  44.0 4.8 %all-to-all-start.1 = ((f32[4,512,256]{2,1,0:T(8,128)}), f32[4,512,256]{2,1,0:T(8,128)S(1)}, u32[]{:S(2)}, u32[]{:S(2)}) async-start(f32[4,512,256]{2,1,0:T(8,128)} %get-tuple-element.26), calls=%async_computation.1 | async-start | bytes 4194304 | tf_op jit(solution)/shard_map/all_to_all | solution.py:403
  48.8 1.9 %collective-permute-start.2 = (f32[4,512,128]{2,1,0:T(8,128)}, f32[4,512,128]{2,1,0:T(8,128)}, u32[]{:S(2)}, u32[]{:S(2)}) collective-permute-start(f32[4,512,128]{2,1,0:T(8,128)} %copy-done.6), channel_id=1, source_target_pairs={{0,4},{4,0},{8,12},{12,8},{16,20},{20,16},{24,28},{28,24},{1,5},{5... | collective-permute-start | bytes 3145736 | tf_op jit(solution)/shard_map/ppermute | solution.py:404
  50.7 2.8 %collective-permute-start.5 = (f32[40,512]{1,0:T(8,128)S(1)}, f32[40,512]{1,0:T(8,128)S(1)}, u32[]{:S(2)}, u32[]{:S(2)}) collective-permute-start(f32[40,512]{1,0:T(8,128)S(1)} %get-tuple-element.30.taps_own), channel_id=1, source_target_pairs={{0,3},{1,0},{2,1},{3,2},{4,7},{5,4},{6,5},{7,6},{8,11},{9,8},{10,9... | collective-permute-start | bytes 245768 | tf_op jit(solution)/shard_map/ppermute | solution.py:406
  53.5 4.3 %collective-permute-start.4 = (f32[40,512]{1,0:T(8,128)S(1)}, f32[40,512]{1,0:T(8,128)S(1)}, u32[]{:S(2)}, u32[]{:S(2)}) collective-permute-start(f32[40,512]{1,0:T(8,128)S(1)} %get-tuple-element.30.taps_own), channel_id=1, source_target_pairs={{0,1},{1,2},{2,3},{3,0},{4,5},{5,6},{6,7},{7,4},{8,9},{9,10},{10,1... | collective-permute-start | bytes 245768 | tf_op jit(solution)/shard_map/ppermute | solution.py:406
  57.8 2.2 %collective-permute-start.3 = (f32[40,512]{1,0:T(8,128)S(1)}, f32[40,512]{1,0:T(8,128)S(1)}, u32[]{:S(2)}, u32[]{:S(2)}) collective-permute-start(f32[40,512]{1,0:T(8,128)S(1)} %get-tuple-element.30.taps_own), channel_id=1, source_target_pairs={{0,2},{1,3},{2,0},{3,1},{4,6},{5,7},{6,4},{7,5},{8,10},{9,11},{10,... | collective-permute-start | bytes 245768 | tf_op jit(solution)/shard_map/ppermute | solution.py:406
  59.9 0.0 collective-permute-done.2
  59.9 14.6 %all-to-all-done.1.arrived = f32[4,512,256]{2,1,0:T(8,128)S(1)} async-done(((f32[4,512,256]{2,1,0:T(8,128)}), f32[4,512,256]{2,1,0:T(8,128)S(1)}, u32[]{:S(2)}, u32[]{:S(2)}) %all-to-all-start.1) | async-done | bytes 2097184 | tf_op jit(solution)/shard_map/all_to_all | solution.py:403
  74.6 0.0 collective-permute-done.5.taps_ahead
  74.6 0.4 collective-permute-done.4.taps_behind
  75.0 1.5 collective-permute-done.3.taps_far
  76.5 1.0 shard_map.80
  77.5 15.9 %all-to-all-start.2 = ((f32[16,40,256]{2,1,0:T(8,128)}), f32[16,40,256]{2,1,0:T(8,128)S(1)}, u32[]{:S(2)}, u32[]{:S(2)}) async-start(f32[16,40,256]{2,1,0:T(8,128)} %shard_map.80), calls=%async_computation.2 | async-start | bytes 1310720 | tf_op jit(solution)/shard_map/all_to_all | solution.py:418
  93.4 1.2 add_bitcast_fusion.2
  94.6 2.5 %collective-permute-start.6 = (f32[512,128]{1,0:T(8,128)S(1)}, f32[512,128]{1,0:T(8,128)S(1)}, u32[]{:S(2)}, u32[]{:S(2)}) collective-permute-start(f32[512,128]{1,0:T(8,128)S(1)} %get-tuple-element.37), channel_id=1, source_target_pairs={{0,8},{4,12},{8,16},{12,20},{16,24},{20,28},{24,0},{28,4},{1,9},{5... | collective-permute-start | bytes 786440 | tf_op jit(solution)/shard_map/ppermute | solution.py:422
  97.1 4.6 %collective-permute-start.8 = (f32[512,128]{1,0:T(8,128)S(1)}, f32[512,128]{1,0:T(8,128)S(1)}, u32[]{:S(2)}, u32[]{:S(2)}) collective-permute-start(f32[512,128]{1,0:T(8,128)S(1)} %get-tuple-element.38), channel_id=1, source_target_pairs={{0,24},{4,28},{8,0},{12,4},{16,8},{20,12},{24,16},{28,20},{1,25},{... | collective-permute-start | bytes 786440 | tf_op jit(solution)/shard_map/ppermute | solution.py:422
  101.7 1.9 %collective-permute-start.7 = (f32[512,128]{1,0:T(8,128)S(1)}, f32[512,128]{1,0:T(8,128)S(1)}, u32[]{:S(2)}, u32[]{:S(2)}) collective-permute-start(f32[512,128]{1,0:T(8,128)S(1)} %get-tuple-element.39), channel_id=1, source_target_pairs={{0,16},{4,20},{8,24},{12,28},{16,0},{20,4},{24,8},{28,12},{1,17},{... | collective-permute-start | bytes 786440 | tf_op jit(solution)/shard_map/ppermute | solution.py:422
  103.6 0.5 collective-permute-done.6
  104.1 6.6 %collective-permute-done.8 = f32[512,128]{1,0:T(8,128)S(1)} collective-permute-done((f32[512,128]{1,0:T(8,128)S(1)}, f32[512,128]{1,0:T(8,128)S(1)}, u32[]{:S(2)}, u32[]{:S(2)}) %collective-permute-start.8) | collective-permute-done | bytes 262176 | tf_op jit(solution)/shard_map/ppermute | solution.py:422
  110.7 0.7 collective-permute-done.7
  111.4 1.7 %fusion.4 = bf16[1,512,128]{2,1,0:T(8,128)(2,1)} fusion(f32[512,128]{1,0:T(8,128)S(1)} %collective-permute-done.8, f32[512,128]{1,0:T(8,128)S(1)} %collective-permute-done.7, f32[512,128]{1,0:T(8,128)S(1)} %collective-permute-done.6, f32[4,512,128]{2,1,0:T(8,128)} %collective-permute-done.2, f32[4,512,128]{2,1,0:T(8,128)S(1)} %get-tuple-element.31), kind=kLoop, calls=%fused_computation.8 | loop fusion | flops 393216 | bytes 1441792 | tf_op jit(solution)/shard_map/broadcast_in_dim | solution.py:423
  113.1 11.7 %all-to-all-done.2 = f32[16,40,256]{2,1,0:T(8,128)S(1)} async-done(((f32[16,40,256]{2,1,0:T(8,128)}), f32[16,40,256]{2,1,0:T(8,128)S(1)}, u32[]{:S(2)}, u32[]{:S(2)}) %all-to-all-start.2) | async-done | bytes 655392 | tf_op jit(solution)/shard_map/all_to_all | solution.py:418
  124.8 35.8 %all-gather = f32[640,256]{1,0:T(8,128)S(1)} all-gather(f32[40,256]{1,0:T(8,128)S(1)} %reduce_sum.9), channel_id=2, replica_groups=mesh['tm'=16,'query'=8,'rec'=4] {'tm'}, dimensions={0}, use_global_device_ids=true | all-gather | bytes 696320 | tf_op jit(solution)/shard_map/all_gather | solution.py:425
  160.6 0.8 shard_map.81
  (2 shorter events, 0.0 us)
Async XLA Ops:
  0.6 1.2 copy-start
  1.9 0.7 copy-start.4
  2.5 6.2 %copy-start.1 = (bf16[1,512,1024]{2,1,0:T(8,128)(2,1)S(1)}, bf16[1,512,1024]{2,1,0:T(8,128)(2,1)}, u32[]{:S(2)}) copy-start(bf16[1,512,1024]{2,1,0:T(8,128)(2,1)} %param.5) | copy-start | bytes 3145732
  2.5 6.2 %copy-start.2 = (bf16[512,1024]{1,0:T(8,128)(2,1)S(1)}, bf16[512,1024]{1,0:T(8,128)(2,1)}, u32[]{:S(2)}) copy-start(bf16[512,1024]{1,0:T(8,128)(2,1)} %refs_7_.1) | copy-start | bytes 3145732
  2.6 11.7 %copy-start.3 = (f32[33,512]{1,0:T(8,128)S(1)}, f32[33,512]{1,0:T(8,128)}, u32[]{:S(2)}) copy-start(f32[33,512]{1,0:T(8,128)} %refs_8_.1) | copy-start | bytes 202756
  2.6 11.7 %copy-start.5 = (s32[1,512]{1,0:T(1,128)S(1)}, s32[1,512]{1,0:T(1,128)}, u32[]{:S(2)}) copy-start(s32[1,512]{1,0:T(1,128)} %refs_4_.1) | copy-start | bytes 6148
  2.6 10.4 %collective-permute-start = (f32[40,1024]{1,0:T(8,128)S(1)}, f32[40,1024]{1,0:T(8,128)S(1)}, u32[]{:S(2)}, u32[]{:S(2)}) collective-permute-start(f32[40,1024]{1,0:T(8,128)S(1)} %get-tuple-element.20), channel_id=1, source_target_pairs={{0,32},{32,64},{64,96},{96,128},{128,160},{160,192},{192,224},{224... | collective-permute-start | bytes 491528 | tf_op jit(solution)/shard_map/ppermute | solution.py:338
  6.6 7.7 %collective-permute-start.1 = (f32[40,1024]{1,0:T(8,128)S(1)}, f32[40,1024]{1,0:T(8,128)S(1)}, u32[]{:S(2)}, u32[]{:S(2)}) collective-permute-start(f32[40,1024]{1,0:T(8,128)S(1)} %get-tuple-element.21), channel_id=1, source_target_pairs={{32,0},{64,32},{96,64},{128,96},{160,128},{192,160},{224,192},{256... | collective-permute-start | bytes 491528 | tf_op jit(solution)/shard_map/ppermute | solution.py:339
  43.0 1.0 copy-start.6
  44.0 30.6 %all-to-all-start.1 = ((f32[4,512,256]{2,1,0:T(8,128)}), f32[4,512,256]{2,1,0:T(8,128)S(1)}, u32[]{:S(2)}, u32[]{:S(2)}) async-start(f32[4,512,256]{2,1,0:T(8,128)} %get-tuple-element.26), calls=%async_computation.1 | async-start | bytes 4194304 | tf_op jit(solution)/shard_map/all_to_all | solution.py:403
  48.8 11.2 %collective-permute-start.2 = (f32[4,512,128]{2,1,0:T(8,128)}, f32[4,512,128]{2,1,0:T(8,128)}, u32[]{:S(2)}, u32[]{:S(2)}) collective-permute-start(f32[4,512,128]{2,1,0:T(8,128)} %copy-done.6), channel_id=1, source_target_pairs={{0,4},{4,0},{8,12},{12,8},{16,20},{20,16},{24,28},{28,24},{1,5},{5... | collective-permute-start | bytes 3145736 | tf_op jit(solution)/shard_map/ppermute | solution.py:404
  50.7 23.9 %collective-permute-start.5 = (f32[40,512]{1,0:T(8,128)S(1)}, f32[40,512]{1,0:T(8,128)S(1)}, u32[]{:S(2)}, u32[]{:S(2)}) collective-permute-start(f32[40,512]{1,0:T(8,128)S(1)} %get-tuple-element.30.taps_own), channel_id=1, source_target_pairs={{0,3},{1,0},{2,1},{3,2},{4,7},{5,4},{6,5},{7,6},{8,11},{9,8},{10,9... | collective-permute-start | bytes 245768 | tf_op jit(solution)/shard_map/ppermute | solution.py:406
  53.5 21.6 %collective-permute-start.4 = (f32[40,512]{1,0:T(8,128)S(1)}, f32[40,512]{1,0:T(8,128)S(1)}, u32[]{:S(2)}, u32[]{:S(2)}) collective-permute-start(f32[40,512]{1,0:T(8,128)S(1)} %get-tuple-element.30.taps_own), channel_id=1, source_target_pairs={{0,1},{1,2},{2,3},{3,0},{4,5},{5,6},{6,7},{7,4},{8,9},{9,10},{10,1... | collective-permute-start | bytes 245768 | tf_op jit(solution)/shard_map/ppermute | solution.py:406
  57.8 18.7 %collective-permute-start.3 = (f32[40,512]{1,0:T(8,128)S(1)}, f32[40,512]{1,0:T(8,128)S(1)}, u32[]{:S(2)}, u32[]{:S(2)}) collective-permute-start(f32[40,512]{1,0:T(8,128)S(1)} %get-tuple-element.30.taps_own), channel_id=1, source_target_pairs={{0,2},{1,3},{2,0},{3,1},{4,6},{5,7},{6,4},{7,5},{8,10},{9,11},{10,... | collective-permute-start | bytes 245768 | tf_op jit(solution)/shard_map/ppermute | solution.py:406
  77.5 47.3 %all-to-all-start.2 = ((f32[16,40,256]{2,1,0:T(8,128)}), f32[16,40,256]{2,1,0:T(8,128)S(1)}, u32[]{:S(2)}, u32[]{:S(2)}) async-start(f32[16,40,256]{2,1,0:T(8,128)} %shard_map.80), calls=%async_computation.2 | async-start | bytes 1310720 | tf_op jit(solution)/shard_map/all_to_all | solution.py:418
  94.6 9.5 %collective-permute-start.6 = (f32[512,128]{1,0:T(8,128)S(1)}, f32[512,128]{1,0:T(8,128)S(1)}, u32[]{:S(2)}, u32[]{:S(2)}) collective-permute-start(f32[512,128]{1,0:T(8,128)S(1)} %get-tuple-element.37), channel_id=1, source_target_pairs={{0,8},{4,12},{8,16},{12,20},{16,24},{20,28},{24,0},{28,4},{1,9},{5... | collective-permute-start | bytes 786440 | tf_op jit(solution)/shard_map/ppermute | solution.py:422
  97.1 13.6 %collective-permute-start.8 = (f32[512,128]{1,0:T(8,128)S(1)}, f32[512,128]{1,0:T(8,128)S(1)}, u32[]{:S(2)}, u32[]{:S(2)}) collective-permute-start(f32[512,128]{1,0:T(8,128)S(1)} %get-tuple-element.38), channel_id=1, source_target_pairs={{0,24},{4,28},{8,0},{12,4},{16,8},{20,12},{24,16},{28,20},{1,25},{... | collective-permute-start | bytes 786440 | tf_op jit(solution)/shard_map/ppermute | solution.py:422
  101.7 9.8 %collective-permute-start.7 = (f32[512,128]{1,0:T(8,128)S(1)}, f32[512,128]{1,0:T(8,128)S(1)}, u32[]{:S(2)}, u32[]{:S(2)}) collective-permute-start(f32[512,128]{1,0:T(8,128)S(1)} %get-tuple-element.39), channel_id=1, source_target_pairs={{0,16},{4,20},{8,24},{12,28},{16,0},{20,4},{24,8},{28,12},{1,17},{... | collective-permute-start | bytes 786440 | tf_op jit(solution)/shard_map/ppermute | solution.py:422

commit v8 on v7

--- a/solution.py
+++ b/solution.py
@@ -46,31 +46,13 @@
     down[rim:, :LANES] = jnp.broadcast_to(labels[:, :LANES].astype(F32), (UNIT, LANES))
 
 
-def score_kernel(scale, steps, scalars, frames, queries, out, place):
+def score_kernel(scale, scalars, frames, queries, out):
     rows = frames.shape[0]
     blk = rows // SUB
-    step = pl.program_id(0)
-
-    @pl.when(step == 0)
-    def _():
-        place[...] = placement(rows, blk)
-
-    placed = jnp.dot(place[...], frames[...], preferred_element_type=F32).astype(jnp.bfloat16)
-    term = dot_t(placed, queries[...])
-
-    @pl.when(step == 0)
-    def _():
-        out[...] = term
-
-    @pl.when(step > 0)
-    def _():
-        out[...] += term
-
-    @pl.when(step == steps - 1)
-    def _():
-        m = lax.broadcasted_iota(jnp.int32, (rows, 1), 0)
-        frame = scalars[0] + (m & (SUB - 1)) * blk + m // SUB
-        out[...] = jnp.where(frame < scalars[1], out[...] * scale, 0.0)
+    placed = jnp.dot(placement(rows, blk), frames[...], preferred_element_type=F32).astype(jnp.bfloat16)
+    m = lax.broadcasted_iota(jnp.int32, (rows, 1), 0)
+    frame = scalars[0] + (m & (SUB - 1)) * blk + m // SUB
+    out[...] = jnp.where(frame < scalars[1], dot_t(placed, queries[...]) * scale, 0.0)
 
 
 def label_tile(half, blk, labels, before, after):
@@ -337,19 +319,12 @@
     down = [(j, i) for i, j in up]
     before = lax.ppermute(last, "tm", up)
     after = lax.ppermute(first, "tm", down)
-    steps = 4
     main = pl.pallas_call(
-        lambda *refs: score_kernel(scale, steps, *refs),
+        lambda *refs: score_kernel(scale, *refs),
         out_shape=jax.ShapeDtypeStruct((rows, query_count), F32),
-        grid=(steps,),
-        in_specs=[
-            smem,
-            pl.BlockSpec((rows, width // steps), lambda k: (0, k)),
-            pl.BlockSpec((query_count, width // steps), lambda k: (0, k)),
-        ],
-        out_specs=pl.BlockSpec((rows, query_count), lambda k: (0, 0)),
-        scratch_shapes=[VMEM((rows, rows), jnp.bfloat16)],
-        compiler_params=params(16),
+        in_specs=[smem] + whole_spec(2),
+        out_specs=pl.BlockSpec(memory_space=VMEM),
+        compiler_params=params(12),
         cost_estimate=cost(2 * rows * width * (rows + query_count), 3 << 20),
     )(scalars, frame_rows, queries)
     main = main.reshape(blk, SUB, query_count)

time: 163 us -> 162 us (level)
  Pallas kernels: 24.9 us -> 22.4 us
  waiting for transfers between devices: 37.3 us -> 39.8 us
    ppermute x1, waiting for transfers between devices: 1.25 us -> 3.76 us  [per_device(): after = lax.ppermute(first, 'tm', down)]
    pallas_call x1, Pallas kernels: 4.32 us -> 1.81 us  [per_device(): pl.pallas_call(lambda *refs: score_kernel(scale, *refs), out_shape=jax.Sh...]
  transfers between devices with their start and end apart: 11 -> 11, of which waited for: 8 -> 8; matrix products, arithmetic and copies ran while one was open for 2% -> 2% of each run, Pallas kernels for 3% -> 1%
where the time goes in v8:
time: 162 us; the launch traced here: 160 us
  blocking collectives  45.7 us (28%)
  starting transfers between devices  45 us (28%)
  waiting for transfers between devices  39.8 us (25%)
  Pallas kernels  22.4 us (14%)
  local copies, waits for them, and re-layouts  2.97 us (2%)
  other arithmetic  2.93 us (2%)
    all_gather x1, blocking collectives, per_device(): whole = lax.all_gather(chunk, 'tm')  35.8 us
    all_to_all x1, starting transfers between devices, per_device(): chunk = jnp.sum(lax.all_to_all(chunks, 'tm', 0, 0), axis=0)  14.9 us
    all_to_all x1, waiting for transfers between devices, per_device(): parts = lax.all_to_all(parts, 'rec', 0, 0)  14.6 us
    all_to_all x1, waiting for transfers between devices, per_device(): chunk = jnp.sum(lax.all_to_all(chunks, 'tm', 0, 0), axis=0)  11.6 us
    all_to_all x1, blocking collectives, per_device(): lax.all_to_all(jnp.broadcast_to(stats[None], (blocks,) + stats.shape), 'q...  9.89 us
    pallas_call x1, Pallas kernels, per_device(): pl.pallas_call(lambda *refs: grad_kernel(half, *refs), out_shape=[jax.Sha...  9.81 us
    ppermute x3, starting transfers between devices, per_device(): lax.ppermute(tap_sum, 'rec', [(i, (i + k) % recs) for i in range(recs)])  9.21 us
    pallas_call x1, Pallas kernels, per_device(): pl.pallas_call(lambda *refs: smooth_kernel(scale, half, *refs), out_shape...  8.98 us
  transfers between devices with their start and end apart: 11, of which 8 were waited for; matrix products, arithmetic and copies ran while one was open for 2% of the time, Pallas kernels for 1%

profile of v8, /device:TPU:6, one launch (start us, length us, event | category | flops | bytes accessed | tf_op | source)
XLA Modules:
  0.0 160.4 jit_solution(10524872211005260587)
XLA Ops:
  0.6 0.0 copy-start
  0.6 1.2 copy-done
  1.9 0.0 copy-start.4
  1.9 0.7 copy-done.4
  2.5 0.0 copy-start.1
  2.5 0.0 copy-start.2
  2.5 0.1 shard_map.77
  2.6 0.0 copy-start.3
  2.6 0.0 copy-start.5
  2.6 4.0 %collective-permute-start = (f32[40,1024]{1,0:T(8,128)S(1)}, f32[40,1024]{1,0:T(8,128)S(1)}, u32[]{:S(2)}, u32[]{:S(2)}) collective-permute-start(f32[40,1024]{1,0:T(8,128)S(1)} %get-tuple-element.20), channel_id=1, source_target_pairs={{0,32},{32,64},{64,96},{96,128},{128,160},{160,192},{192,224},{224... | collective-permute-start | bytes 491528 | tf_op jit(solution)/shard_map/ppermute | solution.py:320
  6.6 1.3 collective-permute-start.1
  8.6 0.1 stack.43.refs_0_
  8.7 0.0 copy-done.1
  8.7 0.0 copy-done.2
  8.7 1.8 %shard_map.76 = f32[512,512]{1,0:T(8,128)S(1)} custom-call(s32[11]{0:T(128)S(1)} %stack.43.refs_0_, bf16[512,1024]{1,0:T(8,128)(2,1)S(1)} %bitcast.35, bf16[512,1024]{1,0:T(8,128)(2,1)S(1)} %copy-done.2), custom_call_target="tpu_custom_call" | custom-call | flops 1073741824 | bytes 3145728 | tf_op jit(solution)/shard_map/pallas_call | solution.py:322
  10.5 0.0 collective-permute-done.refs_2_
  10.6 3.8 %collective-permute-done.1.refs_3_ = f32[40,1024]{1,0:T(8,128)S(1)} collective-permute-done((f32[40,1024]{1,0:T(8,128)S(1)}, f32[40,1024]{1,0:T(8,128)S(1)}, u32[]{:S(2)}, u32[]{:S(2)}) %collective-permute-start.1) | collective-permute-done | bytes 163872 | tf_op jit(solution)/shard_map/ppermute | solution.py:321
  14.3 0.0 copy-done.3
  14.3 0.0 copy-done.5
  14.3 9.0 %shard_map.78 = (f32[128,8,512]{2,1,0:T(8,128)}, f32[96,8,512]{2,1,0:T(8,128)S(1)}, f32[2,8,128]{2,1,0:T(8,128)S(1)}, f32[8,128]{1,0:T(8,128)S(1)}) custom-call(s32[11]{0:T(128)S(1)} %stack.43.refs_0_, f32[64,8,512]{2,1,0:T(8,128)S(1)} %bitcast.38, f32[40,1024]{1,0:T(8,128)S(1)} %collective-permute-done.refs_2_, ...), custom_call_target="tpu_custom_call" | custom-call | flops 34603008 | bytes 6291456 | tf_op jit(solution)/shard_map/pallas_call | solution.py:331
  23.3 9.9 %all_to_all.15.refs_4_ = f32[8,2,8,128]{3,2,1,0:T(8,128)S(1)} all-to-all(f32[8,2,8,128]{3,2,1,0:T(8,128)S(1)} %broadcast_in_dim.4), channel_id=1, replica_groups=mesh['tm'=16,'query'=8,'rec'=4] {'query'}, dimensions={0} | all-to-all | bytes 131072 | tf_op jit(solution)/shard_map/all_to_all | solution.py:349
  33.2 9.8 %shard_map.79 = (f32[4,512,256]{2,1,0:T(8,128)}, f32[40,512]{1,0:T(8,128)S(1)}, f32[4,512,128]{2,1,0:T(8,128)S(1)}, f32[4,512,128]{2,1,0:T(8,128)S(1)}) custom-call(s32[11]{0:T(128)S(1)} %stack.43.refs_0_, f32[96,8,512]{2,1,0:T(8,128)S(1)} %get-tuple-element.22.refs_1_, f32[128,8,512]{2,1,0:T(8,128)} %get-tuple-element.23.refs_2_, ...), custom_call_target="tpu_custom_call" | custom-call | flops 571473920 | bytes 8388608 | tf_op jit(solution)/shard_map/pallas_call | solution.py:354
  43.0 0.0 copy-start.6
  43.0 1.0 copy-done.6
  44.0 4.8 %all-to-all-start.1 = ((f32[4,512,256]{2,1,0:T(8,128)}), f32[4,512,256]{2,1,0:T(8,128)S(1)}, u32[]{:S(2)}, u32[]{:S(2)}) async-start(f32[4,512,256]{2,1,0:T(8,128)} %get-tuple-element.26), calls=%async_computation.1 | async-start | bytes 4194304 | tf_op jit(solution)/shard_map/all_to_all | solution.py:378
  48.8 1.9 %collective-permute-start.2 = (f32[4,512,128]{2,1,0:T(8,128)}, f32[4,512,128]{2,1,0:T(8,128)}, u32[]{:S(2)}, u32[]{:S(2)}) collective-permute-start(f32[4,512,128]{2,1,0:T(8,128)} %copy-done.6), channel_id=1, source_target_pairs={{0,4},{4,0},{8,12},{12,8},{16,20},{20,16},{24,28},{28,24},{1,5},{5... | collective-permute-start | bytes 3145736 | tf_op jit(solution)/shard_map/ppermute | solution.py:379
  50.7 2.8 %collective-permute-start.5 = (f32[40,512]{1,0:T(8,128)S(1)}, f32[40,512]{1,0:T(8,128)S(1)}, u32[]{:S(2)}, u32[]{:S(2)}) collective-permute-start(f32[40,512]{1,0:T(8,128)S(1)} %get-tuple-element.30.taps_own), channel_id=1, source_target_pairs={{0,3},{1,0},{2,1},{3,2},{4,7},{5,4},{6,5},{7,6},{8,11},{9,8},{10,9... | collective-permute-start | bytes 245768 | tf_op jit(solution)/shard_map/ppermute | solution.py:381
  53.5 4.3 %collective-permute-start.4 = (f32[40,512]{1,0:T(8,128)S(1)}, f32[40,512]{1,0:T(8,128)S(1)}, u32[]{:S(2)}, u32[]{:S(2)}) collective-permute-start(f32[40,512]{1,0:T(8,128)S(1)} %get-tuple-element.30.taps_own), channel_id=1, source_target_pairs={{0,1},{1,2},{2,3},{3,0},{4,5},{5,6},{6,7},{7,4},{8,9},{9,10},{10,1... | collective-permute-start | bytes 245768 | tf_op jit(solution)/shard_map/ppermute | solution.py:381
  57.8 2.2 %collective-permute-start.3 = (f32[40,512]{1,0:T(8,128)S(1)}, f32[40,512]{1,0:T(8,128)S(1)}, u32[]{:S(2)}, u32[]{:S(2)}) collective-permute-start(f32[40,512]{1,0:T(8,128)S(1)} %get-tuple-element.30.taps_own), channel_id=1, source_target_pairs={{0,2},{1,3},{2,0},{3,1},{4,6},{5,7},{6,4},{7,5},{8,10},{9,11},{10,... | collective-permute-start | bytes 245768 | tf_op jit(solution)/shard_map/ppermute | solution.py:381
  59.9 0.0 collective-permute-done.2
  59.9 14.6 %all-to-all-done.1.arrived = f32[4,512,256]{2,1,0:T(8,128)S(1)} async-done(((f32[4,512,256]{2,1,0:T(8,128)}), f32[4,512,256]{2,1,0:T(8,128)S(1)}, u32[]{:S(2)}, u32[]{:S(2)}) %all-to-all-start.1) | async-done | bytes 2097184 | tf_op jit(solution)/shard_map/all_to_all | solution.py:378
  74.6 0.0 collective-permute-done.5.taps_ahead
  74.6 0.4 collective-permute-done.4.taps_behind
  75.0 1.5 collective-permute-done.3.taps_far
  76.5 1.0 shard_map.80
  77.5 14.9 %all-to-all-start.2 = ((f32[16,40,256]{2,1,0:T(8,128)}), f32[16,40,256]{2,1,0:T(8,128)S(1)}, u32[]{:S(2)}, u32[]{:S(2)}) async-start(f32[16,40,256]{2,1,0:T(8,128)} %shard_map.80), calls=%async_computation.2 | async-start | bytes 1310720 | tf_op jit(solution)/shard_map/all_to_all | solution.py:393
  92.3 1.2 add_bitcast_fusion.2
  93.5 2.5 %collective-permute-start.6 = (f32[512,128]{1,0:T(8,128)S(1)}, f32[512,128]{1,0:T(8,128)S(1)}, u32[]{:S(2)}, u32[]{:S(2)}) collective-permute-start(f32[512,128]{1,0:T(8,128)S(1)} %get-tuple-element.37), channel_id=1, source_target_pairs={{0,8},{4,12},{8,16},{12,20},{16,24},{20,28},{24,0},{28,4},{1,9},{5... | collective-permute-start | bytes 786440 | tf_op jit(solution)/shard_map/ppermute | solution.py:397
  96.0 4.6 %collective-permute-start.8 = (f32[512,128]{1,0:T(8,128)S(1)}, f32[512,128]{1,0:T(8,128)S(1)}, u32[]{:S(2)}, u32[]{:S(2)}) collective-permute-start(f32[512,128]{1,0:T(8,128)S(1)} %get-tuple-element.38), channel_id=1, source_target_pairs={{0,24},{4,28},{8,0},{12,4},{16,8},{20,12},{24,16},{28,20},{1,25},{... | collective-permute-start | bytes 786440 | tf_op jit(solution)/shard_map/ppermute | solution.py:397
  100.6 1.9 %collective-permute-start.7 = (f32[512,128]{1,0:T(8,128)S(1)}, f32[512,128]{1,0:T(8,128)S(1)}, u32[]{:S(2)}, u32[]{:S(2)}) collective-permute-start(f32[512,128]{1,0:T(8,128)S(1)} %get-tuple-element.39), channel_id=1, source_target_pairs={{0,16},{4,20},{8,24},{12,28},{16,0},{20,4},{24,8},{28,12},{1,17},{... | collective-permute-start | bytes 786440 | tf_op jit(solution)/shard_map/ppermute | solution.py:397
  102.5 0.5 collective-permute-done.6
  103.0 6.6 %collective-permute-done.8 = f32[512,128]{1,0:T(8,128)S(1)} collective-permute-done((f32[512,128]{1,0:T(8,128)S(1)}, f32[512,128]{1,0:T(8,128)S(1)}, u32[]{:S(2)}, u32[]{:S(2)}) %collective-permute-start.8) | collective-permute-done | bytes 262176 | tf_op jit(solution)/shard_map/ppermute | solution.py:397
  109.6 0.7 collective-permute-done.7
  110.4 1.7 %fusion.4 = bf16[1,512,128]{2,1,0:T(8,128)(2,1)} fusion(f32[512,128]{1,0:T(8,128)S(1)} %collective-permute-done.8, f32[512,128]{1,0:T(8,128)S(1)} %collective-permute-done.7, f32[512,128]{1,0:T(8,128)S(1)} %collective-permute-done.6, f32[4,512,128]{2,1,0:T(8,128)} %collective-permute-done.2, f32[4,512,128]{2,1,0:T(8,128)S(1)} %get-tuple-element.31), kind=kLoop, calls=%fused_computation.8 | loop fusion | flops 393216 | bytes 1441792 | tf_op jit(solution)/shard_map/broadcast_in_dim | solution.py:398
  112.1 11.6 %all-to-all-done.2 = f32[16,40,256]{2,1,0:T(8,128)S(1)} async-done(((f32[16,40,256]{2,1,0:T(8,128)}), f32[16,40,256]{2,1,0:T(8,128)S(1)}, u32[]{:S(2)}, u32[]{:S(2)}) %all-to-all-start.2) | async-done | bytes 655392 | tf_op jit(solution)/shard_map/all_to_all | solution.py:393
  123.8 35.8 %all-gather = f32[640,256]{1,0:T(8,128)S(1)} all-gather(f32[40,256]{1,0:T(8,128)S(1)} %reduce_sum.9), channel_id=2, replica_groups=mesh['tm'=16,'query'=8,'rec'=4] {'tm'}, dimensions={0}, use_global_device_ids=true | all-gather | bytes 696320 | tf_op jit(solution)/shard_map/all_gather | solution.py:400
  159.6 0.8 shard_map.81
  (2 shorter events, 0.0 us)
Async XLA Ops:
  0.6 1.2 copy-start
  1.9 0.7 copy-start.4
  2.5 6.2 %copy-start.1 = (bf16[1,512,1024]{2,1,0:T(8,128)(2,1)S(1)}, bf16[1,512,1024]{2,1,0:T(8,128)(2,1)}, u32[]{:S(2)}) copy-start(bf16[1,512,1024]{2,1,0:T(8,128)(2,1)} %param.5) | copy-start | bytes 3145732
  2.5 6.2 %copy-start.2 = (bf16[512,1024]{1,0:T(8,128)(2,1)S(1)}, bf16[512,1024]{1,0:T(8,128)(2,1)}, u32[]{:S(2)}) copy-start(bf16[512,1024]{1,0:T(8,128)(2,1)} %refs_7_.1) | copy-start | bytes 3145732
  2.6 11.7 %copy-start.3 = (f32[33,512]{1,0:T(8,128)S(1)}, f32[33,512]{1,0:T(8,128)}, u32[]{:S(2)}) copy-start(f32[33,512]{1,0:T(8,128)} %refs_8_.1) | copy-start | bytes 202756
  2.6 11.7 %copy-start.5 = (s32[1,512]{1,0:T(1,128)S(1)}, s32[1,512]{1,0:T(1,128)}, u32[]{:S(2)}) copy-start(s32[1,512]{1,0:T(1,128)} %refs_4_.1) | copy-start | bytes 6148
  2.6 7.9 %collective-permute-start = (f32[40,1024]{1,0:T(8,128)S(1)}, f32[40,1024]{1,0:T(8,128)S(1)}, u32[]{:S(2)}, u32[]{:S(2)}) collective-permute-start(f32[40,1024]{1,0:T(8,128)S(1)} %get-tuple-element.20), channel_id=1, source_target_pairs={{0,32},{32,64},{64,96},{96,128},{128,160},{160,192},{192,224},{224... | collective-permute-start | bytes 491528 | tf_op jit(solution)/shard_map/ppermute | solution.py:320
  6.6 7.7 %collective-permute-start.1 = (f32[40,1024]{1,0:T(8,128)S(1)}, f32[40,1024]{1,0:T(8,128)S(1)}, u32[]{:S(2)}, u32[]{:S(2)}) collective-permute-start(f32[40,1024]{1,0:T(8,128)S(1)} %get-tuple-element.21), channel_id=1, source_target_pairs={{32,0},{64,32},{96,64},{128,96},{160,128},{192,160},{224,192},{256... | collective-permute-start | bytes 491528 | tf_op jit(solution)/shard_map/ppermute | solution.py:321
  43.0 1.0 copy-start.6
  44.0 30.6 %all-to-all-start.1 = ((f32[4,512,256]{2,1,0:T(8,128)}), f32[4,512,256]{2,1,0:T(8,128)S(1)}, u32[]{:S(2)}, u32[]{:S(2)}) async-start(f32[4,512,256]{2,1,0:T(8,128)} %get-tuple-element.26), calls=%async_computation.1 | async-start | bytes 4194304 | tf_op jit(solution)/shard_map/all_to_all | solution.py:378
  48.8 11.2 %collective-permute-start.2 = (f32[4,512,128]{2,1,0:T(8,128)}, f32[4,512,128]{2,1,0:T(8,128)}, u32[]{:S(2)}, u32[]{:S(2)}) collective-permute-start(f32[4,512,128]{2,1,0:T(8,128)} %copy-done.6), channel_id=1, source_target_pairs={{0,4},{4,0},{8,12},{12,8},{16,20},{20,16},{24,28},{28,24},{1,5},{5... | collective-permute-start | bytes 3145736 | tf_op jit(solution)/shard_map/ppermute | solution.py:379
  50.7 23.9 %collective-permute-start.5 = (f32[40,512]{1,0:T(8,128)S(1)}, f32[40,512]{1,0:T(8,128)S(1)}, u32[]{:S(2)}, u32[]{:S(2)}) collective-permute-start(f32[40,512]{1,0:T(8,128)S(1)} %get-tuple-element.30.taps_own), channel_id=1, source_target_pairs={{0,3},{1,0},{2,1},{3,2},{4,7},{5,4},{6,5},{7,6},{8,11},{9,8},{10,9... | collective-permute-start | bytes 245768 | tf_op jit(solution)/shard_map/ppermute | solution.py:381
  53.5 21.6 %collective-permute-start.4 = (f32[40,512]{1,0:T(8,128)S(1)}, f32[40,512]{1,0:T(8,128)S(1)}, u32[]{:S(2)}, u32[]{:S(2)}) collective-permute-start(f32[40,512]{1,0:T(8,128)S(1)} %get-tuple-element.30.taps_own), channel_id=1, source_target_pairs={{0,1},{1,2},{2,3},{3,0},{4,5},{5,6},{6,7},{7,4},{8,9},{9,10},{10,1... | collective-permute-start | bytes 245768 | tf_op jit(solution)/shard_map/ppermute | solution.py:381
  57.8 18.7 %collective-permute-start.3 = (f32[40,512]{1,0:T(8,128)S(1)}, f32[40,512]{1,0:T(8,128)S(1)}, u32[]{:S(2)}, u32[]{:S(2)}) collective-permute-start(f32[40,512]{1,0:T(8,128)S(1)} %get-tuple-element.30.taps_own), channel_id=1, source_target_pairs={{0,2},{1,3},{2,0},{3,1},{4,6},{5,7},{6,4},{7,5},{8,10},{9,11},{10,... | collective-permute-start | bytes 245768 | tf_op jit(solution)/shard_map/ppermute | solution.py:381
  77.5 46.2 %all-to-all-start.2 = ((f32[16,40,256]{2,1,0:T(8,128)}), f32[16,40,256]{2,1,0:T(8,128)S(1)}, u32[]{:S(2)}, u32[]{:S(2)}) async-start(f32[16,40,256]{2,1,0:T(8,128)} %shard_map.80), calls=%async_computation.2 | async-start | bytes 1310720 | tf_op jit(solution)/shard_map/all_to_all | solution.py:393
  93.5 9.5 %collective-permute-start.6 = (f32[512,128]{1,0:T(8,128)S(1)}, f32[512,128]{1,0:T(8,128)S(1)}, u32[]{:S(2)}, u32[]{:S(2)}) collective-permute-start(f32[512,128]{1,0:T(8,128)S(1)} %get-tuple-element.37), channel_id=1, source_target_pairs={{0,8},{4,12},{8,16},{12,20},{16,24},{20,28},{24,0},{28,4},{1,9},{5... | collective-permute-start | bytes 786440 | tf_op jit(solution)/shard_map/ppermute | solution.py:397
  96.0 13.6 %collective-permute-start.8 = (f32[512,128]{1,0:T(8,128)S(1)}, f32[512,128]{1,0:T(8,128)S(1)}, u32[]{:S(2)}, u32[]{:S(2)}) collective-permute-start(f32[512,128]{1,0:T(8,128)S(1)} %get-tuple-element.38), channel_id=1, source_target_pairs={{0,24},{4,28},{8,0},{12,4},{16,8},{20,12},{24,16},{28,20},{1,25},{... | collective-permute-start | bytes 786440 | tf_op jit(solution)/shard_map/ppermute | solution.py:397
  100.6 9.8 %collective-permute-start.7 = (f32[512,128]{1,0:T(8,128)S(1)}, f32[512,128]{1,0:T(8,128)S(1)}, u32[]{:S(2)}, u32[]{:S(2)}) collective-permute-start(f32[512,128]{1,0:T(8,128)S(1)} %get-tuple-element.39), channel_id=1, source_target_pairs={{0,16},{4,20},{8,24},{12,28},{16,0},{20,4},{24,8},{28,12},{1,17},{... | collective-permute-start | bytes 786440 | tf_op jit(solution)/shard_map/ppermute | solution.py:397
